TPU v7x, 32 devices: a whole 2x2x4 slice. The times are simulated.
32 devices in a mesh: rows: 16 (over z, x, core), snap: 2 (over y).
Axes of the slice: x: 2, y: 2, z: 4, core: 2. Of those that a mesh axis runs over, the one named last changes fastest.
Arguments:
- primal: float32 [16384, 1024], P('rows', 'snap'), may hold values from -6 to 6
- adjoint: float32 [16384, 1024], P('rows', 'snap'), may hold values from -6 to 6
- right_vectors: float32 [1024, 1024], P(None, 'snap'), may hold values from -0.1875 to 0.1875
- left_vectors: float32 [1024, 1024], P(None, 'snap'), may hold values from -0.1875 to 0.1875
- singular: float32 [1024], P('snap'), may hold values from 0.1 to 10
Outputs:
- gram: float32 [1024, 1024], P('rows', 'snap')
- phi_modes: float32 [16384, 1024], P('rows', 'snap')
- psi_modes: float32 [16384, 1024], P('rows', 'snap')
All inputs are finite; a program needn't handle non-finite values.
Results may differ from a plain program's by a relative error of at most 0.00008.
Values sent between devices are 32-bit elements; how exact they have to be, the bound alone decides.
No kernel may reach another device: no remote copies, remote signals or barrier semaphores. Data moves between devices by JAX's collectives and lax.ppermute only.
A program may use at most 64 MiB of HBM per device.

v0:
```python
import jax
import jax.numpy as jnp
from jax import lax
from jax.sharding import PartitionSpec as P


def inner_cols(left, right):
    return lax.dot_general(
        left,
        right,
        (((0,), (0,)), ((), ())),
        precision=lax.Precision.HIGHEST,
        preferred_element_type=jnp.float32,
    )


def shards(primal, adjoint, right_vectors, left_vectors, singular):
    full_adjoint = lax.all_gather(adjoint, "snap", axis=1, tiled=True)
    weights = 1.0 / jnp.sqrt(singular)
    psi_modes = (
        jnp.dot(
            full_adjoint,
            left_vectors,
            precision=lax.Precision.HIGHEST,
            preferred_element_type=jnp.float32,
        )
        * weights
    )
    phi_modes = (
        jnp.dot(
            lax.all_gather(primal, "snap", axis=1, tiled=True),
            right_vectors,
            precision=lax.Precision.HIGHEST,
            preferred_element_type=jnp.float32,
        )
        * weights
    )
    total_rows = primal.shape[0] * lax.axis_size("rows")
    norm = 1.0 / jnp.sqrt(jnp.float32(total_rows))
    width = full_adjoint.shape[1]
    share = width // lax.axis_size("rows")
    summed = lax.psum(inner_cols(full_adjoint, primal), "rows")
    gram = lax.dynamic_slice_in_dim(summed, lax.axis_index("rows") * share, share, 0) * norm
    return (gram, phi_modes, psi_modes)


def solution(mesh):
    in_specs = (P("rows", "snap"), P("rows", "snap"), P(None, "snap"), P(None, "snap"), P("snap"))
    out_specs = (P("rows", "snap"), P("rows", "snap"), P("rows", "snap"))
    return jax.shard_map(shards, mesh=mesh, in_specs=in_specs, out_specs=out_specs, check_vma=False)
```

profile of v0, /device:TPU:0, one launch (start us, length us, event | category | flops | bytes accessed | tf_op | source)
XLA Modules:
  0.0 236.8 jit_solution(5125719837970886138)
XLA Ops:
  7.2 0.0 copy-start
  7.2 0.0 all-gather.3.cloned.1.call-start
  7.2 0.7 all-gather.3.cloned.1.call-update
  7.9 0.0 all-gather.5.cloned.1.call-start
  8.0 0.7 all-gather.5.cloned.1.call-update
  8.7 0.0 all-reduce.2.cloned.1.call-start
  8.7 60.3 %all-gather.3.cloned.1.call-done = f32[1024,1024]{1,0:T(8,128)} async-done(((f32[1024,512]{1,0:T(8,128)}), f32[1024,1024]{1,0:T(8,128)}) %all-gather.3.cloned.1.call-update) | async-done | bytes 4194320 | tf_op jit(solution)/shard_map/all_gather | solution.py:18
  69.0 10.2 %fusion = f32[1024,512]{1,0:T(8,128)} fusion(f32[1024,1024]{1,0:T(8,128)} %all-gather.3.cloned.1.call-done, f32[1024,512]{1,0:T(8,128)} %param.5), kind=kOutput, calls=%fused_computation.3 | convolution fusion | flops 6442450944 | bytes 8388608 | tf_op jit(solution)/shard_map/dot_general | solution.py:8
  79.2 0.0 copy-start.1
  79.2 0.0 all-reduce.2.cloned.1.call-update
  79.3 0.7 copy-done.1
  79.9 0.0 copy-done
  79.9 9.7 %convolution_multiply_fusion = f32[1024,512]{1,0:T(8,128)} fusion(f32[1024,1024]{1,0:T(8,128)} %all-gather.3.cloned.1.call-done, f32[1024,512]{1,0:T(8,128)S(1)} %copy-done, f32[512]{0:T(512)S(1)} %sqrt.3), kind=kOutput, calls=%fused_computation | convolution fusion | flops 6442975232 | bytes 8390656 | tf_op jit(solution)/shard_map/dot_general | solution.py:21
  89.6 37.7 %all-gather.5.cloned.1.call-done = f32[1024,1024]{1,0:T(8,128)} async-done(((f32[1024,512]{1,0:T(8,128)}), f32[1024,1024]{1,0:T(8,128)}) %all-gather.5.cloned.1.call-update) | async-done | bytes 4194320 | tf_op jit(solution)/shard_map/all_gather | solution.py:31
  127.4 10.2 %convolution_multiply_fusion.1 = f32[1024,512]{1,0:T(8,128)} fusion(f32[1024,1024]{1,0:T(8,128)} %all-gather.5.cloned.1.call-done, f32[1024,512]{1,0:T(8,128)} %param.7, f32[512]{0:T(512)S(1)} %sqrt.3), kind=kOutput, calls=%fused_computation.1 | convolution fusion | flops 6442975232 | bytes 8390656 | tf_op jit(solution)/shard_map/dot_general | solution.py:30
  137.6 91.1 %all-reduce.2.cloned.1.call-done = f32[1024,512]{1,0:T(8,128)} async-done(((f32[1024,512]{1,0:T(8,128)}), f32[1024,512]{1,0:T(8,128)}) %all-reduce.2.cloned.1.call-update) | async-done | bytes 2097168 | tf_op jit(solution)/shard_map/psum | solution.py:42
  228.7 1.6 dynamic-slice_multiply_fusion
  (1 shorter events, 0.0 us)
Async XLA Ops:
  7.2 72.8 %copy-start = (f32[1024,512]{1,0:T(8,128)S(1)}, f32[1024,512]{1,0:T(8,128)}, u32[]{:S(2)}) copy-start(f32[1024,512]{1,0:T(8,128)} %param.8) | copy-start | bytes 6291460
  7.2 61.9 %all-gather.3.cloned.1.call-start = ((), (), s32[]{:S(2)}) async-start(), calls=%async_computation | async-start | bytes 6291456 | tf_op jit(solution)/shard_map/all_gather | solution.py:18
  7.9 119.5 %all-gather.5.cloned.1.call-start = ((), (), s32[]{:S(2)}) async-start(), calls=%async_computation.2 | async-start | bytes 6291456 | tf_op jit(solution)/shard_map/all_gather | solution.py:31
  8.7 220.1 %all-reduce.2.cloned.1.call-start = ((), (), s32[]{:S(2)}) async-start(), calls=%async_computation.1 | async-start | bytes 4194304 | tf_op jit(solution)/shard_map/psum | solution.py:42
  79.2 0.7 copy-start.1
Sparse Core Ops, SparseCore 0:
  9.6 59.4 all-gather.2
  70.6 56.7 all-gather.4
  130.9 97.7 all-reduce.1
where the time goes:
time: 237 us
  waiting for transfers between devices  191 us (81%)
  matrix products  30.1 us (13%)
  between operations  13.8 us (6%)
    psum x1, waiting for transfers between devices, shards(): summed = lax.psum(inner_cols(full_adjoint, primal), 'rows')  91.1 us
    all_gather x1, waiting for transfers between devices, shards(): full_adjoint = lax.all_gather(adjoint, 'snap', axis=1, tiled=True)  60.3 us
    all_gather x1, waiting for transfers between devices, shards(): lax.all_gather(primal, 'snap', axis=1, tiled=True)  37.7 us
    dot_general x1, matrix products, shards(): jnp.dot(lax.all_gather(primal, 'snap', axis=1, tiled=True), right_vectors...  10.2 us
    dot_general x1, matrix products, inner_cols(): lax.dot_general(left, right, (((0,), (0,)), ((), ())), precision=lax.Prec...  10.2 us
    dot_general x1, matrix products, shards(): jnp.dot(full_adjoint, left_vectors, precision=lax.Precision.HIGHEST, pref...  9.7 us
  transfers between devices with their start and end apart: 3, of which 3 were waited for; matrix products, arithmetic and copies ran while one was open for 13% of the time, Pallas kernels for 0%

commit v1 on v0

v1 whole, which is shorter than its diff:
```python
import functools

import jax
import jax.numpy as jnp
from jax import lax
from jax.experimental import pallas as pl
from jax.experimental.pallas import tpu as pltpu
from jax.sharding import PartitionSpec as P

HIGH = lax.Precision.HIGH


def mul(left, right):
    return jnp.dot(left, right, precision=HIGH, preferred_element_type=jnp.float32)


def split(x):
    high = x.astype(jnp.bfloat16)
    return high, (x - high.astype(jnp.float32)).astype(jnp.bfloat16)


def split_kernel(x_ref, high_ref, low_ref):
    high_ref[...], low_ref[...] = split(x_ref[...])


FREE = pl.CostEstimate(flops=0, bytes_accessed=0, transcendentals=0)


def split_matrix(matrix):
    return pl.pallas_call(
        split_kernel,
        out_shape=[jax.ShapeDtypeStruct(matrix.shape, jnp.bfloat16)] * 2,
        cost_estimate=FREE,
    )(matrix)


def inner_cols(left, right):
    return lax.dot_general(
        left, right, (((0,), (0,)), ((), ())), precision=HIGH, preferred_element_type=jnp.float32
    )


def add_rows_kernel(last, total_ref, x_ref, high_ref, low_ref, weights_ref, out_ref):
    dot = functools.partial(jnp.dot, preferred_element_type=jnp.float32)
    x_high, x_low = split(x_ref[...])
    total = total_ref[...] + (
        dot(x_high, high_ref[...]) + (dot(x_high, low_ref[...]) + dot(x_low, high_ref[...]))
    )
    out_ref[...] = total * weights_ref[...] if last else total


def add_rows(total, x, matrix, weights, start, tile, last):
    width = total.shape[1]
    depth = x.shape[1]
    first = start // tile
    rows = pl.BlockSpec((tile, width), lambda i: (first + i, 0))
    whole = pl.BlockSpec((depth, width), lambda i: (0, 0))
    return pl.pallas_call(
        functools.partial(add_rows_kernel, last),
        grid=(x.shape[0] // tile,),
        in_specs=[
            rows,
            pl.BlockSpec((tile, depth), lambda i: (i, 0)),
            whole,
            whole,
            pl.BlockSpec((1, width), lambda i: (0, 0)),
        ],
        out_specs=rows,
        out_shape=jax.ShapeDtypeStruct(total.shape, total.dtype),
        input_output_aliases={0: 0},
        cost_estimate=FREE,
    )(total, x, *matrix, weights[None])


def exchange(parts, axis, stride):
    count = lax.axis_size("rows")
    digits = parts.shape[axis]
    mine = (lax.axis_index("rows") // stride) % digits
    total = lax.dynamic_index_in_dim(parts, mine, axis, keepdims=False)
    for flip in range(1, digits):
        give = lax.dynamic_index_in_dim(parts, mine ^ flip, axis, keepdims=False)
        total += lax.ppermute(give, "rows", [(i, i ^ (flip * stride)) for i in range(count)])
    return total


def shards(primal, adjoint, right_vectors, left_vectors, singular):
    count = lax.axis_size("rows")
    sides = lax.axis_size("snap")
    side = lax.axis_index("snap")
    rows, width = primal.shape
    weights = 1.0 / jnp.sqrt(singular)
    norm = 1.0 / jnp.sqrt(jnp.float32(rows * count))
    ring = [(i, (i + 1) % sides) for i in range(sides)]
    cuts = [0, rows * 7 // 8, rows]
    spans = list(zip(cuts[:-1], cuts[1:]))

    def block(matrix, owner):
        return lax.dynamic_slice_in_dim(matrix, owner * width, width, 0)

    group = count // sides
    share = width // group

    near = min(group, 1 << (count.bit_length() - 1) // 2)

    def within(term):
        return exchange(term.reshape(group // near, near, share, width), 1, 1)

    adjoints = [adjoint]
    primals = [[primal[a:b] for a, b in spans]]
    for step in range(1, sides):
        adjoints.append(lax.ppermute(adjoints[-1], "snap", ring))
        primals.append([lax.ppermute(piece, "snap", ring) for piece in primals[-1]])

    terms = [within(inner_cols(adjoint, primal))]
    psi = mul(adjoint, block(left_vectors, side))
    phi = mul(primal, block(right_vectors, side))
    rights = []
    for step in range(1, sides):
        owner = (side - step) % sides
        left = split_matrix(block(left_vectors, owner))
        rights.append(split_matrix(block(right_vectors, owner)))
        theirs, left, rights, terms, psi, phi = lax.optimization_barrier(
            (adjoints[step], left, rights, terms, psi, phi)
        )
        terms.append(within(inner_cols(theirs, primal)))
        psi = add_rows(psi, theirs, left, weights, 0, rows // 2, step == sides - 1)
    blocks = [terms[-t % sides] for t in range(sides)]
    bit = 1
    while bit < sides:
        turn = (side // bit) % 2 == 1
        blocks = [jnp.where(turn, blocks[t - bit], blocks[t]) for t in range(sides)]
        bit *= 2
    total = exchange(jnp.concatenate(blocks), 0, near)
    gram = total * norm
    gram, psi, phi = lax.optimization_barrier((gram, psi, phi))
    for step in range(1, sides):
        for (start, stop), piece in zip(spans, primals[step]):
            tile = (stop - start) // (1 if start else 2)
            phi = add_rows(phi, piece, rights[step - 1], weights, start, tile, step == sides - 1)
    return (gram, phi, psi)


def solution(mesh):
    in_specs = (P("rows", "snap"), P("rows", "snap"), P(None, "snap"), P(None, "snap"), P("snap"))
    out_specs = (P("rows", "snap"), P("rows", "snap"), P("rows", "snap"))
    return jax.shard_map(shards, mesh=mesh, in_specs=in_specs, out_specs=out_specs, check_vma=False)
```

time: 237 us -> 98 us (0.41)
  waiting for transfers between devices: 191 us -> 39.2 us
  Pallas kernels: 0 us -> 16.3 us
  matrix products: 30.1 us -> 15.3 us
  starting transfers between devices: 0.11 us -> 13.4 us
  between operations: 13.8 us -> 0.71 us
  local copies, waits for them, and re-layouts: 0.67 us -> 8.4 us
  other arithmetic: 1.57 us -> 4.17 us
    all_gather x2 -> x0, waiting for transfers between devices: 98.1 us -> none  [the longest x1 60.3 us: shards(): full_adjoint = lax.all_gather(adjoint, 'snap', axis=1, tiled=True)]
    psum x1 -> x0, waiting for transfers between devices: 91.1 us -> none  [shards(): summed = lax.psum(inner_cols(full_adjoint, primal), 'rows')]
    ppermute x0 -> x12, waiting for transfers between devices: none -> 39.2 us  [the longest x1 20.9 us: shards(): adjoints.append(lax.ppermute(adjoints[-1], 'snap', ring))]
    pallas_call x0 -> x5, Pallas kernels: none -> 16.3 us  [the longest x3 11.8 us: add_rows(): pl.pallas_call(functools.partial(add_rows_kernel, last), grid=(x.shape[0]...]
    dot_general x3 -> x4, matrix products: 30.1 us -> 15.3 us  [the longest x2 7.69 us: mul(): jnp.dot(left, right, precision=HIGH, preferred_element_type=jnp.float32)]
    ppermute x0 -> x12, starting transfers between devices: none -> 13.4 us  [the longest x9 8.49 us: exchange(): lax.ppermute(give, 'rows', [(i, i ^ flip * stride) for i in range(count)])]
    dynamic_slice x0 -> x1, local copies, waits for them, and re-layouts: none -> 3.03 us  [block(): return lax.dynamic_slice_in_dim(matrix, owner * width, width, 0)]
  transfers between devices with their start and end apart: 3 -> 12, of which waited for: 3 -> 6; matrix products, arithmetic and copies ran while one was open for 13% -> 27% of each run, Pallas kernels for 0% -> 14%
where the time goes in v1:
time: 98 us; the launch traced here: 97.6 us
  waiting for transfers between devices  39.2 us (40%)
  Pallas kernels  16.3 us (17%)
  matrix products  15.3 us (16%)
  starting transfers between devices  13.4 us (14%)
  local copies, waits for them, and re-layouts  8.4 us (9%)
  other arithmetic  4.17 us (4%)
    ppermute x1, waiting for transfers between devices, shards(): adjoints.append(lax.ppermute(adjoints[-1], 'snap', ring))  20.9 us
    ppermute x9, waiting for transfers between devices, exchange(): lax.ppermute(give, 'rows', [(i, i ^ flip * stride) for i in range(count)])  15.6 us
    pallas_call x3, Pallas kernels, add_rows(): pl.pallas_call(functools.partial(add_rows_kernel, last), grid=(x.shape[0]...  11.8 us
    ppermute x9, starting transfers between devices, exchange(): lax.ppermute(give, 'rows', [(i, i ^ flip * stride) for i in range(count)])  8.49 us
    dot_general x2, matrix products, mul(): jnp.dot(left, right, precision=HIGH, preferred_element_type=jnp.float32)  7.69 us
    dot_general x2, matrix products, inner_cols(): lax.dot_general(left, right, (((0,), (0,)), ((), ())), precision=HIGH, pr...  7.61 us
    pallas_call x2, Pallas kernels, split_matrix(): pl.pallas_call(split_kernel, out_shape=[jax.ShapeDtypeStruct(matrix.shape...  4.55 us
    ppermute x1, starting transfers between devices, shards(): adjoints.append(lax.ppermute(adjoints[-1], 'snap', ring))  3.03 us
  transfers between devices with their start and end apart: 12, of which 6 were waited for; matrix products, arithmetic and copies ran while one was open for 27% of the time, Pallas kernels for 14%

profile of v1, /device:TPU:0, one launch (start us, length us, event | category | flops | bytes accessed | tf_op | source)
XLA Modules:
  0.0 97.6 jit_solution(17452115778526788095)
XLA Ops:
  0.6 3.0 %collective-permute-start = (f32[1024,512]{1,0:T(8,128)}, f32[1024,512]{1,0:T(8,128)}, u32[]{:S(2)}, u32[]{:S(2)}) collective-permute-start(f32[1024,512]{1,0:T(8,128)} %param.6), channel_id=1, source_target_pairs={{0,1},{1,0},{2,3},{3,2},{4,5},{5,4},{6,7},{7,6},{8,9},{9,8},{10,11... | collective-permute-start | bytes 6291464 | tf_op jit(solution)/shard_map/ppermute | solution.py:111
  3.7 4.2 %fusion.21 = f32[512,512]{1,0:T(8,128)S(1)} fusion(f32[1024,512]{1,0:T(8,128)} %param.6, f32[1024,512]{1,0:T(8,128)} %param.5), kind=kOutput, calls=%fused_computation.42 | convolution fusion | flops 1610612736 | bytes 5242880 | tf_op jit(solution)/shard_map/dot_general | solution.py:38
  8.8 1.5 %collective-permute-start.2 = (f32[2,64,512]{2,1,0:T(8,128)}, f32[2,64,512]{2,1,0:T(8,128)}, u32[]{:S(2)}, u32[]{:S(2)}) collective-permute-start(f32[2,64,512]{2,1,0:T(8,128)} %get-tuple-element.40), channel_id=1, source_target_pairs={{0,4},{2,6},{4,0},{6,2},{8,12},{10,14},{12,8},{14,10},{16,20},{18,... | collective-permute-start | bytes 786440 | tf_op jit(solution)/shard_map/ppermute | solution.py:82
  10.7 1.4 %slice.6 = f32[896,512]{1,0:T(8,128)} slice(f32[1024,512]{1,0:T(8,128)S(1)} %copy-done), slice={[0:896], [0:512]} | slice | bytes 3670016 | tf_op jit(solution)/shard_map/slice | solution.py:109
  12.4 3.0 %constant_dynamic-slice_fusion = (f32[512,512]{1,0:T(8,128)}, f32[512,512]{1,0:T(8,128)}) fusion(f32[1024,512]{1,0:T(8,128)} %param.7, s32[]{:T(128)S(6)} %select_n.81, f32[1024,512]{1,0:T(8,128)} %param.8), kind=kLoop, calls=%fused_computation.40 | loop fusion | bytes 4194308 | tf_op jit(solution)/shard_map/dynamic_slice | solution.py:98
  15.4 2.3 %shard_map.76 = (bf16[512,512]{1,0:T(8,128)(2,1)}, bf16[512,512]{1,0:T(8,128)(2,1)}) custom-call(f32[512,512]{1,0:T(8,128)} %get-tuple-element.45.x_ref), custom_call_target="tpu_custom_call" | custom-call | tf_op jit(solution)/shard_map/pallas_call | solution.py:30
  17.7 2.3 %shard_map.77 = (bf16[512,512]{1,0:T(8,128)(2,1)}, bf16[512,512]{1,0:T(8,128)(2,1)}) custom-call(f32[512,512]{1,0:T(8,128)} %get-tuple-element.44.x_ref), custom_call_target="tpu_custom_call" | custom-call | tf_op jit(solution)/shard_map/pallas_call | solution.py:30
  19.9 4.5 %convolution_bitcast_fusion.total_ref = f32[1024,512]{1,0:T(8,128)} fusion(f32[1024,512]{1,0:T(8,128)S(1)} %copy-done, f32[1024,512]{1,0:T(8,128)} %param.7, s32[]{:T(128)S(6)} %select_n.87), kind=kOutput, calls=%fused_computation | convolution fusion | flops 1610612736 | bytes 5242884 | tf_op jit(solution)/shard_map/dot_general | solution.py:14
  24.4 3.2 %convolution_bitcast_fusion.1.total_ref = f32[1024,512]{1,0:T(8,128)} fusion(f32[1024,512]{1,0:T(8,128)S(1)} %copy-done.1, f32[1024,512]{1,0:T(8,128)S(1)} %copy-done.4, s32[]{:T(128)S(6)} %select_n.87), kind=kOutput, calls=%fused_computation.1 | convolution fusion | flops 1610612736 | bytes 5242884 | tf_op jit(solution)/shard_map/dot_general | solution.py:14
  29.6 20.9 %collective-permute-done.x_ref = f32[1024,512]{1,0:T(8,128)} collective-permute-done((f32[1024,512]{1,0:T(8,128)}, f32[1024,512]{1,0:T(8,128)}, u32[]{:S(2)}, u32[]{:S(2)}) %collective-permute-start) | collective-permute-done | bytes 2097184 | tf_op jit(solution)/shard_map/ppermute | solution.py:111
  50.4 3.4 %fusion.22 = f32[512,512]{1,0:T(8,128)S(1)} fusion(f32[1024,512]{1,0:T(8,128)} %collective-permute-done.x_ref, f32[1024,512]{1,0:T(8,128)S(1)} %copy-done), kind=kOutput, calls=%fused_computation.43 | convolution fusion | flops 1610612736 | bytes 5242880 | tf_op jit(solution)/shard_map/dot_general | solution.py:38
  54.9 2.0 %collective-permute-start.5 = (f32[2,64,512]{2,1,0:T(8,128)}, f32[2,64,512]{2,1,0:T(8,128)}, u32[]{:S(2)}, u32[]{:S(2)}) collective-permute-start(f32[2,64,512]{2,1,0:T(8,128)} %get-tuple-element.37), channel_id=1, source_target_pairs={{0,4},{2,6},{4,0},{6,2},{8,12},{10,14},{12,8},{14,10},{16,20},{18,... | collective-permute-start | bytes 786440 | tf_op jit(solution)/shard_map/ppermute | solution.py:82
  57.1 7.3 %collective-permute-done.5 = f32[2,64,512]{2,1,0:T(8,128)} collective-permute-done((f32[2,64,512]{2,1,0:T(8,128)}, f32[2,64,512]{2,1,0:T(8,128)}, u32[]{:S(2)}, u32[]{:S(2)}) %collective-permute-start.5) | collective-permute-done | bytes 262176 | tf_op jit(solution)/shard_map/ppermute | solution.py:82
  64.4 5.2 %collective-permute-done.6 = f32[2,64,512]{2,1,0:T(8,128)} collective-permute-done((f32[2,64,512]{2,1,0:T(8,128)}, f32[2,64,512]{2,1,0:T(8,128)}, u32[]{:S(2)}, u32[]{:S(2)}) %collective-permute-start.6) | collective-permute-done | bytes 262176 | tf_op jit(solution)/shard_map/ppermute | solution.py:82
  69.6 1.2 %broadcast_select_fusion = (f32[2,64,512]{2,1,0:T(8,128)S(1)}, f32[2,64,512]{2,1,0:T(8,128)S(1)}) fusion(f32[2,64,512]{2,1,0:T(8,128)S(1)} %fusion.5, pred[]{:T(512)S(6)} %eq.9, f32[2,64,512]{2,1,0:T(8,128)} %collective-permute-done.6, f32[2,64,512]{2,1,0:T(8,128)} %collective-permute-done.5, f32[2,64,512]{2,1,0:T(8,128)} %collective-permute-done.4, ...), kind=kLoop, calls=%fused_computation.36 | loop fusion | flops 262144 | bytes 1835013 | tf_op jit(solution)/shard_map/jit(_where)/select_n | solution.py:131
  71.0 1.7 %collective-permute-start.7 = (f32[64,512]{1,0:T(8,128)S(1)}, f32[64,512]{1,0:T(8,128)S(1)}, u32[]{:S(2)}, u32[]{:S(2)}) collective-permute-start(f32[64,512]{1,0:T(8,128)S(1)} %get-tuple-element.41), channel_id=1, source_target_pairs={{0,8},{2,10},{4,12},{6,14},{8,0},{10,2},{12,4},{14,6},{16,24},{18,... | collective-permute-start | bytes 393224 | tf_op jit(solution)/shard_map/ppermute | solution.py:82
  72.7 2.6 %collective-permute-start.8 = (f32[64,512]{1,0:T(8,128)S(1)}, f32[64,512]{1,0:T(8,128)S(1)}, u32[]{:S(2)}, u32[]{:S(2)}) collective-permute-start(f32[64,512]{1,0:T(8,128)S(1)} %get-tuple-element.42), channel_id=1, source_target_pairs={{0,16},{2,18},{4,20},{6,22},{8,24},{10,26},{12,28},{14,30},{16,0},... | collective-permute-start | bytes 393224 | tf_op jit(solution)/shard_map/ppermute | solution.py:82
  75.5 1.6 %collective-permute-start.11 = (f32[128,512]{1,0:T(8,128)S(1)}, f32[128,512]{1,0:T(8,128)S(1)}, u32[]{:S(2)}, u32[]{:S(2)}) collective-permute-start(f32[128,512]{1,0:T(8,128)S(1)} %slice.7), channel_id=1, source_target_pairs={{0,1},{1,0},{2,3},{3,2},{4,5},{5,4},{6,7},{7,6},{8,9},{9,8},{10,11... | collective-permute-start | bytes 786440 | tf_op jit(solution)/shard_map/ppermute | solution.py:112
  77.7 4.8 %shard_map.78 = f32[1024,512]{1,0:T(8,128)} custom-call(f32[1024,512]{1,0:T(8,128)} %convolution_bitcast_fusion.1.total_ref, f32[1024,512]{1,0:T(8,128)} %collective-permute-done.x_ref, bf16[512,512]{1,0:T(8,128)(2,1)} %get-tuple-element.25.high_ref, bf16[512,512]{1,0:T(8,128)(2,1)} %get-tuple-element.26.low_ref, ...), custom_call_target="tpu_custom_call", output_to_operand_aliasing={{}: (0, {})} | custom-call | tf_op jit(solution)/shard_map/pallas_call | solution.py:58
  82.6 3.0 %collective-permute-done.8 = f32[64,512]{1,0:T(8,128)S(1)} collective-permute-done((f32[64,512]{1,0:T(8,128)S(1)}, f32[64,512]{1,0:T(8,128)S(1)}, u32[]{:S(2)}, u32[]{:S(2)}) %collective-permute-start.8) | collective-permute-done | bytes 131104 | tf_op jit(solution)/shard_map/ppermute | solution.py:82
  85.6 1.6 %fusion.13 = f32[64,512]{1,0:T(8,128)} fusion(f32[64,512]{1,0:T(8,128)} %collective-permute-done.9, f32[64,512]{1,0:T(8,128)S(1)} %collective-permute-done.8, f32[64,512]{1,0:T(8,128)S(1)} %collective-permute-done.7, s32[]{:T(128)S(6)} %select_n.92, f32[2,64,512]{2,1,0:T(8,128)S(1)} %broadcast_select_fusion.1, f32[2,64,512]{2,1,0:T(8,128)S(1)} %copy-done.3), kind=kLoop, calls=%fused_computation.31 | loop fusion | flops 163840 | bytes 1048580 | tf_op jit(solution)/shard_map/mul | solution.py:134
  87.2 2.5 %collective-permute-done.10.x_ref = f32[896,512]{1,0:T(8,128)} collective-permute-done((f32[896,512]{1,0:T(8,128)}, f32[896,512]{1,0:T(8,128)}, u32[]{:S(2)}, u32[]{:S(2)}) %collective-permute-start.10) | collective-permute-done | bytes 1835040 | tf_op jit(solution)/shard_map/ppermute | solution.py:112
  89.8 4.5 %shard_map.79.total_ref = f32[1024,512]{1,0:T(8,128)} custom-call(f32[1024,512]{1,0:T(8,128)} %convolution_bitcast_fusion.total_ref, f32[896,512]{1,0:T(8,128)} %collective-permute-done.10.x_ref, bf16[512,512]{1,0:T(8,128)(2,1)} %get-tuple-element.30.high_ref, bf16[512,512]{1,0:T(8,128)(2,1)} %get-tuple-element.31.low_ref, ...), custom_call_target="tpu_custom_call", output_to_operand_aliasing={{}: (0, {})} | custom-call | tf_op jit(solution)/shard_map/pallas_call | solution.py:58
  95.2 2.4 %shard_map.80 = f32[1024,512]{1,0:T(8,128)} custom-call(f32[1024,512]{1,0:T(8,128)} %shard_map.79.total_ref, f32[128,512]{1,0:T(8,128)} %copy-done.6, bf16[512,512]{1,0:T(8,128)(2,1)} %get-tuple-element.30.high_ref, bf16[512,512]{1,0:T(8,128)(2,1)} %get-tuple-element.31.low_ref, f32[1,512]{1,0:T(1,128)} %bitcast.60), custom_call_target="tpu_custom_call", output_to_operand_aliasing={{}: (0, {})} | custom-call | tf_op jit(solution)/shard_map/pallas_call | solution.py:58
  (36 shorter events, 6.5 us)
Async XLA Ops:
  0.6 49.8 %collective-permute-start = (f32[1024,512]{1,0:T(8,128)}, f32[1024,512]{1,0:T(8,128)}, u32[]{:S(2)}, u32[]{:S(2)}) collective-permute-start(f32[1024,512]{1,0:T(8,128)} %param.6), channel_id=1, source_target_pairs={{0,1},{1,0},{2,3},{3,2},{4,5},{5,4},{6,7},{7,6},{8,9},{9,8},{10,11... | collective-permute-start | bytes 6291464 | tf_op jit(solution)/shard_map/ppermute | solution.py:111
  3.7 7.0 %copy-start = (f32[1024,512]{1,0:T(8,128)S(1)}, f32[1024,512]{1,0:T(8,128)}, u32[]{:S(2)}) copy-start(f32[1024,512]{1,0:T(8,128)} %param.5) | copy-start | bytes 6291460
  8.8 18.8 %collective-permute-start.1 = (f32[2,64,512]{2,1,0:T(8,128)}, f32[2,64,512]{2,1,0:T(8,128)S(1)}, u32[]{:S(2)}, u32[]{:S(2)}) collective-permute-start(f32[2,64,512]{2,1,0:T(8,128)} %get-tuple-element.38), channel_id=1, source_target_pairs={{0,2},{2,0},{4,6},{6,4},{8,10},{10,8},{12,14},{14,12},{16,18},{18,... | collective-permute-start | bytes 786440 | tf_op jit(solution)/shard_map/ppermute | solution.py:82
  8.8 18.8 %collective-permute-start.2 = (f32[2,64,512]{2,1,0:T(8,128)}, f32[2,64,512]{2,1,0:T(8,128)}, u32[]{:S(2)}, u32[]{:S(2)}) collective-permute-start(f32[2,64,512]{2,1,0:T(8,128)} %get-tuple-element.40), channel_id=1, source_target_pairs={{0,4},{2,6},{4,0},{6,2},{8,12},{10,14},{12,8},{14,10},{16,20},{18,... | collective-permute-start | bytes 786440 | tf_op jit(solution)/shard_map/ppermute | solution.py:82
  10.3 18.0 %collective-permute-start.3 = (f32[2,64,512]{2,1,0:T(8,128)}, f32[2,64,512]{2,1,0:T(8,128)}, u32[]{:S(2)}, u32[]{:S(2)}) collective-permute-start(f32[2,64,512]{2,1,0:T(8,128)} %get-tuple-element.39), channel_id=1, source_target_pairs={{0,6},{2,4},{4,2},{6,0},{8,14},{10,12},{12,10},{14,8},{16,22},{18,... | collective-permute-start | bytes 786440 | tf_op jit(solution)/shard_map/ppermute | solution.py:82
  12.1 77.7 %collective-permute-start.10 = (f32[896,512]{1,0:T(8,128)}, f32[896,512]{1,0:T(8,128)}, u32[]{:S(2)}, u32[]{:S(2)}) collective-permute-start(f32[896,512]{1,0:T(8,128)} %slice.6), channel_id=1, source_target_pairs={{0,1},{1,0},{2,3},{3,2},{4,5},{5,4},{6,7},{7,6},{8,9},{9,8},{10,11... | collective-permute-start | bytes 5505032 | tf_op jit(solution)/shard_map/ppermute | solution.py:112
  19.9 4.5 %copy-start.1 = (f32[1024,512]{1,0:T(8,128)S(1)}, f32[1024,512]{1,0:T(8,128)}, u32[]{:S(2)}) copy-start(f32[1024,512]{1,0:T(8,128)} %param.6) | copy-start | bytes 6291460
  19.9 4.5 %copy-start.4 = (f32[1024,512]{1,0:T(8,128)S(1)}, f32[1024,512]{1,0:T(8,128)}, u32[]{:S(2)}) copy-start(f32[1024,512]{1,0:T(8,128)} %param.8) | copy-start | bytes 6291460
  27.7 0.7 copy-start.5
  54.9 22.3 %copy-start.7 = (f32[512]{0:T(512)S(1)}, f32[512]{0:T(512)}, u32[]{:S(2)}) copy-start(f32[512]{0:T(512)} %param.9) | copy-start | bytes 6148
  54.9 2.2 %collective-permute-start.4 = (f32[2,64,512]{2,1,0:T(8,128)}, f32[2,64,512]{2,1,0:T(8,128)}, u32[]{:S(2)}, u32[]{:S(2)}) collective-permute-start(f32[2,64,512]{2,1,0:T(8,128)} %get-tuple-element.35), channel_id=1, source_target_pairs={{0,2},{2,0},{4,6},{6,4},{8,10},{10,8},{12,14},{14,12},{16,18},{18,... | collective-permute-start | bytes 786440 | tf_op jit(solution)/shard_map/ppermute | solution.py:82
  54.9 9.5 %collective-permute-start.5 = (f32[2,64,512]{2,1,0:T(8,128)}, f32[2,64,512]{2,1,0:T(8,128)}, u32[]{:S(2)}, u32[]{:S(2)}) collective-permute-start(f32[2,64,512]{2,1,0:T(8,128)} %get-tuple-element.37), channel_id=1, source_target_pairs={{0,4},{2,6},{4,0},{6,2},{8,12},{10,14},{12,8},{14,10},{16,20},{18,... | collective-permute-start | bytes 786440 | tf_op jit(solution)/shard_map/ppermute | solution.py:82
  56.9 12.7 %collective-permute-start.6 = (f32[2,64,512]{2,1,0:T(8,128)}, f32[2,64,512]{2,1,0:T(8,128)}, u32[]{:S(2)}, u32[]{:S(2)}) collective-permute-start(f32[2,64,512]{2,1,0:T(8,128)} %get-tuple-element.36), channel_id=1, source_target_pairs={{0,6},{2,4},{4,2},{6,0},{8,14},{10,12},{12,10},{14,8},{16,22},{18,... | collective-permute-start | bytes 786440 | tf_op jit(solution)/shard_map/ppermute | solution.py:82
  70.9 4.6 %copy-start.2 = (f32[2,64,512]{2,1,0:T(8,128)}, f32[2,64,512]{2,1,0:T(8,128)S(1)}, u32[]{:S(2)}) copy-start(f32[2,64,512]{2,1,0:T(8,128)S(1)} %get-tuple-element.33) | copy-start | bytes 786436
  71.0 11.6 %collective-permute-start.7 = (f32[64,512]{1,0:T(8,128)S(1)}, f32[64,512]{1,0:T(8,128)S(1)}, u32[]{:S(2)}, u32[]{:S(2)}) collective-permute-start(f32[64,512]{1,0:T(8,128)S(1)} %get-tuple-element.41), channel_id=1, source_target_pairs={{0,8},{2,10},{4,12},{6,14},{8,0},{10,2},{12,4},{14,6},{16,24},{18,... | collective-permute-start | bytes 393224 | tf_op jit(solution)/shard_map/ppermute | solution.py:82
  72.7 12.9 %collective-permute-start.8 = (f32[64,512]{1,0:T(8,128)S(1)}, f32[64,512]{1,0:T(8,128)S(1)}, u32[]{:S(2)}, u32[]{:S(2)}) collective-permute-start(f32[64,512]{1,0:T(8,128)S(1)} %get-tuple-element.42), channel_id=1, source_target_pairs={{0,16},{2,18},{4,20},{6,22},{8,24},{10,26},{12,28},{14,30},{16,0},... | collective-permute-start | bytes 393224 | tf_op jit(solution)/shard_map/ppermute | solution.py:82
  75.3 10.3 %collective-permute-start.9 = (f32[64,512]{1,0:T(8,128)S(1)}, f32[64,512]{1,0:T(8,128)}, u32[]{:S(2)}, u32[]{:S(2)}) collective-permute-start(f32[64,512]{1,0:T(8,128)S(1)} %get-tuple-element.43), channel_id=1, source_target_pairs={{0,24},{2,26},{4,28},{6,30},{8,16},{10,18},{12,20},{14,22},{16,8},... | collective-permute-start | bytes 393224 | tf_op jit(solution)/shard_map/ppermute | solution.py:82
  75.5 18.9 %collective-permute-start.11 = (f32[128,512]{1,0:T(8,128)S(1)}, f32[128,512]{1,0:T(8,128)S(1)}, u32[]{:S(2)}, u32[]{:S(2)}) collective-permute-start(f32[128,512]{1,0:T(8,128)S(1)} %slice.7), channel_id=1, source_target_pairs={{0,1},{1,0},{2,3},{3,2},{4,5},{5,4},{6,7},{7,6},{8,9},{9,8},{10,11... | collective-permute-start | bytes 786440 | tf_op jit(solution)/shard_map/ppermute | solution.py:112
  77.7 7.9 %copy-start.3 = (f32[2,64,512]{2,1,0:T(8,128)S(1)}, f32[2,64,512]{2,1,0:T(8,128)}, u32[]{:S(2)}) copy-start(f32[2,64,512]{2,1,0:T(8,128)} %copy-done.2) | copy-start | bytes 786436
  94.4 0.7 copy-start.6

commit v2 on v1

--- a/solution.py
+++ b/solution.py
@@ -23,6 +23,7 @@
     high_ref[...], low_ref[...] = split(x_ref[...])
 
 
+LIMIT = 16 << 20
 FREE = pl.CostEstimate(flops=0, bytes_accessed=0, transcendentals=0)
 
 
@@ -31,6 +32,7 @@
         split_kernel,
         out_shape=[jax.ShapeDtypeStruct(matrix.shape, jnp.bfloat16)] * 2,
         cost_estimate=FREE,
+        compiler_params=pltpu.CompilerParams(vmem_limit_bytes=LIMIT),
     )(matrix)
 
 
@@ -69,6 +71,40 @@
         out_shape=jax.ShapeDtypeStruct(total.shape, total.dtype),
         input_output_aliases={0: 0},
         cost_estimate=FREE,
+        compiler_params=pltpu.CompilerParams(vmem_limit_bytes=LIMIT),
+    )(total, x, *matrix, weights[None])
+
+
+def end_rows_kernel(first, last, total_ref, x_ref, high_ref, low_ref, weights_ref, out_ref, held, sems):
+    rows = x_ref.shape[0]
+    fetch = pltpu.make_async_copy(total_ref.at[pl.ds(first, rows)], held, sems.at[0])
+    fetch.start()
+    dot = functools.partial(jnp.dot, preferred_element_type=jnp.float32)
+    x_high, x_low = split(x_ref[...])
+    term = dot(x_high, high_ref[...]) + (dot(x_high, low_ref[...]) + dot(x_low, high_ref[...]))
+    fetch.wait()
+    total = held[...] + term
+    held[...] = total * weights_ref[...] if last else total
+    store = pltpu.make_async_copy(held, out_ref.at[pl.ds(first, rows)], sems.at[1])
+    store.start()
+    store.wait()
+
+
+def end_rows(total, x, matrix, weights, start, last):
+    vmem = pl.BlockSpec(memory_space=pltpu.VMEM)
+    apart = pl.BlockSpec(memory_space=pl.ANY)
+    return pl.pallas_call(
+        functools.partial(end_rows_kernel, start, last),
+        in_specs=[apart, vmem, vmem, vmem, vmem],
+        out_specs=apart,
+        out_shape=jax.ShapeDtypeStruct(total.shape, total.dtype),
+        scratch_shapes=[
+            pltpu.VMEM((x.shape[0], total.shape[1]), jnp.float32),
+            pltpu.SemaphoreType.DMA((2,)),
+        ],
+        input_output_aliases={0: 0},
+        cost_estimate=FREE,
+        compiler_params=pltpu.CompilerParams(vmem_limit_bytes=LIMIT),
     )(total, x, *matrix, weights[None])
 
 
@@ -135,8 +171,11 @@
     gram, psi, phi = lax.optimization_barrier((gram, psi, phi))
     for step in range(1, sides):
         for (start, stop), piece in zip(spans, primals[step]):
-            tile = (stop - start) // (1 if start else 2)
-            phi = add_rows(phi, piece, rights[step - 1], weights, start, tile, step == sides - 1)
+            last = step == sides - 1
+            if start == 0:
+                phi = add_rows(phi, piece, rights[step - 1], weights, start, stop // 2, last)
+            else:
+                phi = end_rows(phi, piece, rights[step - 1], weights, start, last)
     return (gram, phi, psi)
 
 

time: 98 us -> 96.8 us (0.988)
  Pallas kernels: 16.3 us -> 10.6 us
  local copies, waits for them, and re-layouts: 8.4 us -> 12 us
  other arithmetic: 4.17 us -> 5.15 us
    pallas_call x2, Pallas kernels: 4.55 us -> 0.29 us  [split_matrix(): pl.pallas_call(split_kernel, out_shape=[jax.ShapeDtypeStruct(matrix.shape...]
    unnamed x16 -> x32, local copies, waits for them, and re-layouts: 1.43 us -> 5.41 us
    pallas_call x3 -> x2, Pallas kernels: 11.8 us -> 8.42 us  [add_rows(): pl.pallas_call(functools.partial(add_rows_kernel, last), grid=(x.shape[0]...]
    ppermute x1, waiting for transfers between devices: 20.9 us -> 23.9 us  [shards(): adjoints.append(lax.ppermute(adjoints[-1], 'snap', ring))]
    ppermute x9, waiting for transfers between devices: 15.6 us -> 13.5 us  [exchange(): lax.ppermute(give, 'rows', [(i, i ^ flip * stride) for i in range(count)])]
    pallas_call x0 -> x1, Pallas kernels: none -> 1.92 us  [end_rows(): pl.pallas_call(functools.partial(end_rows_kernel, start, last), in_specs=...]
    slice x2, local copies, waits for them, and re-layouts: 1.41 us -> 3.06 us  [shards(): primals = [[primal[a:b] for a, b in spans]]]
    dot_general x2, matrix products: 7.61 us -> 6.12 us  [inner_cols(): lax.dot_general(left, right, (((0,), (0,)), ((), ())), precision=HIGH, pr...]
  transfers between devices with their start and end apart: 12 -> 12, of which waited for: 6 -> 6; matrix products, arithmetic and copies ran while one was open for 27% -> 27% of each run, Pallas kernels for 14% -> 9%
where the time goes in v2:
time: 96.8 us; the launch traced here: 96.4 us
  waiting for transfers between devices  39.9 us (41%)
  matrix products  14.5 us (15%)
  starting transfers between devices  13.3 us (14%)
  local copies, waits for them, and re-layouts  12 us (12%)
  Pallas kernels  10.6 us (11%)
  other arithmetic  5.15 us (5%)
    ppermute x1, waiting for transfers between devices, shards(): adjoints.append(lax.ppermute(adjoints[-1], 'snap', ring))  23.9 us
    ppermute x9, waiting for transfers between devices, exchange(): lax.ppermute(give, 'rows', [(i, i ^ flip * stride) for i in range(count)])  13.5 us
    pallas_call x2, Pallas kernels, add_rows(): pl.pallas_call(functools.partial(add_rows_kernel, last), grid=(x.shape[0]...  8.42 us
    ppermute x9, starting transfers between devices, exchange(): lax.ppermute(give, 'rows', [(i, i ^ flip * stride) for i in range(count)])  8.42 us
    dot_general x2, matrix products, mul(): jnp.dot(left, right, precision=HIGH, preferred_element_type=jnp.float32)  8.4 us
    dot_general x2, matrix products, inner_cols(): lax.dot_general(left, right, (((0,), (0,)), ((), ())), precision=HIGH, pr...  6.12 us
    unnamed x32, local copies, waits for them, and re-layouts  5.41 us
    slice x2, local copies, waits for them, and re-layouts, shards(): primals = [[primal[a:b] for a, b in spans]]  3.06 us
  transfers between devices with their start and end apart: 12, of which 6 were waited for; matrix products, arithmetic and copies ran while one was open for 27% of the time, Pallas kernels for 9%

profile of v2, /device:TPU:0, one launch (start us, length us, event | category | flops | bytes accessed | tf_op | source)
XLA Modules:
  0.0 96.4 jit_solution(4216096115598204258)
XLA Ops:
  0.6 3.0 %collective-permute-start = (f32[1024,512]{1,0:T(8,128)}, f32[1024,512]{1,0:T(8,128)S(1)}, u32[]{:S(2)}, u32[]{:S(2)}) collective-permute-start(f32[1024,512]{1,0:T(8,128)} %param.6), channel_id=1, source_target_pairs={{0,1},{1,0},{2,3},{3,2},{4,5},{5,4},{6,7},{7,6},{8,9},{9,8},{10,11... | collective-permute-start | bytes 6291464 | tf_op jit(solution)/shard_map/ppermute | solution.py:147
  3.7 4.2 %fusion.21 = f32[512,512]{1,0:T(8,128)S(1)} fusion(f32[1024,512]{1,0:T(8,128)} %param.6, f32[1024,512]{1,0:T(8,128)} %param.5), kind=kOutput, calls=%fused_computation.42 | convolution fusion | flops 1610612736 | bytes 5242880 | tf_op jit(solution)/shard_map/dot_general | solution.py:40
  8.8 1.5 %collective-permute-start.2 = (f32[2,64,512]{2,1,0:T(8,128)}, f32[2,64,512]{2,1,0:T(8,128)}, u32[]{:S(2)}, u32[]{:S(2)}) collective-permute-start(f32[2,64,512]{2,1,0:T(8,128)} %get-tuple-element.40), channel_id=1, source_target_pairs={{0,4},{2,6},{4,0},{6,2},{8,12},{10,14},{12,8},{14,10},{16,20},{18,... | collective-permute-start | bytes 786440 | tf_op jit(solution)/shard_map/ppermute | solution.py:118
  10.7 1.4 %slice.6 = f32[896,512]{1,0:T(8,128)} slice(f32[1024,512]{1,0:T(8,128)S(1)} %copy-done.4), slice={[0:896], [0:512]} | slice | bytes 3670016 | tf_op jit(solution)/shard_map/slice | solution.py:145
  12.4 1.7 %constant_dynamic-slice_fusion = (f32[512,512]{1,0:T(8,128)S(1)}, f32[512,512]{1,0:T(8,128)S(1)}) fusion(f32[1024,512]{1,0:T(8,128)} %param.7, s32[]{:T(128)S(6)} %select_n.81, f32[1024,512]{1,0:T(8,128)} %param.8), kind=kLoop, calls=%fused_computation.40 | loop fusion | bytes 4194308 | tf_op jit(solution)/shard_map/dynamic_slice | solution.py:134
  16.1 5.2 %convolution_bitcast_fusion.total_ref = f32[1024,512]{1,0:T(8,128)} fusion(f32[1024,512]{1,0:T(8,128)} %param.5, f32[1024,512]{1,0:T(8,128)} %param.7, s32[]{:T(128)S(6)} %select_n.87), kind=kOutput, calls=%fused_computation | convolution fusion | flops 1610612736 | bytes 5242884 | tf_op jit(solution)/shard_map/dot_general | solution.py:14
  21.3 3.2 %convolution_bitcast_fusion.1.total_ref = f32[1024,512]{1,0:T(8,128)} fusion(f32[1024,512]{1,0:T(8,128)S(1)} %copy-done.6, f32[1024,512]{1,0:T(8,128)S(1)} %copy-done.13, s32[]{:T(128)S(6)} %select_n.87), kind=kOutput, calls=%fused_computation.1 | convolution fusion | flops 1610612736 | bytes 5242884 | tf_op jit(solution)/shard_map/dot_general | solution.py:14
  25.2 1.3 %fusion.5 = f32[2,64,512]{2,1,0:T(8,128)S(1)} fusion(f32[2,64,512]{2,1,0:T(8,128)} %collective-permute-done.3, f32[2,64,512]{2,1,0:T(8,128)} %collective-permute-done.2, f32[2,64,512]{2,1,0:T(8,128)} %copy-done.14, f32[2,4,64,512]{3,2,1,0:T(8,128)} %bitcast.60, s32[]{:T(128)S(6)} %select_n.83), kind=kLoop, calls=%fused_computation.17 | loop fusion | flops 196608 | bytes 1310724 | tf_op jit(solution)/shard_map/add | solution.py:118
  26.4 23.9 %collective-permute-done.x_ref = f32[1024,512]{1,0:T(8,128)S(1)} collective-permute-done((f32[1024,512]{1,0:T(8,128)}, f32[1024,512]{1,0:T(8,128)S(1)}, u32[]{:S(2)}, u32[]{:S(2)}) %collective-permute-start) | collective-permute-done | bytes 2097184 | tf_op jit(solution)/shard_map/ppermute | solution.py:147
  50.3 1.9 %fusion.22 = f32[512,512]{1,0:T(8,128)S(1)} fusion(f32[1024,512]{1,0:T(8,128)S(1)} %collective-permute-done.x_ref, f32[1024,512]{1,0:T(8,128)S(1)} %copy-done.5), kind=kOutput, calls=%fused_computation.43 | convolution fusion | flops 1610612736 | bytes 5242880 | tf_op jit(solution)/shard_map/dot_general | solution.py:40
  54.2 2.0 %collective-permute-start.5 = (f32[2,64,512]{2,1,0:T(8,128)}, f32[2,64,512]{2,1,0:T(8,128)}, u32[]{:S(2)}, u32[]{:S(2)}) collective-permute-start(f32[2,64,512]{2,1,0:T(8,128)} %get-tuple-element.37), channel_id=1, source_target_pairs={{0,4},{2,6},{4,0},{6,2},{8,12},{10,14},{12,8},{14,10},{16,20},{18,... | collective-permute-start | bytes 786440 | tf_op jit(solution)/shard_map/ppermute | solution.py:118
  56.3 7.3 %collective-permute-done.5 = f32[2,64,512]{2,1,0:T(8,128)} collective-permute-done((f32[2,64,512]{2,1,0:T(8,128)}, f32[2,64,512]{2,1,0:T(8,128)}, u32[]{:S(2)}, u32[]{:S(2)}) %collective-permute-start.5) | collective-permute-done | bytes 262176 | tf_op jit(solution)/shard_map/ppermute | solution.py:118
  63.7 5.2 %collective-permute-done.6 = f32[2,64,512]{2,1,0:T(8,128)} collective-permute-done((f32[2,64,512]{2,1,0:T(8,128)}, f32[2,64,512]{2,1,0:T(8,128)}, u32[]{:S(2)}, u32[]{:S(2)}) %collective-permute-start.6) | collective-permute-done | bytes 262176 | tf_op jit(solution)/shard_map/ppermute | solution.py:118
  68.9 1.3 %broadcast_select_fusion = (f32[2,64,512]{2,1,0:T(8,128)S(1)}, f32[2,64,512]{2,1,0:T(8,128)S(1)}) fusion(f32[2,64,512]{2,1,0:T(8,128)S(1)} %fusion.5, pred[]{:T(512)S(6)} %eq.9, f32[2,64,512]{2,1,0:T(8,128)} %collective-permute-done.6, f32[2,64,512]{2,1,0:T(8,128)} %collective-permute-done.5, f32[2,64,512]{2,1,0:T(8,128)} %collective-permute-done.4, ...), kind=kLoop, calls=%fused_computation.36 | loop fusion | flops 262144 | bytes 1835013 | tf_op jit(solution)/shard_map/jit(_where)/select_n | solution.py:167
  71.1 1.6 %collective-permute-start.7 = (f32[64,512]{1,0:T(8,128)}, f32[64,512]{1,0:T(8,128)}, u32[]{:S(2)}, u32[]{:S(2)}) collective-permute-start(f32[64,512]{1,0:T(8,128)} %get-tuple-element.41), channel_id=1, source_target_pairs={{0,8},{2,10},{4,12},{6,14},{8,0},{10,2},{12,4},{14,6},{16,24},{18,... | collective-permute-start | bytes 393224 | tf_op jit(solution)/shard_map/ppermute | solution.py:118
  72.7 2.6 %collective-permute-start.8 = (f32[64,512]{1,0:T(8,128)}, f32[64,512]{1,0:T(8,128)}, u32[]{:S(2)}, u32[]{:S(2)}) collective-permute-start(f32[64,512]{1,0:T(8,128)} %get-tuple-element.42), channel_id=1, source_target_pairs={{0,16},{2,18},{4,20},{6,22},{8,24},{10,26},{12,28},{14,30},{16,0},... | collective-permute-start | bytes 393224 | tf_op jit(solution)/shard_map/ppermute | solution.py:118
  75.5 1.7 %slice.7 = f32[128,512]{1,0:T(8,128)} slice(f32[1024,512]{1,0:T(8,128)} %param.5), slice={[896:1024], [0:512]} | slice | bytes 524288 | tf_op jit(solution)/shard_map/slice | solution.py:145
  77.1 1.6 %collective-permute-start.11 = (f32[128,512]{1,0:T(8,128)}, f32[128,512]{1,0:T(8,128)S(1)}, u32[]{:S(2)}, u32[]{:S(2)}) collective-permute-start(f32[128,512]{1,0:T(8,128)} %slice.7), channel_id=1, source_target_pairs={{0,1},{1,0},{2,3},{3,2},{4,5},{5,4},{6,7},{7,6},{8,9},{9,8},{10,11... | collective-permute-start | bytes 786440 | tf_op jit(solution)/shard_map/ppermute | solution.py:148
  78.7 1.0 %copy-done.1 = bf16[512,512]{1,0:T(8,128)(2,1)S(1)} copy-done((bf16[512,512]{1,0:T(8,128)(2,1)S(1)}, bf16[512,512]{1,0:T(8,128)(2,1)}, u32[]{:S(2)}) %copy-start.1) | copy-done | bytes 524312
  80.8 4.2 %shard_map.78 = f32[1024,512]{1,0:T(8,128)} custom-call(f32[1024,512]{1,0:T(8,128)} %convolution_bitcast_fusion.1.total_ref, f32[1024,512]{1,0:T(8,128)S(1)} %collective-permute-done.x_ref, bf16[512,512]{1,0:T(8,128)(2,1)S(1)} %copy-done.1, bf16[512,512]{1,0:T(8,128)(2,1)S(1)} %copy-done.3, f32[1,512]{1,0:T(1,128)S(1)} %bitcast.54), custom_call_target="tpu_custom_call", output_to_operand_aliasing={{}: (0, {})} | custom-call | tf_op jit(solution)/shard_map/pallas_call | solution.py:60
  85.9 1.7 %fusion.13 = f32[64,512]{1,0:T(8,128)} fusion(f32[64,512]{1,0:T(8,128)} %collective-permute-done.9, f32[64,512]{1,0:T(8,128)} %collective-permute-done.8, f32[64,512]{1,0:T(8,128)} %collective-permute-done.7, s32[]{:T(128)S(6)} %select_n.92, f32[2,64,512]{2,1,0:T(8,128)S(1)} %copy-done.12, f32[2,64,512]{2,1,0:T(8,128)S(1)} %copy-done.10), kind=kLoop, calls=%fused_computation.31 | loop fusion | flops 163840 | bytes 1048580 | tf_op jit(solution)/shard_map/mul | solution.py:170
  87.7 2.1 %collective-permute-done.10.x_ref = f32[896,512]{1,0:T(8,128)} collective-permute-done((f32[896,512]{1,0:T(8,128)}, f32[896,512]{1,0:T(8,128)}, u32[]{:S(2)}, u32[]{:S(2)}) %collective-permute-start.10) | collective-permute-done | bytes 1835040 | tf_op jit(solution)/shard_map/ppermute | solution.py:148
  89.8 4.2 %shard_map.79.total_ref = f32[1024,512]{1,0:T(8,128)} custom-call(f32[1024,512]{1,0:T(8,128)} %convolution_bitcast_fusion.total_ref, f32[896,512]{1,0:T(8,128)} %collective-permute-done.10.x_ref, bf16[512,512]{1,0:T(8,128)(2,1)S(1)} %get-tuple-element.30.high_ref, bf16[512,512]{1,0:T(8,128)(2,1)S(1)} %get-tuple-element.31.low_ref, ...), custom_call_target="tpu_custom_call", output_to_operand_aliasing={{}: (0, {})} | custom-call | tf_op jit(solution)/shard_map/pallas_call | solution.py:60
  94.4 1.9 %shard_map.80 = f32[1024,512]{1,0:T(8,128)} custom-call(f32[1024,512]{1,0:T(8,128)} %shard_map.79.total_ref, f32[128,512]{1,0:T(8,128)S(1)} %collective-permute-done.11.x_ref, bf16[512,512]{1,0:T(8,128)(2,1)S(1)} %get-tuple-element.30.high_ref, bf16[512,512]{1,0:T(8,128)(2,1)S(1)} %get-tuple-element.31.low_ref, ...), custom_call_target="tpu_custom_call", output_to_operand_aliasing={{}: (0, {})} | custom-call | tf_op jit(solution)/shard_map/pallas_call | solution.py:96
  (52 shorter events, 9.7 us)
Async XLA Ops:
  0.6 49.7 %collective-permute-start = (f32[1024,512]{1,0:T(8,128)}, f32[1024,512]{1,0:T(8,128)S(1)}, u32[]{:S(2)}, u32[]{:S(2)}) collective-permute-start(f32[1024,512]{1,0:T(8,128)} %param.6), channel_id=1, source_target_pairs={{0,1},{1,0},{2,3},{3,2},{4,5},{5,4},{6,7},{7,6},{8,9},{9,8},{10,11... | collective-permute-start | bytes 6291464 | tf_op jit(solution)/shard_map/ppermute | solution.py:147
  3.7 7.0 %copy-start.4 = (f32[1024,512]{1,0:T(8,128)S(1)}, f32[1024,512]{1,0:T(8,128)}, u32[]{:S(2)}) copy-start(f32[1024,512]{1,0:T(8,128)} %param.5) | copy-start | bytes 6291460
  7.9 4.2 %copy-start.8 = (f32[512,512]{1,0:T(8,128)}, f32[512,512]{1,0:T(8,128)S(1)}, u32[]{:S(2)}) copy-start(f32[512,512]{1,0:T(8,128)S(1)} %fusion.21) | copy-start | bytes 3145732
  8.8 15.6 %collective-permute-start.1 = (f32[2,64,512]{2,1,0:T(8,128)}, f32[2,64,512]{2,1,0:T(8,128)S(1)}, u32[]{:S(2)}, u32[]{:S(2)}) collective-permute-start(f32[2,64,512]{2,1,0:T(8,128)} %get-tuple-element.38), channel_id=1, source_target_pairs={{0,2},{2,0},{4,6},{6,4},{8,10},{10,8},{12,14},{14,12},{16,18},{18,... | collective-permute-start | bytes 786440 | tf_op jit(solution)/shard_map/ppermute | solution.py:118
  8.8 15.6 %collective-permute-start.2 = (f32[2,64,512]{2,1,0:T(8,128)}, f32[2,64,512]{2,1,0:T(8,128)}, u32[]{:S(2)}, u32[]{:S(2)}) collective-permute-start(f32[2,64,512]{2,1,0:T(8,128)} %get-tuple-element.40), channel_id=1, source_target_pairs={{0,4},{2,6},{4,0},{6,2},{8,12},{10,14},{12,8},{14,10},{16,20},{18,... | collective-permute-start | bytes 786440 | tf_op jit(solution)/shard_map/ppermute | solution.py:118
  10.3 14.8 %collective-permute-start.3 = (f32[2,64,512]{2,1,0:T(8,128)}, f32[2,64,512]{2,1,0:T(8,128)}, u32[]{:S(2)}, u32[]{:S(2)}) collective-permute-start(f32[2,64,512]{2,1,0:T(8,128)} %get-tuple-element.39), channel_id=1, source_target_pairs={{0,6},{2,4},{4,2},{6,0},{8,14},{10,12},{12,10},{14,8},{16,22},{18,... | collective-permute-start | bytes 786440 | tf_op jit(solution)/shard_map/ppermute | solution.py:118
  12.1 77.7 %collective-permute-start.10 = (f32[896,512]{1,0:T(8,128)}, f32[896,512]{1,0:T(8,128)}, u32[]{:S(2)}, u32[]{:S(2)}) collective-permute-start(f32[896,512]{1,0:T(8,128)} %slice.6), channel_id=1, source_target_pairs={{0,1},{1,0},{2,3},{3,2},{4,5},{5,4},{6,7},{7,6},{8,9},{9,8},{10,11... | collective-permute-start | bytes 5505032 | tf_op jit(solution)/shard_map/ppermute | solution.py:148
  16.0 5.2 %copy-start.6 = (f32[1024,512]{1,0:T(8,128)S(1)}, f32[1024,512]{1,0:T(8,128)}, u32[]{:S(2)}) copy-start(f32[1024,512]{1,0:T(8,128)} %param.6) | copy-start | bytes 6291460
  16.0 5.2 %copy-start.13 = (f32[1024,512]{1,0:T(8,128)S(1)}, f32[1024,512]{1,0:T(8,128)}, u32[]{:S(2)}) copy-start(f32[1024,512]{1,0:T(8,128)} %param.8) | copy-start | bytes 6291460
  21.3 29.1 %copy-start.5 = (f32[1024,512]{1,0:T(8,128)S(1)}, f32[1024,512]{1,0:T(8,128)}, u32[]{:S(2)}) copy-start(f32[1024,512]{1,0:T(8,128)} %param.5) | copy-start | bytes 6291460
  54.2 24.6 %copy-start.15 = (f32[512]{0:T(512)S(1)}, f32[512]{0:T(512)}, u32[]{:S(2)}) copy-start(f32[512]{0:T(512)} %param.9) | copy-start | bytes 6148
  54.2 2.2 %collective-permute-start.4 = (f32[2,64,512]{2,1,0:T(8,128)}, f32[2,64,512]{2,1,0:T(8,128)}, u32[]{:S(2)}, u32[]{:S(2)}) collective-permute-start(f32[2,64,512]{2,1,0:T(8,128)} %get-tuple-element.35), channel_id=1, source_target_pairs={{0,2},{2,0},{4,6},{6,4},{8,10},{10,8},{12,14},{14,12},{16,18},{18,... | collective-permute-start | bytes 786440 | tf_op jit(solution)/shard_map/ppermute | solution.py:118
  54.2 9.5 %collective-permute-start.5 = (f32[2,64,512]{2,1,0:T(8,128)}, f32[2,64,512]{2,1,0:T(8,128)}, u32[]{:S(2)}, u32[]{:S(2)}) collective-permute-start(f32[2,64,512]{2,1,0:T(8,128)} %get-tuple-element.37), channel_id=1, source_target_pairs={{0,4},{2,6},{4,0},{6,2},{8,12},{10,14},{12,8},{14,10},{16,20},{18,... | collective-permute-start | bytes 786440 | tf_op jit(solution)/shard_map/ppermute | solution.py:118
  56.2 12.7 %collective-permute-start.6 = (f32[2,64,512]{2,1,0:T(8,128)}, f32[2,64,512]{2,1,0:T(8,128)}, u32[]{:S(2)}, u32[]{:S(2)}) collective-permute-start(f32[2,64,512]{2,1,0:T(8,128)} %get-tuple-element.36), channel_id=1, source_target_pairs={{0,6},{2,4},{4,2},{6,0},{8,14},{10,12},{12,10},{14,8},{16,22},{18,... | collective-permute-start | bytes 786440 | tf_op jit(solution)/shard_map/ppermute | solution.py:118
  70.2 5.3 %copy-start.9 = (f32[2,64,512]{2,1,0:T(8,128)}, f32[2,64,512]{2,1,0:T(8,128)S(1)}, u32[]{:S(2)}) copy-start(f32[2,64,512]{2,1,0:T(8,128)S(1)} %get-tuple-element.33) | copy-start | bytes 786436
  70.3 6.9 %copy-start.11 = (f32[2,64,512]{2,1,0:T(8,128)}, f32[2,64,512]{2,1,0:T(8,128)S(1)}, u32[]{:S(2)}) copy-start(f32[2,64,512]{2,1,0:T(8,128)S(1)} %broadcast_select_fusion.1) | copy-start | bytes 786436
  71.1 14.0 %collective-permute-start.7 = (f32[64,512]{1,0:T(8,128)}, f32[64,512]{1,0:T(8,128)}, u32[]{:S(2)}, u32[]{:S(2)}) collective-permute-start(f32[64,512]{1,0:T(8,128)} %get-tuple-element.41), channel_id=1, source_target_pairs={{0,8},{2,10},{4,12},{6,14},{8,0},{10,2},{12,4},{14,6},{16,24},{18,... | collective-permute-start | bytes 393224 | tf_op jit(solution)/shard_map/ppermute | solution.py:118
  72.7 13.2 %collective-permute-start.8 = (f32[64,512]{1,0:T(8,128)}, f32[64,512]{1,0:T(8,128)}, u32[]{:S(2)}, u32[]{:S(2)}) collective-permute-start(f32[64,512]{1,0:T(8,128)} %get-tuple-element.42), channel_id=1, source_target_pairs={{0,16},{2,18},{4,20},{6,22},{8,24},{10,26},{12,28},{14,30},{16,0},... | collective-permute-start | bytes 393224 | tf_op jit(solution)/shard_map/ppermute | solution.py:118
  75.3 10.6 %collective-permute-start.9 = (f32[64,512]{1,0:T(8,128)S(1)}, f32[64,512]{1,0:T(8,128)}, u32[]{:S(2)}, u32[]{:S(2)}) collective-permute-start(f32[64,512]{1,0:T(8,128)S(1)} %get-tuple-element.43), channel_id=1, source_target_pairs={{0,24},{2,26},{4,28},{6,30},{8,16},{10,18},{12,20},{14,22},{16,8},... | collective-permute-start | bytes 393224 | tf_op jit(solution)/shard_map/ppermute | solution.py:118
  77.1 17.3 %collective-permute-start.11 = (f32[128,512]{1,0:T(8,128)}, f32[128,512]{1,0:T(8,128)S(1)}, u32[]{:S(2)}, u32[]{:S(2)}) collective-permute-start(f32[128,512]{1,0:T(8,128)} %slice.7), channel_id=1, source_target_pairs={{0,1},{1,0},{2,3},{3,2},{4,5},{5,4},{6,7},{7,6},{8,9},{9,8},{10,11... | collective-permute-start | bytes 786440 | tf_op jit(solution)/shard_map/ppermute | solution.py:148
  78.7 1.0 %copy-start.1 = (bf16[512,512]{1,0:T(8,128)(2,1)S(1)}, bf16[512,512]{1,0:T(8,128)(2,1)}, u32[]{:S(2)}) copy-start(bf16[512,512]{1,0:T(8,128)(2,1)} %copy-done) | copy-start | bytes 1572868
  79.8 1.0 %copy-start.3 = (bf16[512,512]{1,0:T(8,128)(2,1)S(1)}, bf16[512,512]{1,0:T(8,128)(2,1)}, u32[]{:S(2)}) copy-start(bf16[512,512]{1,0:T(8,128)(2,1)} %copy-done.2) | copy-start | bytes 1572868
  80.8 5.1 %copy-start.10 = (f32[2,64,512]{2,1,0:T(8,128)S(1)}, f32[2,64,512]{2,1,0:T(8,128)}, u32[]{:S(2)}) copy-start(f32[2,64,512]{2,1,0:T(8,128)} %copy-done.9) | copy-start | bytes 786436
  80.8 5.1 %copy-start.12 = (f32[2,64,512]{2,1,0:T(8,128)S(1)}, f32[2,64,512]{2,1,0:T(8,128)}, u32[]{:S(2)}) copy-start(f32[2,64,512]{2,1,0:T(8,128)} %copy-done.11) | copy-start | bytes 786436
  (4 other events, 3.3 us)

commit v3 on v2

--- a/solution.py
+++ b/solution.py
@@ -75,37 +75,31 @@
     )(total, x, *matrix, weights[None])
 
 
-def end_rows_kernel(first, last, total_ref, x_ref, high_ref, low_ref, weights_ref, out_ref, held, sems):
-    rows = x_ref.shape[0]
-    fetch = pltpu.make_async_copy(total_ref.at[pl.ds(first, rows)], held, sems.at[0])
-    fetch.start()
+def end_rows_kernel(first, last, total_ref, own_ref, x_ref, high_ref, low_ref, weights_ref, out_ref, held, sem):
     dot = functools.partial(jnp.dot, preferred_element_type=jnp.float32)
     x_high, x_low = split(x_ref[...])
-    term = dot(x_high, high_ref[...]) + (dot(x_high, low_ref[...]) + dot(x_low, high_ref[...]))
-    fetch.wait()
-    total = held[...] + term
+    total = own_ref[...] + (
+        dot(x_high, high_ref[...]) + (dot(x_high, low_ref[...]) + dot(x_low, high_ref[...]))
+    )
     held[...] = total * weights_ref[...] if last else total
-    store = pltpu.make_async_copy(held, out_ref.at[pl.ds(first, rows)], sems.at[1])
+    store = pltpu.make_async_copy(held, out_ref.at[pl.ds(first, x_ref.shape[0])], sem)
     store.start()
     store.wait()
 
 
-def end_rows(total, x, matrix, weights, start, last):
+def end_rows(total, own, x, matrix, weights, start, last):
     vmem = pl.BlockSpec(memory_space=pltpu.VMEM)
     apart = pl.BlockSpec(memory_space=pl.ANY)
     return pl.pallas_call(
         functools.partial(end_rows_kernel, start, last),
-        in_specs=[apart, vmem, vmem, vmem, vmem],
+        in_specs=[apart, vmem, vmem, vmem, vmem, vmem],
         out_specs=apart,
         out_shape=jax.ShapeDtypeStruct(total.shape, total.dtype),
-        scratch_shapes=[
-            pltpu.VMEM((x.shape[0], total.shape[1]), jnp.float32),
-            pltpu.SemaphoreType.DMA((2,)),
-        ],
+        scratch_shapes=[pltpu.VMEM((x.shape[0], total.shape[1]), jnp.float32), pltpu.SemaphoreType.DMA],
         input_output_aliases={0: 0},
         cost_estimate=FREE,
         compiler_params=pltpu.CompilerParams(vmem_limit_bytes=LIMIT),
-    )(total, x, *matrix, weights[None])
+    )(total, own, x, *matrix, weights[None])
 
 
 def exchange(parts, axis, stride):
@@ -173,9 +167,10 @@
         for (start, stop), piece in zip(spans, primals[step]):
             last = step == sides - 1
             if start == 0:
+                own = phi[stop:]
                 phi = add_rows(phi, piece, rights[step - 1], weights, start, stop // 2, last)
             else:
-                phi = end_rows(phi, piece, rights[step - 1], weights, start, last)
+                phi = end_rows(phi, own, piece, rights[step - 1], weights, start, last)
     return (gram, phi, psi)
 
 

time: 96.8 us -> 95.9 us (level)
  local copies, waits for them, and re-layouts: 12 us -> 13 us
    ppermute x2, waiting for transfers between devices: 2.58 us -> 1.61 us  [shards(): primals.append([lax.ppermute(piece, 'snap', ring) for piece in primals[-1]])]
  transfers between devices with their start and end apart: 12 -> 12, of which waited for: 6 -> 6; matrix products, arithmetic and copies ran while one was open for 27% -> 29% of each run, Pallas kernels for 9% -> 9%
where the time goes in v3:
time: 95.9 us; the launch traced here: 95.5 us
  waiting for transfers between devices  39 us (41%)
  matrix products  14.5 us (15%)
  starting transfers between devices  13.3 us (14%)
  local copies, waits for them, and re-layouts  13 us (14%)
  Pallas kernels  9.8 us (10%)
  other arithmetic  5.15 us (5%)
    ppermute x1, waiting for transfers between devices, shards(): adjoints.append(lax.ppermute(adjoints[-1], 'snap', ring))  23.9 us
    ppermute x9, waiting for transfers between devices, exchange(): lax.ppermute(give, 'rows', [(i, i ^ flip * stride) for i in range(count)])  13.5 us
    pallas_call x2, Pallas kernels, add_rows(): pl.pallas_call(functools.partial(add_rows_kernel, last), grid=(x.shape[0]...  8.42 us
    ppermute x9, starting transfers between devices, exchange(): lax.ppermute(give, 'rows', [(i, i ^ flip * stride) for i in range(count)])  8.42 us
    dot_general x2, matrix products, mul(): jnp.dot(left, right, precision=HIGH, preferred_element_type=jnp.float32)  8.4 us
    dot_general x2, matrix products, inner_cols(): lax.dot_general(left, right, (((0,), (0,)), ((), ())), precision=HIGH, pr...  6.12 us
    unnamed x32, local copies, waits for them, and re-layouts  5.41 us
    slice x2, local copies, waits for them, and re-layouts, shards(): primals = [[primal[a:b] for a, b in spans]]  3.06 us
  transfers between devices with their start and end apart: 12, of which 6 were waited for; matrix products, arithmetic and copies ran while one was open for 29% of the time, Pallas kernels for 9%

profile of v3, /device:TPU:0, one launch (start us, length us, event | category | flops | bytes accessed | tf_op | source)
XLA Modules:
  0.0 95.5 jit_solution(2064235441169959515)
XLA Ops:
  0.6 3.0 %collective-permute-start = (f32[1024,512]{1,0:T(8,128)}, f32[1024,512]{1,0:T(8,128)S(1)}, u32[]{:S(2)}, u32[]{:S(2)}) collective-permute-start(f32[1024,512]{1,0:T(8,128)} %param.6), channel_id=1, source_target_pairs={{0,1},{1,0},{2,3},{3,2},{4,5},{5,4},{6,7},{7,6},{8,9},{9,8},{10,11... | collective-permute-start | bytes 6291464 | tf_op jit(solution)/shard_map/ppermute | solution.py:141
  3.7 4.2 %fusion.21 = f32[512,512]{1,0:T(8,128)S(1)} fusion(f32[1024,512]{1,0:T(8,128)} %param.6, f32[1024,512]{1,0:T(8,128)} %param.5), kind=kOutput, calls=%fused_computation.42 | convolution fusion | flops 1610612736 | bytes 5242880 | tf_op jit(solution)/shard_map/dot_general | solution.py:40
  8.8 1.5 %collective-permute-start.2 = (f32[2,64,512]{2,1,0:T(8,128)}, f32[2,64,512]{2,1,0:T(8,128)}, u32[]{:S(2)}, u32[]{:S(2)}) collective-permute-start(f32[2,64,512]{2,1,0:T(8,128)} %get-tuple-element.40), channel_id=1, source_target_pairs={{0,4},{2,6},{4,0},{6,2},{8,12},{10,14},{12,8},{14,10},{16,20},{18,... | collective-permute-start | bytes 786440 | tf_op jit(solution)/shard_map/ppermute | solution.py:112
  10.7 1.4 %slice.9 = f32[896,512]{1,0:T(8,128)} slice(f32[1024,512]{1,0:T(8,128)S(1)} %copy-done.4), slice={[0:896], [0:512]} | slice | bytes 3670016 | tf_op jit(solution)/shard_map/slice | solution.py:139
  12.4 1.7 %constant_dynamic-slice_fusion = (f32[512,512]{1,0:T(8,128)S(1)}, f32[512,512]{1,0:T(8,128)S(1)}) fusion(f32[1024,512]{1,0:T(8,128)} %param.7, s32[]{:T(128)S(6)} %select_n.81, f32[1024,512]{1,0:T(8,128)} %param.8), kind=kLoop, calls=%fused_computation.40 | loop fusion | bytes 4194308 | tf_op jit(solution)/shard_map/dynamic_slice | solution.py:128
  16.1 5.2 %convolution_bitcast_fusion.total_ref = f32[1024,512]{1,0:T(8,128)} fusion(f32[1024,512]{1,0:T(8,128)} %param.5, f32[1024,512]{1,0:T(8,128)} %param.7, s32[]{:T(128)S(6)} %select_n.87), kind=kOutput, calls=%fused_computation | convolution fusion | flops 1610612736 | bytes 5242884 | tf_op jit(solution)/shard_map/dot_general | solution.py:14
  21.3 3.2 %convolution_bitcast_fusion.1.total_ref = f32[1024,512]{1,0:T(8,128)} fusion(f32[1024,512]{1,0:T(8,128)S(1)} %copy-done.6, f32[1024,512]{1,0:T(8,128)S(1)} %copy-done.13, s32[]{:T(128)S(6)} %select_n.87), kind=kOutput, calls=%fused_computation.1 | convolution fusion | flops 1610612736 | bytes 5242884 | tf_op jit(solution)/shard_map/dot_general | solution.py:14
  25.2 1.3 %fusion.5 = f32[2,64,512]{2,1,0:T(8,128)S(1)} fusion(f32[2,64,512]{2,1,0:T(8,128)} %collective-permute-done.3, f32[2,64,512]{2,1,0:T(8,128)} %collective-permute-done.2, f32[2,64,512]{2,1,0:T(8,128)} %copy-done.14, f32[2,4,64,512]{3,2,1,0:T(8,128)} %bitcast.60, s32[]{:T(128)S(6)} %select_n.83), kind=kLoop, calls=%fused_computation.17 | loop fusion | flops 196608 | bytes 1310724 | tf_op jit(solution)/shard_map/add | solution.py:112
  26.4 23.9 %collective-permute-done.x_ref = f32[1024,512]{1,0:T(8,128)S(1)} collective-permute-done((f32[1024,512]{1,0:T(8,128)}, f32[1024,512]{1,0:T(8,128)S(1)}, u32[]{:S(2)}, u32[]{:S(2)}) %collective-permute-start) | collective-permute-done | bytes 2097184 | tf_op jit(solution)/shard_map/ppermute | solution.py:141
  50.3 1.9 %fusion.22 = f32[512,512]{1,0:T(8,128)S(1)} fusion(f32[1024,512]{1,0:T(8,128)S(1)} %collective-permute-done.x_ref, f32[1024,512]{1,0:T(8,128)S(1)} %copy-done.5), kind=kOutput, calls=%fused_computation.43 | convolution fusion | flops 1610612736 | bytes 5242880 | tf_op jit(solution)/shard_map/dot_general | solution.py:40
  54.2 2.0 %collective-permute-start.5 = (f32[2,64,512]{2,1,0:T(8,128)}, f32[2,64,512]{2,1,0:T(8,128)}, u32[]{:S(2)}, u32[]{:S(2)}) collective-permute-start(f32[2,64,512]{2,1,0:T(8,128)} %get-tuple-element.37), channel_id=1, source_target_pairs={{0,4},{2,6},{4,0},{6,2},{8,12},{10,14},{12,8},{14,10},{16,20},{18,... | collective-permute-start | bytes 786440 | tf_op jit(solution)/shard_map/ppermute | solution.py:112
  56.3 7.3 %collective-permute-done.5 = f32[2,64,512]{2,1,0:T(8,128)} collective-permute-done((f32[2,64,512]{2,1,0:T(8,128)}, f32[2,64,512]{2,1,0:T(8,128)}, u32[]{:S(2)}, u32[]{:S(2)}) %collective-permute-start.5) | collective-permute-done | bytes 262176 | tf_op jit(solution)/shard_map/ppermute | solution.py:112
  63.7 5.2 %collective-permute-done.6 = f32[2,64,512]{2,1,0:T(8,128)} collective-permute-done((f32[2,64,512]{2,1,0:T(8,128)}, f32[2,64,512]{2,1,0:T(8,128)}, u32[]{:S(2)}, u32[]{:S(2)}) %collective-permute-start.6) | collective-permute-done | bytes 262176 | tf_op jit(solution)/shard_map/ppermute | solution.py:112
  68.9 1.3 %broadcast_select_fusion = (f32[2,64,512]{2,1,0:T(8,128)S(1)}, f32[2,64,512]{2,1,0:T(8,128)S(1)}) fusion(f32[2,64,512]{2,1,0:T(8,128)S(1)} %fusion.5, pred[]{:T(512)S(6)} %eq.9, f32[2,64,512]{2,1,0:T(8,128)} %collective-permute-done.6, f32[2,64,512]{2,1,0:T(8,128)} %collective-permute-done.5, f32[2,64,512]{2,1,0:T(8,128)} %collective-permute-done.4, ...), kind=kLoop, calls=%fused_computation.36 | loop fusion | flops 262144 | bytes 1835013 | tf_op jit(solution)/shard_map/jit(_where)/select_n | solution.py:161
  71.1 1.6 %collective-permute-start.7 = (f32[64,512]{1,0:T(8,128)}, f32[64,512]{1,0:T(8,128)}, u32[]{:S(2)}, u32[]{:S(2)}) collective-permute-start(f32[64,512]{1,0:T(8,128)} %get-tuple-element.41), channel_id=1, source_target_pairs={{0,8},{2,10},{4,12},{6,14},{8,0},{10,2},{12,4},{14,6},{16,24},{18,... | collective-permute-start | bytes 393224 | tf_op jit(solution)/shard_map/ppermute | solution.py:112
  72.7 2.6 %collective-permute-start.8 = (f32[64,512]{1,0:T(8,128)}, f32[64,512]{1,0:T(8,128)}, u32[]{:S(2)}, u32[]{:S(2)}) collective-permute-start(f32[64,512]{1,0:T(8,128)} %get-tuple-element.42), channel_id=1, source_target_pairs={{0,16},{2,18},{4,20},{6,22},{8,24},{10,26},{12,28},{14,30},{16,0},... | collective-permute-start | bytes 393224 | tf_op jit(solution)/shard_map/ppermute | solution.py:112
  75.5 1.7 %slice.11 = f32[128,512]{1,0:T(8,128)} slice(f32[1024,512]{1,0:T(8,128)} %param.5), slice={[896:1024], [0:512]} | slice | bytes 524288 | tf_op jit(solution)/shard_map/slice | solution.py:139
  77.1 1.6 %collective-permute-start.11 = (f32[128,512]{1,0:T(8,128)}, f32[128,512]{1,0:T(8,128)S(1)}, u32[]{:S(2)}, u32[]{:S(2)}) collective-permute-start(f32[128,512]{1,0:T(8,128)} %slice.11), channel_id=1, source_target_pairs={{0,1},{1,0},{2,3},{3,2},{4,5},{5,4},{6,7},{7,6},{8,9},{9,8},{10,11... | collective-permute-start | bytes 786440 | tf_op jit(solution)/shard_map/ppermute | solution.py:142
  78.7 1.0 %copy-done.1 = bf16[512,512]{1,0:T(8,128)(2,1)S(1)} copy-done((bf16[512,512]{1,0:T(8,128)(2,1)S(1)}, bf16[512,512]{1,0:T(8,128)(2,1)}, u32[]{:S(2)}) %copy-start.1) | copy-done | bytes 524312
  80.8 4.2 %shard_map.78 = f32[1024,512]{1,0:T(8,128)} custom-call(f32[1024,512]{1,0:T(8,128)} %convolution_bitcast_fusion.1.total_ref, f32[1024,512]{1,0:T(8,128)S(1)} %collective-permute-done.x_ref, bf16[512,512]{1,0:T(8,128)(2,1)S(1)} %copy-done.1, bf16[512,512]{1,0:T(8,128)(2,1)S(1)} %copy-done.3, f32[1,512]{1,0:T(1,128)S(1)} %bitcast.54), custom_call_target="tpu_custom_call", output_to_operand_aliasing={{}: (0, {})} | custom-call | tf_op jit(solution)/shard_map/pallas_call | solution.py:60
  85.9 1.7 %fusion.13 = f32[64,512]{1,0:T(8,128)} fusion(f32[64,512]{1,0:T(8,128)} %collective-permute-done.9, f32[64,512]{1,0:T(8,128)} %collective-permute-done.8, f32[64,512]{1,0:T(8,128)} %collective-permute-done.7, s32[]{:T(128)S(6)} %select_n.92, f32[2,64,512]{2,1,0:T(8,128)S(1)} %copy-done.12, f32[2,64,512]{2,1,0:T(8,128)S(1)} %copy-done.10), kind=kLoop, calls=%fused_computation.31 | loop fusion | flops 163840 | bytes 1048580 | tf_op jit(solution)/shard_map/mul | solution.py:164
  88.6 1.1 %collective-permute-done.10.x_ref = f32[896,512]{1,0:T(8,128)} collective-permute-done((f32[896,512]{1,0:T(8,128)}, f32[896,512]{1,0:T(8,128)}, u32[]{:S(2)}, u32[]{:S(2)}) %collective-permute-start.10) | collective-permute-done | bytes 1835040 | tf_op jit(solution)/shard_map/ppermute | solution.py:142
  89.8 4.2 %shard_map.79.total_ref = f32[1024,512]{1,0:T(8,128)} custom-call(f32[1024,512]{1,0:T(8,128)} %convolution_bitcast_fusion.total_ref, f32[896,512]{1,0:T(8,128)} %collective-permute-done.10.x_ref, bf16[512,512]{1,0:T(8,128)(2,1)S(1)} %get-tuple-element.30.high_ref, bf16[512,512]{1,0:T(8,128)(2,1)S(1)} %get-tuple-element.31.low_ref, ...), custom_call_target="tpu_custom_call", output_to_operand_aliasing={{}: (0, {})} | custom-call | tf_op jit(solution)/shard_map/pallas_call | solution.py:60
  94.4 1.1 %shard_map.80 = f32[1024,512]{1,0:T(8,128)} custom-call(f32[1024,512]{1,0:T(8,128)} %shard_map.79.total_ref, f32[128,512]{1,0:T(8,128)S(1)} %slice.10.own_ref, f32[128,512]{1,0:T(8,128)S(1)} %collective-permute-done.11.x_ref, bf16[512,512]{1,0:T(8,128)(2,1)S(1)} %get-tuple-element.30.high_ref, ...), custom_call_target="tpu_custom_call", output_to_operand_aliasing={{}: (0, {})} | custom-call | tf_op jit(solution)/shard_map/pallas_call | solution.py:93
  (53 shorter events, 10.7 us)
Async XLA Ops:
  0.6 49.7 %collective-permute-start = (f32[1024,512]{1,0:T(8,128)}, f32[1024,512]{1,0:T(8,128)S(1)}, u32[]{:S(2)}, u32[]{:S(2)}) collective-permute-start(f32[1024,512]{1,0:T(8,128)} %param.6), channel_id=1, source_target_pairs={{0,1},{1,0},{2,3},{3,2},{4,5},{5,4},{6,7},{7,6},{8,9},{9,8},{10,11... | collective-permute-start | bytes 6291464 | tf_op jit(solution)/shard_map/ppermute | solution.py:141
  3.7 7.0 %copy-start.4 = (f32[1024,512]{1,0:T(8,128)S(1)}, f32[1024,512]{1,0:T(8,128)}, u32[]{:S(2)}) copy-start(f32[1024,512]{1,0:T(8,128)} %param.5) | copy-start | bytes 6291460
  7.9 4.2 %copy-start.8 = (f32[512,512]{1,0:T(8,128)}, f32[512,512]{1,0:T(8,128)S(1)}, u32[]{:S(2)}) copy-start(f32[512,512]{1,0:T(8,128)S(1)} %fusion.21) | copy-start | bytes 3145732
  8.8 15.6 %collective-permute-start.1 = (f32[2,64,512]{2,1,0:T(8,128)}, f32[2,64,512]{2,1,0:T(8,128)S(1)}, u32[]{:S(2)}, u32[]{:S(2)}) collective-permute-start(f32[2,64,512]{2,1,0:T(8,128)} %get-tuple-element.38), channel_id=1, source_target_pairs={{0,2},{2,0},{4,6},{6,4},{8,10},{10,8},{12,14},{14,12},{16,18},{18,... | collective-permute-start | bytes 786440 | tf_op jit(solution)/shard_map/ppermute | solution.py:112
  8.8 15.6 %collective-permute-start.2 = (f32[2,64,512]{2,1,0:T(8,128)}, f32[2,64,512]{2,1,0:T(8,128)}, u32[]{:S(2)}, u32[]{:S(2)}) collective-permute-start(f32[2,64,512]{2,1,0:T(8,128)} %get-tuple-element.40), channel_id=1, source_target_pairs={{0,4},{2,6},{4,0},{6,2},{8,12},{10,14},{12,8},{14,10},{16,20},{18,... | collective-permute-start | bytes 786440 | tf_op jit(solution)/shard_map/ppermute | solution.py:112
  10.3 14.8 %collective-permute-start.3 = (f32[2,64,512]{2,1,0:T(8,128)}, f32[2,64,512]{2,1,0:T(8,128)}, u32[]{:S(2)}, u32[]{:S(2)}) collective-permute-start(f32[2,64,512]{2,1,0:T(8,128)} %get-tuple-element.39), channel_id=1, source_target_pairs={{0,6},{2,4},{4,2},{6,0},{8,14},{10,12},{12,10},{14,8},{16,22},{18,... | collective-permute-start | bytes 786440 | tf_op jit(solution)/shard_map/ppermute | solution.py:112
  12.1 77.7 %collective-permute-start.10 = (f32[896,512]{1,0:T(8,128)}, f32[896,512]{1,0:T(8,128)}, u32[]{:S(2)}, u32[]{:S(2)}) collective-permute-start(f32[896,512]{1,0:T(8,128)} %slice.9), channel_id=1, source_target_pairs={{0,1},{1,0},{2,3},{3,2},{4,5},{5,4},{6,7},{7,6},{8,9},{9,8},{10,11... | collective-permute-start | bytes 5505032 | tf_op jit(solution)/shard_map/ppermute | solution.py:142
  16.0 5.2 %copy-start.6 = (f32[1024,512]{1,0:T(8,128)S(1)}, f32[1024,512]{1,0:T(8,128)}, u32[]{:S(2)}) copy-start(f32[1024,512]{1,0:T(8,128)} %param.6) | copy-start | bytes 6291460
  16.0 5.2 %copy-start.13 = (f32[1024,512]{1,0:T(8,128)S(1)}, f32[1024,512]{1,0:T(8,128)}, u32[]{:S(2)}) copy-start(f32[1024,512]{1,0:T(8,128)} %param.8) | copy-start | bytes 6291460
  21.3 29.1 %copy-start.5 = (f32[1024,512]{1,0:T(8,128)S(1)}, f32[1024,512]{1,0:T(8,128)}, u32[]{:S(2)}) copy-start(f32[1024,512]{1,0:T(8,128)} %param.5) | copy-start | bytes 6291460
  54.2 24.6 %copy-start.15 = (f32[512]{0:T(512)S(1)}, f32[512]{0:T(512)}, u32[]{:S(2)}) copy-start(f32[512]{0:T(512)} %param.9) | copy-start | bytes 6148
  54.2 2.2 %collective-permute-start.4 = (f32[2,64,512]{2,1,0:T(8,128)}, f32[2,64,512]{2,1,0:T(8,128)}, u32[]{:S(2)}, u32[]{:S(2)}) collective-permute-start(f32[2,64,512]{2,1,0:T(8,128)} %get-tuple-element.35), channel_id=1, source_target_pairs={{0,2},{2,0},{4,6},{6,4},{8,10},{10,8},{12,14},{14,12},{16,18},{18,... | collective-permute-start | bytes 786440 | tf_op jit(solution)/shard_map/ppermute | solution.py:112
  54.2 9.5 %collective-permute-start.5 = (f32[2,64,512]{2,1,0:T(8,128)}, f32[2,64,512]{2,1,0:T(8,128)}, u32[]{:S(2)}, u32[]{:S(2)}) collective-permute-start(f32[2,64,512]{2,1,0:T(8,128)} %get-tuple-element.37), channel_id=1, source_target_pairs={{0,4},{2,6},{4,0},{6,2},{8,12},{10,14},{12,8},{14,10},{16,20},{18,... | collective-permute-start | bytes 786440 | tf_op jit(solution)/shard_map/ppermute | solution.py:112
  56.2 12.7 %collective-permute-start.6 = (f32[2,64,512]{2,1,0:T(8,128)}, f32[2,64,512]{2,1,0:T(8,128)}, u32[]{:S(2)}, u32[]{:S(2)}) collective-permute-start(f32[2,64,512]{2,1,0:T(8,128)} %get-tuple-element.36), channel_id=1, source_target_pairs={{0,6},{2,4},{4,2},{6,0},{8,14},{10,12},{12,10},{14,8},{16,22},{18,... | collective-permute-start | bytes 786440 | tf_op jit(solution)/shard_map/ppermute | solution.py:112
  70.2 5.3 %copy-start.9 = (f32[2,64,512]{2,1,0:T(8,128)}, f32[2,64,512]{2,1,0:T(8,128)S(1)}, u32[]{:S(2)}) copy-start(f32[2,64,512]{2,1,0:T(8,128)S(1)} %get-tuple-element.33) | copy-start | bytes 786436
  70.3 6.9 %copy-start.11 = (f32[2,64,512]{2,1,0:T(8,128)}, f32[2,64,512]{2,1,0:T(8,128)S(1)}, u32[]{:S(2)}) copy-start(f32[2,64,512]{2,1,0:T(8,128)S(1)} %broadcast_select_fusion.1) | copy-start | bytes 786436
  71.1 14.0 %collective-permute-start.7 = (f32[64,512]{1,0:T(8,128)}, f32[64,512]{1,0:T(8,128)}, u32[]{:S(2)}, u32[]{:S(2)}) collective-permute-start(f32[64,512]{1,0:T(8,128)} %get-tuple-element.41), channel_id=1, source_target_pairs={{0,8},{2,10},{4,12},{6,14},{8,0},{10,2},{12,4},{14,6},{16,24},{18,... | collective-permute-start | bytes 393224 | tf_op jit(solution)/shard_map/ppermute | solution.py:112
  72.7 13.2 %collective-permute-start.8 = (f32[64,512]{1,0:T(8,128)}, f32[64,512]{1,0:T(8,128)}, u32[]{:S(2)}, u32[]{:S(2)}) collective-permute-start(f32[64,512]{1,0:T(8,128)} %get-tuple-element.42), channel_id=1, source_target_pairs={{0,16},{2,18},{4,20},{6,22},{8,24},{10,26},{12,28},{14,30},{16,0},... | collective-permute-start | bytes 393224 | tf_op jit(solution)/shard_map/ppermute | solution.py:112
  75.3 10.6 %collective-permute-start.9 = (f32[64,512]{1,0:T(8,128)S(1)}, f32[64,512]{1,0:T(8,128)}, u32[]{:S(2)}, u32[]{:S(2)}) collective-permute-start(f32[64,512]{1,0:T(8,128)S(1)} %get-tuple-element.43), channel_id=1, source_target_pairs={{0,24},{2,26},{4,28},{6,30},{8,16},{10,18},{12,20},{14,22},{16,8},... | collective-permute-start | bytes 393224 | tf_op jit(solution)/shard_map/ppermute | solution.py:112
  77.1 17.3 %collective-permute-start.11 = (f32[128,512]{1,0:T(8,128)}, f32[128,512]{1,0:T(8,128)S(1)}, u32[]{:S(2)}, u32[]{:S(2)}) collective-permute-start(f32[128,512]{1,0:T(8,128)} %slice.11), channel_id=1, source_target_pairs={{0,1},{1,0},{2,3},{3,2},{4,5},{5,4},{6,7},{7,6},{8,9},{9,8},{10,11... | collective-permute-start | bytes 786440 | tf_op jit(solution)/shard_map/ppermute | solution.py:142
  78.7 1.0 %copy-start.1 = (bf16[512,512]{1,0:T(8,128)(2,1)S(1)}, bf16[512,512]{1,0:T(8,128)(2,1)}, u32[]{:S(2)}) copy-start(bf16[512,512]{1,0:T(8,128)(2,1)} %copy-done) | copy-start | bytes 1572868
  79.8 1.0 %copy-start.3 = (bf16[512,512]{1,0:T(8,128)(2,1)S(1)}, bf16[512,512]{1,0:T(8,128)(2,1)}, u32[]{:S(2)}) copy-start(bf16[512,512]{1,0:T(8,128)(2,1)} %copy-done.2) | copy-start | bytes 1572868
  80.8 5.1 %copy-start.10 = (f32[2,64,512]{2,1,0:T(8,128)S(1)}, f32[2,64,512]{2,1,0:T(8,128)}, u32[]{:S(2)}) copy-start(f32[2,64,512]{2,1,0:T(8,128)} %copy-done.9) | copy-start | bytes 786436
  80.8 5.1 %copy-start.12 = (f32[2,64,512]{2,1,0:T(8,128)S(1)}, f32[2,64,512]{2,1,0:T(8,128)}, u32[]{:S(2)}) copy-start(f32[2,64,512]{2,1,0:T(8,128)} %copy-done.11) | copy-start | bytes 786436
  (4 other events, 3.3 us)

commit v4 on v3

--- a/solution.py
+++ b/solution.py
@@ -25,13 +25,14 @@
 
 LIMIT = 16 << 20
 FREE = pl.CostEstimate(flops=0, bytes_accessed=0, transcendentals=0)
-
-
-def split_matrix(matrix):
+LONG = pl.CostEstimate(flops=6_000_000_000, bytes_accessed=0, transcendentals=0)
+
+
+def split_matrix(matrix, cost=FREE):
     return pl.pallas_call(
         split_kernel,
         out_shape=[jax.ShapeDtypeStruct(matrix.shape, jnp.bfloat16)] * 2,
-        cost_estimate=FREE,
+        cost_estimate=cost,
         compiler_params=pltpu.CompilerParams(vmem_limit_bytes=LIMIT),
     )(matrix)
 
@@ -75,31 +76,48 @@
     )(total, x, *matrix, weights[None])
 
 
-def end_rows_kernel(first, last, total_ref, own_ref, x_ref, high_ref, low_ref, weights_ref, out_ref, held, sem):
+def end_rows_kernel(total_ref, own_ref, *refs):
+    *x_refs, high_ref, low_ref, weights_ref, out_ref, held, sem = refs
     dot = functools.partial(jnp.dot, preferred_element_type=jnp.float32)
-    x_high, x_low = split(x_ref[...])
+    rows = held.shape[0]
+    x_high, x_low = split(jnp.concatenate([x_ref[...] for x_ref in x_refs]))
     total = own_ref[...] + (
         dot(x_high, high_ref[...]) + (dot(x_high, low_ref[...]) + dot(x_low, high_ref[...]))
     )
-    held[...] = total * weights_ref[...] if last else total
-    store = pltpu.make_async_copy(held, out_ref.at[pl.ds(first, x_ref.shape[0])], sem)
+    held[...] = total * weights_ref[...]
+    store = pltpu.make_async_copy(held, out_ref.at[pl.ds(out_ref.shape[0] - rows, rows)], sem)
     store.start()
     store.wait()
 
 
-def end_rows(total, own, x, matrix, weights, start, last):
+def end_rows(total, own, xs, matrix, weights):
     vmem = pl.BlockSpec(memory_space=pltpu.VMEM)
     apart = pl.BlockSpec(memory_space=pl.ANY)
     return pl.pallas_call(
-        functools.partial(end_rows_kernel, start, last),
-        in_specs=[apart, vmem, vmem, vmem, vmem, vmem],
+        end_rows_kernel,
+        in_specs=[apart] + [vmem] * (4 + len(xs)),
         out_specs=apart,
         out_shape=jax.ShapeDtypeStruct(total.shape, total.dtype),
-        scratch_shapes=[pltpu.VMEM((x.shape[0], total.shape[1]), jnp.float32), pltpu.SemaphoreType.DMA],
+        scratch_shapes=[pltpu.VMEM(own.shape, jnp.float32), pltpu.SemaphoreType.DMA],
         input_output_aliases={0: 0},
         cost_estimate=FREE,
         compiler_params=pltpu.CompilerParams(vmem_limit_bytes=LIMIT),
-    )(total, own, x, *matrix, weights[None])
+    )(total, own, *xs, *matrix, weights[None])
+
+
+def swap(x):
+    return lax.ppermute(x, "rows", [(i, i ^ 1) for i in range(lax.axis_size("rows"))])
+
+
+def pass_on(x, parity):
+    count = lax.axis_size("rows")
+    sides = lax.axis_size("snap")
+    pairs = [
+        (row * sides + side, row * sides + (side + 1) % sides)
+        for row in range(parity, count, 2)
+        for side in range(sides)
+    ]
+    return lax.ppermute(x, ("rows", "snap"), pairs)
 
 
 def exchange(parts, axis, stride):
@@ -121,7 +139,7 @@
     weights = 1.0 / jnp.sqrt(singular)
     norm = 1.0 / jnp.sqrt(jnp.float32(rows * count))
     ring = [(i, (i + 1) % sides) for i in range(sides)]
-    cuts = [0, rows * 7 // 8, rows]
+    cuts = [0, rows * 27 // 32, rows * 28 // 32, rows]
     spans = list(zip(cuts[:-1], cuts[1:]))
 
     def block(matrix, owner):
@@ -137,23 +155,41 @@
 
     adjoints = [adjoint]
     primals = [[primal[a:b] for a, b in spans]]
-    for step in range(1, sides):
-        adjoints.append(lax.ppermute(adjoints[-1], "snap", ring))
+    for step in range(1, sides - 1):
         primals.append([lax.ppermute(piece, "snap", ring) for piece in primals[-1]])
-
+    most, few, end = primals[-1]
+    odd = lax.axis_index("rows") % 2 == 1
     terms = [within(inner_cols(adjoint, primal))]
+    both, most, terms = lax.optimization_barrier(
+        (jnp.concatenate([few, swap(few)]), most, terms)
+    )
+    extra = pass_on(both, 1)
+    most, end = lax.ppermute(most, "snap", ring), lax.ppermute(end, "snap", ring)
     psi = mul(adjoint, block(left_vectors, side))
     phi = mul(primal, block(right_vectors, side))
     rights = []
     for step in range(1, sides):
         owner = (side - step) % sides
-        left = split_matrix(block(left_vectors, owner))
+        left = block(left_vectors, owner)
+        if step == 1:
+            left, extra = lax.optimization_barrier((left, extra))
+            left = split_matrix(left, LONG)
+        else:
+            left = split_matrix(left)
         rights.append(split_matrix(block(right_vectors, owner)))
+        adjoints.append(lax.ppermute(adjoints[-1], "snap", ring))
         theirs, left, rights, terms, psi, phi = lax.optimization_barrier(
             (adjoints[step], left, rights, terms, psi, phi)
         )
         terms.append(within(inner_cols(theirs, primal)))
         psi = add_rows(psi, theirs, left, weights, 0, rows // 2, step == sides - 1)
+    back = swap(extra[few.shape[0] :])
+    few = jnp.where(odd, extra[: few.shape[0]], back)
+    for step in range(1, sides - 1):
+        for (start, stop), piece in zip(spans, primals[step]):
+            phi = add_rows(phi, piece, rights[step - 1], weights, start, stop - start, False)
+    phi = add_rows(phi, few, rights[-1], weights, cuts[1], len(few), True)
+    own = phi[cuts[2] :]
     blocks = [terms[-t % sides] for t in range(sides)]
     bit = 1
     while bit < sides:
@@ -162,15 +198,9 @@
         bit *= 2
     total = exchange(jnp.concatenate(blocks), 0, near)
     gram = total * norm
-    gram, psi, phi = lax.optimization_barrier((gram, psi, phi))
-    for step in range(1, sides):
-        for (start, stop), piece in zip(spans, primals[step]):
-            last = step == sides - 1
-            if start == 0:
-                own = phi[stop:]
-                phi = add_rows(phi, piece, rights[step - 1], weights, start, stop // 2, last)
-            else:
-                phi = end_rows(phi, own, piece, rights[step - 1], weights, start, last)
+    gram, psi, phi, own = lax.optimization_barrier((gram, psi, phi, own))
+    phi = add_rows(phi, most, rights[-1], weights, 0, cuts[1] // 2, True)
+    phi = end_rows(phi, own, [end], rights[-1], weights)
     return (gram, phi, psi)
 
 

time: 95.9 us -> 95.4 us (level)
  waiting for transfers between devices: 39 us -> 34.4 us
  starting transfers between devices: 13.3 us -> 16.6 us
  Pallas kernels: 9.8 us -> 11.9 us
  local copies, waits for them, and re-layouts: 13 us -> 11.5 us
  matrix products: 14.5 us -> 15.6 us
  other arithmetic: 5.15 us -> 4.11 us
    unnamed x32 -> x26, local copies, waits for them, and re-layouts: 5.41 us -> 1.63 us
    ppermute x1, waiting for transfers between devices: 23.9 us -> 20.5 us  [shards(): adjoints.append(lax.ppermute(adjoints[-1], 'snap', ring))]
    pallas_call x2 -> x3, Pallas kernels: 8.42 us -> 10.5 us  [add_rows(): pl.pallas_call(functools.partial(add_rows_kernel, last), grid=(x.shape[0]...]
    ppermute x9, starting transfers between devices: 8.42 us -> 10.4 us  [exchange(): lax.ppermute(give, 'rows', [(i, i ^ flip * stride) for i in range(count)])]
    ppermute x9, waiting for transfers between devices: 13.5 us -> 11.9 us  [exchange(): lax.ppermute(give, 'rows', [(i, i ^ flip * stride) for i in range(count)])]
    slice x2 -> x3, local copies, waits for them, and re-layouts: 3.06 us -> 4.51 us  [shards(): primals = [[primal[a:b] for a, b in spans]]]
    dot_general x2, matrix products: 6.12 us -> 7.55 us  [inner_cols(): lax.dot_general(left, right, (((0,), (0,)), ((), ())), precision=HIGH, pr...]
    ppermute x2 -> x5, starting transfers between devices: 1.85 us -> 3.13 us  [the longest x1 1.5 us: shards(): lax.ppermute(end, 'snap', ring)]
  transfers between devices with their start and end apart: 12 -> 15, of which waited for: 6 -> 7; matrix products, arithmetic and copies ran while one was open for 29% -> 31% of each run, Pallas kernels for 9% -> 11%
where the time goes in v4:
time: 95.4 us; the launch traced here: 95 us
  waiting for transfers between devices  34.4 us (36%)
  starting transfers between devices  16.6 us (17%)
  matrix products  15.6 us (16%)
  Pallas kernels  11.9 us (12%)
  local copies, waits for them, and re-layouts  11.5 us (12%)
  other arithmetic  4.11 us (4%)
    ppermute x1, waiting for transfers between devices, shards(): adjoints.append(lax.ppermute(adjoints[-1], 'snap', ring))  20.5 us
    ppermute x9, waiting for transfers between devices, exchange(): lax.ppermute(give, 'rows', [(i, i ^ flip * stride) for i in range(count)])  11.9 us
    pallas_call x3, Pallas kernels, add_rows(): pl.pallas_call(functools.partial(add_rows_kernel, last), grid=(x.shape[0]...  10.5 us
    ppermute x9, starting transfers between devices, exchange(): lax.ppermute(give, 'rows', [(i, i ^ flip * stride) for i in range(count)])  10.4 us
    dot_general x2, matrix products, mul(): jnp.dot(left, right, precision=HIGH, preferred_element_type=jnp.float32)  8.06 us
    dot_general x2, matrix products, inner_cols(): lax.dot_general(left, right, (((0,), (0,)), ((), ())), precision=HIGH, pr...  7.55 us
    slice x3, local copies, waits for them, and re-layouts, shards(): primals = [[primal[a:b] for a, b in spans]]  4.51 us
    ppermute x1, starting transfers between devices, shards(): adjoints.append(lax.ppermute(adjoints[-1], 'snap', ring))  3.03 us
  transfers between devices with their start and end apart: 15, of which 7 were waited for; matrix products, arithmetic and copies ran while one was open for 31% of the time, Pallas kernels for 11%

profile of v4, /device:TPU:0, one launch (start us, length us, event | category | flops | bytes accessed | tf_op | source)
XLA Modules:
  0.0 95.0 jit_solution(11654327697971064981)
XLA Ops:
  0.6 3.0 %collective-permute-start = (f32[1024,512]{1,0:T(8,128)}, f32[1024,512]{1,0:T(8,128)}, u32[]{:S(2)}, u32[]{:S(2)}) collective-permute-start(f32[1024,512]{1,0:T(8,128)} %param.6), channel_id=1, source_target_pairs={{0,1},{1,0},{2,3},{3,2},{4,5},{5,4},{6,7},{7,6},{8,9},{9,8},{10,11... | collective-permute-start | bytes 6291464 | tf_op jit(solution)/shard_map/ppermute | solution.py:180
  3.7 4.0 %fusion.21 = f32[512,512]{1,0:T(8,128)S(1)} fusion(f32[1024,512]{1,0:T(8,128)} %param.6, f32[1024,512]{1,0:T(8,128)} %param.5), kind=kOutput, calls=%fused_computation.44 | convolution fusion | flops 1610612736 | bytes 5242880 | tf_op jit(solution)/shard_map/dot_general | solution.py:41
  8.8 1.5 %collective-permute-start.3 = (f32[2,64,512]{2,1,0:T(8,128)}, f32[2,64,512]{2,1,0:T(8,128)}, u32[]{:S(2)}, u32[]{:S(2)}) collective-permute-start(f32[2,64,512]{2,1,0:T(8,128)} %get-tuple-element.52), channel_id=1, source_target_pairs={{0,4},{2,6},{4,0},{6,2},{8,12},{10,14},{12,8},{14,10},{16,20},{18,... | collective-permute-start | bytes 786440 | tf_op jit(solution)/shard_map/ppermute | solution.py:130
  11.8 4.9 %convolution_bitcast_fusion.total_ref = f32[1024,512]{1,0:T(8,128)} fusion(f32[1024,512]{1,0:T(8,128)} %param.5, f32[1024,512]{1,0:T(8,128)S(1)} %copy-done, s32[]{:T(128)S(6)} %select_n.99), kind=kOutput, calls=%fused_computation | convolution fusion | flops 1610612736 | bytes 5242884 | tf_op jit(solution)/shard_map/dot_general | solution.py:14
  16.7 3.2 %convolution_bitcast_fusion.1.total_ref = f32[1024,512]{1,0:T(8,128)} fusion(f32[1024,512]{1,0:T(8,128)S(1)} %copy-done.7, f32[1024,512]{1,0:T(8,128)S(1)} %copy-done.11, s32[]{:T(128)S(6)} %select_n.99), kind=kOutput, calls=%fused_computation.1 | convolution fusion | flops 1610612736 | bytes 5242884 | tf_op jit(solution)/shard_map/dot_general | solution.py:14
  20.9 2.9 %slice.19 = f32[864,512]{1,0:T(8,128)} slice(f32[1024,512]{1,0:T(8,128)} %param.5), slice={[0:864], [0:512]} | slice | bytes 3538944 | tf_op jit(solution)/shard_map/slice | solution.py:157
  24.1 1.9 %fusion.5 = f32[2,64,512]{2,1,0:T(8,128)} fusion(f32[2,64,512]{2,1,0:T(8,128)} %collective-permute-done.4, f32[2,64,512]{2,1,0:T(8,128)} %collective-permute-done.3, f32[2,64,512]{2,1,0:T(8,128)S(1)} %collective-permute-done.2, f32[2,4,64,512]{3,2,1,0:T(8,128)} %bitcast.61, s32[]{:T(128)S(6)} %select_n.95), kind=kLoop, calls=%fused_computation.17 | loop fusion | flops 196608 | bytes 1310724 | tf_op jit(solution)/shard_map/add | solution.py:130
  26.7 1.3 %constant_dynamic-slice_fusion.1.x_ref = f32[512,512]{1,0:T(8,128)S(1)} fusion(f32[1024,512]{1,0:T(8,128)} %param.8, s32[]{:T(128)S(6)} %select_n.93), kind=kLoop, calls=%fused_computation.43 | loop fusion | bytes 2097156 | tf_op jit(solution)/shard_map/dynamic_slice | solution.py:146
  30.0 20.5 %collective-permute-done.x_ref = f32[1024,512]{1,0:T(8,128)} collective-permute-done((f32[1024,512]{1,0:T(8,128)}, f32[1024,512]{1,0:T(8,128)}, u32[]{:S(2)}, u32[]{:S(2)}) %collective-permute-start) | collective-permute-done | bytes 2097184 | tf_op jit(solution)/shard_map/ppermute | solution.py:180
  50.5 3.5 %fusion.22 = f32[512,512]{1,0:T(8,128)S(1)} fusion(f32[1024,512]{1,0:T(8,128)} %collective-permute-done.x_ref, f32[1024,512]{1,0:T(8,128)S(1)} %copy-done.6), kind=kOutput, calls=%fused_computation.45 | convolution fusion | flops 1610612736 | bytes 5242880 | tf_op jit(solution)/shard_map/dot_general | solution.py:41
  55.0 3.0 %collective-permute-start.6 = (f32[2,64,512]{2,1,0:T(8,128)}, f32[2,64,512]{2,1,0:T(8,128)}, u32[]{:S(2)}, u32[]{:S(2)}) collective-permute-start(f32[2,64,512]{2,1,0:T(8,128)} %get-tuple-element.47), channel_id=1, source_target_pairs={{0,2},{2,0},{4,6},{6,4},{8,10},{10,8},{12,14},{14,12},{16,18},{18,... | collective-permute-start | bytes 786440 | tf_op jit(solution)/shard_map/ppermute | solution.py:130
  58.0 1.4 %collective-permute-start.7 = (f32[2,64,512]{2,1,0:T(8,128)}, f32[2,64,512]{2,1,0:T(8,128)}, u32[]{:S(2)}, u32[]{:S(2)}) collective-permute-start(f32[2,64,512]{2,1,0:T(8,128)} %get-tuple-element.49), channel_id=1, source_target_pairs={{0,4},{2,6},{4,0},{6,2},{8,12},{10,14},{12,8},{14,10},{16,20},{18,... | collective-permute-start | bytes 786440 | tf_op jit(solution)/shard_map/ppermute | solution.py:130
  60.1 1.5 %collective-permute-start.14 = (f32[128,512]{1,0:T(8,128)}, f32[128,512]{1,0:T(8,128)S(1)}, u32[]{:S(2)}, u32[]{:S(2)}) collective-permute-start(f32[128,512]{1,0:T(8,128)} %slice.23), channel_id=1, source_target_pairs={{0,1},{1,0},{2,3},{3,2},{4,5},{5,4},{6,7},{7,6},{8,9},{9,8},{10,11... | collective-permute-start | bytes 786440 | tf_op jit(solution)/shard_map/ppermute | solution.py:167
  62.1 5.4 %collective-permute-done.7 = f32[2,64,512]{2,1,0:T(8,128)} collective-permute-done((f32[2,64,512]{2,1,0:T(8,128)}, f32[2,64,512]{2,1,0:T(8,128)}, u32[]{:S(2)}, u32[]{:S(2)}) %collective-permute-start.7) | collective-permute-done | bytes 262176 | tf_op jit(solution)/shard_map/ppermute | solution.py:130
  67.4 3.7 %collective-permute-done.8 = f32[2,64,512]{2,1,0:T(8,128)} collective-permute-done((f32[2,64,512]{2,1,0:T(8,128)}, f32[2,64,512]{2,1,0:T(8,128)}, u32[]{:S(2)}, u32[]{:S(2)}) %collective-permute-start.8) | collective-permute-done | bytes 262176 | tf_op jit(solution)/shard_map/ppermute | solution.py:130
  71.1 1.3 %broadcast_select_fusion = (f32[2,64,512]{2,1,0:T(8,128)S(1)}, f32[2,64,512]{2,1,0:T(8,128)S(1)}) fusion(f32[2,64,512]{2,1,0:T(8,128)} %fusion.5, pred[]{:T(512)S(6)} %eq.13, f32[2,64,512]{2,1,0:T(8,128)} %collective-permute-done.8, f32[2,64,512]{2,1,0:T(8,128)} %collective-permute-done.7, f32[2,64,512]{2,1,0:T(8,128)} %collective-permute-done.6, ...), kind=kLoop, calls=%fused_computation.37 | loop fusion | flops 262144 | bytes 1835013 | tf_op jit(solution)/shard_map/jit(_where)/select_n | solution.py:197
  72.6 2.6 %collective-permute-start.10 = (f32[64,512]{1,0:T(8,128)S(1)}, f32[64,512]{1,0:T(8,128)S(1)}, u32[]{:S(2)}, u32[]{:S(2)}) collective-permute-start(f32[64,512]{1,0:T(8,128)S(1)} %get-tuple-element.54), channel_id=1, source_target_pairs={{0,16},{2,18},{4,20},{6,22},{8,24},{10,26},{12,28},{14,30},{16,0},... | collective-permute-start | bytes 393224 | tf_op jit(solution)/shard_map/ppermute | solution.py:130
  75.2 1.3 %collective-permute-start.11 = (f32[64,512]{1,0:T(8,128)S(1)}, f32[64,512]{1,0:T(8,128)S(1)}, u32[]{:S(2)}, u32[]{:S(2)}) collective-permute-start(f32[64,512]{1,0:T(8,128)S(1)} %get-tuple-element.55), channel_id=1, source_target_pairs={{0,24},{2,26},{4,28},{6,30},{8,16},{10,18},{12,20},{14,22},{16,8},... | collective-permute-start | bytes 393224 | tf_op jit(solution)/shard_map/ppermute | solution.py:130
  76.8 1.9 %shard_map.79.total_ref = f32[1024,512]{1,0:T(8,128)} custom-call(f32[1024,512]{1,0:T(8,128)} %convolution_bitcast_fusion.total_ref, f32[32,512]{1,0:T(8,128)S(1)} %slice_select_fusion.x_ref, bf16[512,512]{1,0:T(8,128)(2,1)S(1)} %get-tuple-element.38.high_ref.refs_1_, ...), custom_call_target="tpu_custom_call", output_to_operand_aliasing={{}: (0, {})} | custom-call | tf_op jit(solution)/shard_map/pallas_call | solution.py:61
  79.7 4.5 %shard_map.78 = f32[1024,512]{1,0:T(8,128)} custom-call(f32[1024,512]{1,0:T(8,128)} %convolution_bitcast_fusion.1.total_ref, f32[1024,512]{1,0:T(8,128)} %collective-permute-done.x_ref, bf16[512,512]{1,0:T(8,128)(2,1)S(1)} %copy-done.3, bf16[512,512]{1,0:T(8,128)(2,1)S(1)} %copy-done.5, f32[1,512]{1,0:T(1,128)S(1)} %bitcast.55), custom_call_target="tpu_custom_call", output_to_operand_aliasing={{}: (0, {})} | custom-call | tf_op jit(solution)/shard_map/pallas_call | solution.py:61
  84.2 1.3 %collective-permute-done.10 = f32[64,512]{1,0:T(8,128)S(1)} collective-permute-done((f32[64,512]{1,0:T(8,128)S(1)}, f32[64,512]{1,0:T(8,128)S(1)}, u32[]{:S(2)}, u32[]{:S(2)}) %collective-permute-start.10) | collective-permute-done | bytes 131104 | tf_op jit(solution)/shard_map/ppermute | solution.py:130
  85.6 1.5 %collective-permute-done.9 = f32[64,512]{1,0:T(8,128)S(1)} collective-permute-done((f32[64,512]{1,0:T(8,128)S(1)}, f32[64,512]{1,0:T(8,128)S(1)}, u32[]{:S(2)}, u32[]{:S(2)}) %collective-permute-start.9) | collective-permute-done | bytes 131104 | tf_op jit(solution)/shard_map/ppermute | solution.py:130
  88.4 4.1 %shard_map.80.total_ref = f32[1024,512]{1,0:T(8,128)} custom-call(f32[1024,512]{1,0:T(8,128)} %shard_map.79.total_ref, f32[864,512]{1,0:T(8,128)} %collective-permute-done.13.x_ref, bf16[512,512]{1,0:T(8,128)(2,1)S(1)} %get-tuple-element.38.high_ref.refs_1_, bf16[512,512]{1,0:T(8,128)(2,1)S(1)} %get-tuple-element.39.low_ref.refs_2_, ...), custom_call_target="tpu_custom_call", output_to_operand_aliasing={{}: (0, {})} | custom-call | tf_op jit(solution)/shard_map/pallas_call | solution.py:61
  92.5 1.4 %collective-permute-done.14.refs_0_ = f32[128,512]{1,0:T(8,128)S(1)} collective-permute-done((f32[128,512]{1,0:T(8,128)}, f32[128,512]{1,0:T(8,128)S(1)}, u32[]{:S(2)}, u32[]{:S(2)}) %collective-permute-start.14) | collective-permute-done | bytes 262176 | tf_op jit(solution)/shard_map/ppermute | solution.py:167
  (59 shorter events, 12.4 us)
Async XLA Ops:
  0.6 11.2 %copy-start = (f32[1024,512]{1,0:T(8,128)S(1)}, f32[1024,512]{1,0:T(8,128)}, u32[]{:S(2)}) copy-start(f32[1024,512]{1,0:T(8,128)} %param.7) | copy-start | bytes 6291460
  0.6 49.8 %collective-permute-start = (f32[1024,512]{1,0:T(8,128)}, f32[1024,512]{1,0:T(8,128)}, u32[]{:S(2)}, u32[]{:S(2)}) collective-permute-start(f32[1024,512]{1,0:T(8,128)} %param.6), channel_id=1, source_target_pairs={{0,1},{1,0},{2,3},{3,2},{4,5},{5,4},{6,7},{7,6},{8,9},{9,8},{10,11... | collective-permute-start | bytes 6291464 | tf_op jit(solution)/shard_map/ppermute | solution.py:180
  7.7 8.9 %copy-start.9 = (f32[512,512]{1,0:T(8,128)}, f32[512,512]{1,0:T(8,128)S(1)}, u32[]{:S(2)}) copy-start(f32[512,512]{1,0:T(8,128)S(1)} %fusion.21) | copy-start | bytes 3145732
  8.8 15.3 %collective-permute-start.2 = (f32[2,64,512]{2,1,0:T(8,128)}, f32[2,64,512]{2,1,0:T(8,128)S(1)}, u32[]{:S(2)}, u32[]{:S(2)}) collective-permute-start(f32[2,64,512]{2,1,0:T(8,128)} %get-tuple-element.50), channel_id=1, source_target_pairs={{0,2},{2,0},{4,6},{6,4},{8,10},{10,8},{12,14},{14,12},{16,18},{18,... | collective-permute-start | bytes 786440 | tf_op jit(solution)/shard_map/ppermute | solution.py:130
  8.8 15.3 %collective-permute-start.3 = (f32[2,64,512]{2,1,0:T(8,128)}, f32[2,64,512]{2,1,0:T(8,128)}, u32[]{:S(2)}, u32[]{:S(2)}) collective-permute-start(f32[2,64,512]{2,1,0:T(8,128)} %get-tuple-element.52), channel_id=1, source_target_pairs={{0,4},{2,6},{4,0},{6,2},{8,12},{10,14},{12,8},{14,10},{16,20},{18,... | collective-permute-start | bytes 786440 | tf_op jit(solution)/shard_map/ppermute | solution.py:130
  10.3 13.8 %collective-permute-start.4 = (f32[2,64,512]{2,1,0:T(8,128)}, f32[2,64,512]{2,1,0:T(8,128)}, u32[]{:S(2)}, u32[]{:S(2)}) collective-permute-start(f32[2,64,512]{2,1,0:T(8,128)} %get-tuple-element.51), channel_id=1, source_target_pairs={{0,6},{2,4},{4,2},{6,0},{8,14},{10,12},{12,10},{14,8},{16,22},{18,... | collective-permute-start | bytes 786440 | tf_op jit(solution)/shard_map/ppermute | solution.py:130
  11.5 12.5 %collective-permute-start.1 = (f32[32,512]{1,0:T(8,128)S(1)}, f32[32,512]{1,0:T(8,128)S(1)}, u32[]{:S(2)}, u32[]{:S(2)}) collective-permute-start(f32[32,512]{1,0:T(8,128)S(1)} %slice.18), channel_id=1, source_target_pairs={{0,2},{2,0},{4,6},{6,4},{8,10},{10,8},{12,14},{14,12},{16,18},{18,... | collective-permute-start | bytes 196616 | tf_op jit(solution)/shard_map/ppermute | solution.py:109
  11.8 4.9 %copy-start.7 = (f32[1024,512]{1,0:T(8,128)S(1)}, f32[1024,512]{1,0:T(8,128)}, u32[]{:S(2)}) copy-start(f32[1024,512]{1,0:T(8,128)} %param.6) | copy-start | bytes 6291460
  11.8 4.9 %copy-start.11 = (f32[1024,512]{1,0:T(8,128)S(1)}, f32[1024,512]{1,0:T(8,128)}, u32[]{:S(2)}) copy-start(f32[1024,512]{1,0:T(8,128)} %param.8) | copy-start | bytes 6291460
  26.0 2.2 %collective-permute-start.5 = (f32[64,512]{1,0:T(8,128)S(1)}, f32[64,512]{1,0:T(8,128)S(1)}, u32[]{:S(2)}, u32[]{:S(2)}) collective-permute-start(f32[64,512]{1,0:T(8,128)S(1)} %pad_maximum_fusion), channel_id=1, source_target_pairs={{2,3},{3,2},{6,7},{7,6},{10,11},{11,10},{14,15},{15,14},{18,19},{1... | collective-permute-start | bytes 393224 | tf_op jit(solution)/shard_map/ppermute | solution.py:120
  28.0 22.5 %copy-start.6 = (f32[1024,512]{1,0:T(8,128)S(1)}, f32[1024,512]{1,0:T(8,128)}, u32[]{:S(2)}) copy-start(f32[1024,512]{1,0:T(8,128)} %param.5) | copy-start | bytes 6291460
  28.0 60.4 %collective-permute-start.13 = (f32[864,512]{1,0:T(8,128)}, f32[864,512]{1,0:T(8,128)}, u32[]{:S(2)}, u32[]{:S(2)}) collective-permute-start(f32[864,512]{1,0:T(8,128)} %slice.19), channel_id=1, source_target_pairs={{0,1},{1,0},{2,3},{3,2},{4,5},{5,4},{6,7},{7,6},{8,9},{9,8},{10,11... | collective-permute-start | bytes 5308424 | tf_op jit(solution)/shard_map/ppermute | solution.py:167
  54.0 6.1 %copy-start.8 = (f32[512,512]{1,0:T(8,128)}, f32[512,512]{1,0:T(8,128)S(1)}, u32[]{:S(2)}) copy-start(f32[512,512]{1,0:T(8,128)S(1)} %fusion.22) | copy-start | bytes 3145732
  54.0 7.6 %copy-start.12 = (f32[512]{0:T(512)S(1)}, f32[512]{0:T(512)}, u32[]{:S(2)}) copy-start(f32[512]{0:T(512)} %param.9) | copy-start | bytes 6148
  55.0 6.7 %collective-permute-start.6 = (f32[2,64,512]{2,1,0:T(8,128)}, f32[2,64,512]{2,1,0:T(8,128)}, u32[]{:S(2)}, u32[]{:S(2)}) collective-permute-start(f32[2,64,512]{2,1,0:T(8,128)} %get-tuple-element.47), channel_id=1, source_target_pairs={{0,2},{2,0},{4,6},{6,4},{8,10},{10,8},{12,14},{14,12},{16,18},{18,... | collective-permute-start | bytes 786440 | tf_op jit(solution)/shard_map/ppermute | solution.py:130
  58.0 9.5 %collective-permute-start.7 = (f32[2,64,512]{2,1,0:T(8,128)}, f32[2,64,512]{2,1,0:T(8,128)}, u32[]{:S(2)}, u32[]{:S(2)}) collective-permute-start(f32[2,64,512]{2,1,0:T(8,128)} %get-tuple-element.49), channel_id=1, source_target_pairs={{0,4},{2,6},{4,0},{6,2},{8,12},{10,14},{12,8},{14,10},{16,20},{18,... | collective-permute-start | bytes 786440 | tf_op jit(solution)/shard_map/ppermute | solution.py:130
  59.4 11.8 %collective-permute-start.8 = (f32[2,64,512]{2,1,0:T(8,128)}, f32[2,64,512]{2,1,0:T(8,128)}, u32[]{:S(2)}, u32[]{:S(2)}) collective-permute-start(f32[2,64,512]{2,1,0:T(8,128)} %get-tuple-element.48), channel_id=1, source_target_pairs={{0,6},{2,4},{4,2},{6,0},{8,14},{10,12},{12,10},{14,8},{16,22},{18,... | collective-permute-start | bytes 786440 | tf_op jit(solution)/shard_map/ppermute | solution.py:130
  60.1 33.8 %collective-permute-start.14 = (f32[128,512]{1,0:T(8,128)}, f32[128,512]{1,0:T(8,128)S(1)}, u32[]{:S(2)}, u32[]{:S(2)}) collective-permute-start(f32[128,512]{1,0:T(8,128)} %slice.23), channel_id=1, source_target_pairs={{0,1},{1,0},{2,3},{3,2},{4,5},{5,4},{6,7},{7,6},{8,9},{9,8},{10,11... | collective-permute-start | bytes 786440 | tf_op jit(solution)/shard_map/ppermute | solution.py:167
  61.6 10.8 %copy-start.10 = (f32[2,64,512]{2,1,0:T(8,128)S(1)}, f32[2,64,512]{2,1,0:T(8,128)}, u32[]{:S(2)}) copy-start(f32[2,64,512]{2,1,0:T(8,128)} %fusion.5) | copy-start | bytes 786436
  61.7 14.9 %collective-permute-start.12 = (f32[32,512]{1,0:T(8,128)S(1)}, f32[32,512]{1,0:T(8,128)S(1)}, u32[]{:S(2)}, u32[]{:S(2)}) collective-permute-start(f32[32,512]{1,0:T(8,128)S(1)} %slice.21), channel_id=1, source_target_pairs={{0,2},{2,0},{4,6},{6,4},{8,10},{10,8},{12,14},{14,12},{16,18},{18,... | collective-permute-start | bytes 196616 | tf_op jit(solution)/shard_map/ppermute | solution.py:109
  72.6 12.9 %collective-permute-start.10 = (f32[64,512]{1,0:T(8,128)S(1)}, f32[64,512]{1,0:T(8,128)S(1)}, u32[]{:S(2)}, u32[]{:S(2)}) collective-permute-start(f32[64,512]{1,0:T(8,128)S(1)} %get-tuple-element.54), channel_id=1, source_target_pairs={{0,16},{2,18},{4,20},{6,22},{8,24},{10,26},{12,28},{14,30},{16,0},... | collective-permute-start | bytes 393224 | tf_op jit(solution)/shard_map/ppermute | solution.py:130
  75.2 10.4 %collective-permute-start.11 = (f32[64,512]{1,0:T(8,128)S(1)}, f32[64,512]{1,0:T(8,128)S(1)}, u32[]{:S(2)}, u32[]{:S(2)}) collective-permute-start(f32[64,512]{1,0:T(8,128)S(1)} %get-tuple-element.55), channel_id=1, source_target_pairs={{0,24},{2,26},{4,28},{6,30},{8,16},{10,18},{12,20},{14,22},{16,8},... | collective-permute-start | bytes 393224 | tf_op jit(solution)/shard_map/ppermute | solution.py:130
  76.5 10.6 %collective-permute-start.9 = (f32[64,512]{1,0:T(8,128)S(1)}, f32[64,512]{1,0:T(8,128)S(1)}, u32[]{:S(2)}, u32[]{:S(2)}) collective-permute-start(f32[64,512]{1,0:T(8,128)S(1)} %get-tuple-element.53), channel_id=1, source_target_pairs={{0,8},{2,10},{4,12},{6,14},{8,0},{10,2},{12,4},{14,6},{16,24},{18,... | collective-permute-start | bytes 393224 | tf_op jit(solution)/shard_map/ppermute | solution.py:130
  76.8 2.9 %copy-start.3 = (bf16[512,512]{1,0:T(8,128)(2,1)S(1)}, bf16[512,512]{1,0:T(8,128)(2,1)}, u32[]{:S(2)}) copy-start(bf16[512,512]{1,0:T(8,128)(2,1)} %copy-done.2) | copy-start | bytes 1572868
  (4 other events, 7.4 us)

commit v5 on v4

--- a/solution.py
+++ b/solution.py
@@ -1,4 +1,5 @@
 import functools
+import math
 
 import jax
 import jax.numpy as jnp
@@ -76,33 +77,31 @@
     )(total, x, *matrix, weights[None])
 
 
-def end_rows_kernel(total_ref, own_ref, *refs):
-    *x_refs, high_ref, low_ref, weights_ref, out_ref, held, sem = refs
+def end_rows_kernel(first, total_ref, own_ref, x_ref, high_ref, low_ref, weights_ref, out_ref, held, sem):
     dot = functools.partial(jnp.dot, preferred_element_type=jnp.float32)
     rows = held.shape[0]
-    x_high, x_low = split(jnp.concatenate([x_ref[...] for x_ref in x_refs]))
-    total = own_ref[...] + (
-        dot(x_high, high_ref[...]) + (dot(x_high, low_ref[...]) + dot(x_low, high_ref[...]))
-    )
+    x_high, x_low = split(x_ref[...])
+    by_high = dot(jnp.concatenate([x_high, x_low]), high_ref[...])
+    total = own_ref[...] + (by_high[:rows] + (dot(x_high, low_ref[...]) + by_high[rows:]))
     held[...] = total * weights_ref[...]
-    store = pltpu.make_async_copy(held, out_ref.at[pl.ds(out_ref.shape[0] - rows, rows)], sem)
+    store = pltpu.make_async_copy(held, out_ref.at[pl.ds(first, rows)], sem)
     store.start()
     store.wait()
 
 
-def end_rows(total, own, xs, matrix, weights):
+def end_rows(total, own, x, matrix, weights, first):
     vmem = pl.BlockSpec(memory_space=pltpu.VMEM)
     apart = pl.BlockSpec(memory_space=pl.ANY)
     return pl.pallas_call(
-        end_rows_kernel,
-        in_specs=[apart] + [vmem] * (4 + len(xs)),
+        functools.partial(end_rows_kernel, first),
+        in_specs=[apart] + [vmem] * 5,
         out_specs=apart,
         out_shape=jax.ShapeDtypeStruct(total.shape, total.dtype),
         scratch_shapes=[pltpu.VMEM(own.shape, jnp.float32), pltpu.SemaphoreType.DMA],
         input_output_aliases={0: 0},
         cost_estimate=FREE,
         compiler_params=pltpu.CompilerParams(vmem_limit_bytes=LIMIT),
-    )(total, own, *xs, *matrix, weights[None])
+    )(total, own, x, *matrix, weights[None])
 
 
 def swap(x):
@@ -120,15 +119,18 @@
     return lax.ppermute(x, ("rows", "snap"), pairs)
 
 
-def exchange(parts, axis, stride):
+def exchange(parts, axis, stride, beside=None):
     count = lax.axis_size("rows")
     digits = parts.shape[axis]
     mine = (lax.axis_index("rows") // stride) % digits
-    total = lax.dynamic_index_in_dim(parts, mine, axis, keepdims=False)
+    arrived = []
     for flip in range(1, digits):
         give = lax.dynamic_index_in_dim(parts, mine ^ flip, axis, keepdims=False)
-        total += lax.ppermute(give, "rows", [(i, i ^ (flip * stride)) for i in range(count)])
-    return total
+        pairs = [(i, i ^ (flip * stride)) for i in range(count)]
+        arrived.append(lax.ppermute(give, "rows", pairs))
+    if beside is not None:
+        arrived, beside = lax.optimization_barrier((arrived, beside))
+    return sum(arrived, lax.dynamic_index_in_dim(parts, mine, axis, keepdims=False)), beside
 
 
 def shards(primal, adjoint, right_vectors, left_vectors, singular):
@@ -150,8 +152,8 @@
 
     near = min(group, 1 << (count.bit_length() - 1) // 2)
 
-    def within(term):
-        return exchange(term.reshape(group // near, near, share, width), 1, 1)
+    def within(term, beside=None):
+        return exchange(term.reshape(group // near, near, share, width), 1, 1, beside)
 
     adjoints = [adjoint]
     primals = [[primal[a:b] for a, b in spans]]
@@ -159,12 +161,12 @@
         primals.append([lax.ppermute(piece, "snap", ring) for piece in primals[-1]])
     most, few, end = primals[-1]
     odd = lax.axis_index("rows") % 2 == 1
-    terms = [within(inner_cols(adjoint, primal))]
+    terms = [within(inner_cols(adjoint, primal))[0]]
     both, most, terms = lax.optimization_barrier(
         (jnp.concatenate([few, swap(few)]), most, terms)
     )
     extra = pass_on(both, 1)
-    most, end = lax.ppermute(most, "snap", ring), lax.ppermute(end, "snap", ring)
+    most, end = [lax.ppermute(piece, "snap", ring) for piece in (most, end)]
     psi = mul(adjoint, block(left_vectors, side))
     phi = mul(primal, block(right_vectors, side))
     rights = []
@@ -181,13 +183,15 @@
         theirs, left, rights, terms, psi, phi = lax.optimization_barrier(
             (adjoints[step], left, rights, terms, psi, phi)
         )
-        terms.append(within(inner_cols(theirs, primal)))
         psi = add_rows(psi, theirs, left, weights, 0, rows // 2, step == sides - 1)
+        term, psi = within(inner_cols(theirs, primal), psi)
+        terms.append(term)
     back = swap(extra[few.shape[0] :])
     few = jnp.where(odd, extra[: few.shape[0]], back)
     for step in range(1, sides - 1):
         for (start, stop), piece in zip(spans, primals[step]):
-            phi = add_rows(phi, piece, rights[step - 1], weights, start, stop - start, False)
+            tile = math.gcd(start, stop - start)
+            phi = add_rows(phi, piece, rights[step - 1], weights, start, tile, False)
     phi = add_rows(phi, few, rights[-1], weights, cuts[1], len(few), True)
     own = phi[cuts[2] :]
     blocks = [terms[-t % sides] for t in range(sides)]
@@ -196,11 +200,11 @@
         turn = (side // bit) % 2 == 1
         blocks = [jnp.where(turn, blocks[t - bit], blocks[t]) for t in range(sides)]
         bit *= 2
-    total = exchange(jnp.concatenate(blocks), 0, near)
+    total, (phi, own) = exchange(jnp.concatenate(blocks), 0, near, (phi, own))
     gram = total * norm
     gram, psi, phi, own = lax.optimization_barrier((gram, psi, phi, own))
     phi = add_rows(phi, most, rights[-1], weights, 0, cuts[1] // 2, True)
-    phi = end_rows(phi, own, [end], rights[-1], weights)
+    phi = end_rows(phi, own, end, rights[-1], weights, cuts[2])
     return (gram, phi, psi)
 
 

time: 95.4 us -> 95.5 us (level)
  local copies, waits for them, and re-layouts: 11.5 us -> 13.5 us
  waiting for transfers between devices: 34.4 us -> 32.5 us
    unnamed x26, local copies, waits for them, and re-layouts: 1.63 us -> 3.7 us
    ppermute x11, waiting for transfers between devices: 13.9 us -> 12 us  [the longest x9 9.99 us: exchange(): arrived.append(lax.ppermute(give, 'rows', pairs))]
  transfers between devices with their start and end apart: 15 -> 15, of which waited for: 7 -> 6; matrix products, arithmetic and copies ran while one was open for 31% -> 31% of each run, Pallas kernels for 11% -> 11%
where the time goes in v5:
time: 95.5 us; the launch traced here: 95 us
  waiting for transfers between devices  32.5 us (34%)
  starting transfers between devices  16.5 us (17%)
  matrix products  15.6 us (16%)
  local copies, waits for them, and re-layouts  13.5 us (14%)
  Pallas kernels  11.9 us (12%)
  other arithmetic  4.11 us (4%)
    ppermute x1, waiting for transfers between devices, shards(): adjoints.append(lax.ppermute(adjoints[-1], 'snap', ring))  20.5 us
    pallas_call x3, Pallas kernels, add_rows(): pl.pallas_call(functools.partial(add_rows_kernel, last), grid=(x.shape[0]...  10.5 us
    ppermute x9, starting transfers between devices, exchange(): arrived.append(lax.ppermute(give, 'rows', pairs))  10.4 us
    ppermute x9, waiting for transfers between devices, exchange(): arrived.append(lax.ppermute(give, 'rows', pairs))  9.99 us
    dot_general x2, matrix products, mul(): jnp.dot(left, right, precision=HIGH, preferred_element_type=jnp.float32)  8.06 us
    dot_general x2, matrix products, inner_cols(): lax.dot_general(left, right, (((0,), (0,)), ((), ())), precision=HIGH, pr...  7.55 us
    slice x3, local copies, waits for them, and re-layouts, shards(): primals = [[primal[a:b] for a, b in spans]]  4.51 us
    unnamed x26, local copies, waits for them, and re-layouts  3.7 us
  transfers between devices with their start and end apart: 15, of which 6 were waited for; matrix products, arithmetic and copies ran while one was open for 31% of the time, Pallas kernels for 11%

profile of v5, /device:TPU:0, one launch (start us, length us, event | category | flops | bytes accessed | tf_op | source)
XLA Modules:
  0.0 95.0 jit_solution(13015877200184258768)
XLA Ops:
  0.6 3.0 %collective-permute-start = (f32[1024,512]{1,0:T(8,128)}, f32[1024,512]{1,0:T(8,128)}, u32[]{:S(2)}, u32[]{:S(2)}) collective-permute-start(f32[1024,512]{1,0:T(8,128)} %param.6), channel_id=1, source_target_pairs={{0,1},{1,0},{2,3},{3,2},{4,5},{5,4},{6,7},{7,6},{8,9},{9,8},{10,11... | collective-permute-start | bytes 6291464 | tf_op jit(solution)/shard_map/ppermute | solution.py:182
  3.7 4.0 %fusion.21 = f32[512,512]{1,0:T(8,128)S(1)} fusion(f32[1024,512]{1,0:T(8,128)} %param.6, f32[1024,512]{1,0:T(8,128)} %param.5), kind=kOutput, calls=%fused_computation.44 | convolution fusion | flops 1610612736 | bytes 5242880 | tf_op jit(solution)/shard_map/dot_general | solution.py:42
  8.8 1.5 %collective-permute-start.3 = (f32[2,64,512]{2,1,0:T(8,128)}, f32[2,64,512]{2,1,0:T(8,128)}, u32[]{:S(2)}, u32[]{:S(2)}) collective-permute-start(f32[2,64,512]{2,1,0:T(8,128)} %get-tuple-element.70), channel_id=1, source_target_pairs={{0,4},{2,6},{4,0},{6,2},{8,12},{10,14},{12,8},{14,10},{16,20},{18,... | collective-permute-start | bytes 786440 | tf_op jit(solution)/shard_map/ppermute | solution.py:130
  11.8 4.9 %convolution_bitcast_fusion.total_ref = f32[1024,512]{1,0:T(8,128)} fusion(f32[1024,512]{1,0:T(8,128)} %param.5, f32[1024,512]{1,0:T(8,128)S(1)} %copy-done, s32[]{:T(128)S(6)} %select_n.99), kind=kOutput, calls=%fused_computation | convolution fusion | flops 1610612736 | bytes 5242884 | tf_op jit(solution)/shard_map/dot_general | solution.py:15
  16.7 3.2 %convolution_bitcast_fusion.1.total_ref = f32[1024,512]{1,0:T(8,128)} fusion(f32[1024,512]{1,0:T(8,128)S(1)} %copy-done.7, f32[1024,512]{1,0:T(8,128)S(1)} %copy-done.11, s32[]{:T(128)S(6)} %select_n.99), kind=kOutput, calls=%fused_computation.1 | convolution fusion | flops 1610612736 | bytes 5242884 | tf_op jit(solution)/shard_map/dot_general | solution.py:15
  20.9 2.9 %slice.19 = f32[864,512]{1,0:T(8,128)} slice(f32[1024,512]{1,0:T(8,128)} %param.5), slice={[0:864], [0:512]} | slice | bytes 3538944 | tf_op jit(solution)/shard_map/slice | solution.py:159
  24.1 1.9 %fusion.5 = f32[2,64,512]{2,1,0:T(8,128)} fusion(f32[2,64,512]{2,1,0:T(8,128)} %collective-permute-done.4, f32[2,64,512]{2,1,0:T(8,128)} %collective-permute-done.3, f32[2,64,512]{2,1,0:T(8,128)S(1)} %collective-permute-done.2, f32[2,4,64,512]{3,2,1,0:T(8,128)} %bitcast.61, s32[]{:T(128)S(6)} %select_n.95), kind=kLoop, calls=%fused_computation.17 | loop fusion | flops 196608 | bytes 1310724 | tf_op jit(solution)/shard_map/add | solution.py:133
  26.7 1.3 %constant_dynamic-slice_fusion.1.x_ref = f32[512,512]{1,0:T(8,128)S(1)} fusion(f32[1024,512]{1,0:T(8,128)} %param.8, s32[]{:T(128)S(6)} %select_n.93), kind=kLoop, calls=%fused_computation.43 | loop fusion | bytes 2097156 | tf_op jit(solution)/shard_map/dynamic_slice | solution.py:148
  30.0 20.5 %collective-permute-done.x_ref = f32[1024,512]{1,0:T(8,128)} collective-permute-done((f32[1024,512]{1,0:T(8,128)}, f32[1024,512]{1,0:T(8,128)}, u32[]{:S(2)}, u32[]{:S(2)}) %collective-permute-start) | collective-permute-done | bytes 2097184 | tf_op jit(solution)/shard_map/ppermute | solution.py:182
  50.5 3.5 %fusion.22 = f32[512,512]{1,0:T(8,128)S(1)} fusion(f32[1024,512]{1,0:T(8,128)} %collective-permute-done.x_ref, f32[1024,512]{1,0:T(8,128)S(1)} %copy-done.6), kind=kOutput, calls=%fused_computation.45 | convolution fusion | flops 1610612736 | bytes 5242880 | tf_op jit(solution)/shard_map/dot_general | solution.py:42
  55.0 3.0 %collective-permute-start.6 = (f32[2,64,512]{2,1,0:T(8,128)}, f32[2,64,512]{2,1,0:T(8,128)}, u32[]{:S(2)}, u32[]{:S(2)}) collective-permute-start(f32[2,64,512]{2,1,0:T(8,128)} %get-tuple-element.67), channel_id=1, source_target_pairs={{0,2},{2,0},{4,6},{6,4},{8,10},{10,8},{12,14},{14,12},{16,18},{18,... | collective-permute-start | bytes 786440 | tf_op jit(solution)/shard_map/ppermute | solution.py:130
  58.0 1.4 %collective-permute-start.7 = (f32[2,64,512]{2,1,0:T(8,128)}, f32[2,64,512]{2,1,0:T(8,128)}, u32[]{:S(2)}, u32[]{:S(2)}) collective-permute-start(f32[2,64,512]{2,1,0:T(8,128)} %get-tuple-element.66), channel_id=1, source_target_pairs={{0,4},{2,6},{4,0},{6,2},{8,12},{10,14},{12,8},{14,10},{16,20},{18,... | collective-permute-start | bytes 786440 | tf_op jit(solution)/shard_map/ppermute | solution.py:130
  60.1 1.5 %collective-permute-start.14 = (f32[128,512]{1,0:T(8,128)}, f32[128,512]{1,0:T(8,128)S(1)}, u32[]{:S(2)}, u32[]{:S(2)}) collective-permute-start(f32[128,512]{1,0:T(8,128)} %slice.23), channel_id=1, source_target_pairs={{0,1},{1,0},{2,3},{3,2},{4,5},{5,4},{6,7},{7,6},{8,9},{9,8},{10,11... | collective-permute-start | bytes 786440 | tf_op jit(solution)/shard_map/ppermute | solution.py:169
  63.7 4.5 %shard_map.78 = f32[1024,512]{1,0:T(8,128)} custom-call(f32[1024,512]{1,0:T(8,128)} %convolution_bitcast_fusion.1.total_ref, f32[1024,512]{1,0:T(8,128)} %collective-permute-done.x_ref, bf16[512,512]{1,0:T(8,128)(2,1)S(1)} %copy-done.3, bf16[512,512]{1,0:T(8,128)(2,1)S(1)} %copy-done.5, f32[1,512]{1,0:T(1,128)S(1)} %bitcast.54), custom_call_target="tpu_custom_call", output_to_operand_aliasing={{}: (0, {})} | custom-call | tf_op jit(solution)/shard_map/pallas_call | solution.py:62
  68.6 2.5 %collective-permute-done.8 = f32[2,64,512]{2,1,0:T(8,128)} collective-permute-done((f32[2,64,512]{2,1,0:T(8,128)}, f32[2,64,512]{2,1,0:T(8,128)}, u32[]{:S(2)}, u32[]{:S(2)}) %collective-permute-start.8) | collective-permute-done | bytes 262176 | tf_op jit(solution)/shard_map/ppermute | solution.py:130
  71.1 1.3 %broadcast_select_fusion = (f32[2,64,512]{2,1,0:T(8,128)S(1)}, f32[2,64,512]{2,1,0:T(8,128)S(1)}) fusion(f32[2,64,512]{2,1,0:T(8,128)S(1)} %copy-done.10, pred[]{:T(512)S(6)} %eq.13, f32[2,64,512]{2,1,0:T(8,128)} %collective-permute-done.8, f32[2,64,512]{2,1,0:T(8,128)} %collective-permute-done.7, f32[2,64,512]{2,1,0:T(8,128)} %collective-permute-done.6, ...), kind=kLoop, calls=%fused_computation.37 | loop fusion | flops 262144 | bytes 1835013 | tf_op jit(solution)/shard_map/jit(_where)/select_n | solution.py:201
  72.6 2.6 %collective-permute-start.10 = (f32[64,512]{1,0:T(8,128)S(1)}, f32[64,512]{1,0:T(8,128)S(1)}, u32[]{:S(2)}, u32[]{:S(2)}) collective-permute-start(f32[64,512]{1,0:T(8,128)S(1)} %get-tuple-element.73), channel_id=1, source_target_pairs={{0,16},{2,18},{4,20},{6,22},{8,24},{10,26},{12,28},{14,30},{16,0},... | collective-permute-start | bytes 393224 | tf_op jit(solution)/shard_map/ppermute | solution.py:130
  75.2 1.3 %collective-permute-start.11 = (f32[64,512]{1,0:T(8,128)S(1)}, f32[64,512]{1,0:T(8,128)S(1)}, u32[]{:S(2)}, u32[]{:S(2)}) collective-permute-start(f32[64,512]{1,0:T(8,128)S(1)} %get-tuple-element.71), channel_id=1, source_target_pairs={{0,24},{2,26},{4,28},{6,30},{8,16},{10,18},{12,20},{14,22},{16,8},... | collective-permute-start | bytes 393224 | tf_op jit(solution)/shard_map/ppermute | solution.py:130
  76.8 1.9 %shard_map.79.total_ref = f32[1024,512]{1,0:T(8,128)} custom-call(f32[1024,512]{1,0:T(8,128)} %convolution_bitcast_fusion.total_ref, f32[32,512]{1,0:T(8,128)S(1)} %slice_select_fusion.x_ref, bf16[512,512]{1,0:T(8,128)(2,1)S(1)} %get-tuple-element.50.high_ref, bf16[512,512]{1,0:T(8,128)(2,1)S(1)} %get-tuple-element.51.low_ref, ...), custom_call_target="tpu_custom_call", output_to_operand_aliasing={{}: (0, {})} | custom-call | tf_op jit(solution)/shard_map/pallas_call | solution.py:62
  79.6 6.0 %collective-permute-done.10 = f32[64,512]{1,0:T(8,128)S(1)} collective-permute-done((f32[64,512]{1,0:T(8,128)S(1)}, f32[64,512]{1,0:T(8,128)S(1)}, u32[]{:S(2)}, u32[]{:S(2)}) %collective-permute-start.10) | collective-permute-done | bytes 131104 | tf_op jit(solution)/shard_map/ppermute | solution.py:130
  85.6 1.5 %collective-permute-done.9 = f32[64,512]{1,0:T(8,128)S(1)} collective-permute-done((f32[64,512]{1,0:T(8,128)S(1)}, f32[64,512]{1,0:T(8,128)S(1)}, u32[]{:S(2)}, u32[]{:S(2)}) %collective-permute-start.9) | collective-permute-done | bytes 131104 | tf_op jit(solution)/shard_map/ppermute | solution.py:130
  88.4 4.1 %shard_map.80.total_ref = f32[1024,512]{1,0:T(8,128)} custom-call(f32[1024,512]{1,0:T(8,128)} %shard_map.79.total_ref, f32[864,512]{1,0:T(8,128)} %collective-permute-done.13.x_ref, bf16[512,512]{1,0:T(8,128)(2,1)S(1)} %get-tuple-element.50.high_ref, bf16[512,512]{1,0:T(8,128)(2,1)S(1)} %get-tuple-element.51.low_ref, ...), custom_call_target="tpu_custom_call", output_to_operand_aliasing={{}: (0, {})} | custom-call | tf_op jit(solution)/shard_map/pallas_call | solution.py:62
  92.5 1.4 %collective-permute-done.14.x_ref = f32[128,512]{1,0:T(8,128)S(1)} collective-permute-done((f32[128,512]{1,0:T(8,128)}, f32[128,512]{1,0:T(8,128)S(1)}, u32[]{:S(2)}, u32[]{:S(2)}) %collective-permute-start.14) | collective-permute-done | bytes 262176 | tf_op jit(solution)/shard_map/ppermute | solution.py:169
  93.9 1.1 %shard_map.81 = f32[1024,512]{1,0:T(8,128)} custom-call(f32[1024,512]{1,0:T(8,128)} %shard_map.80.total_ref, f32[128,512]{1,0:T(8,128)S(1)} %slice.24.own_ref, f32[128,512]{1,0:T(8,128)S(1)} %collective-permute-done.14.x_ref, bf16[512,512]{1,0:T(8,128)(2,1)S(1)} %get-tuple-element.50.high_ref, ...), custom_call_target="tpu_custom_call", output_to_operand_aliasing={{}: (0, {})} | custom-call | tf_op jit(solution)/shard_map/pallas_call | solution.py:95
  (59 shorter events, 13.3 us)
Async XLA Ops:
  0.6 11.2 %copy-start = (f32[1024,512]{1,0:T(8,128)S(1)}, f32[1024,512]{1,0:T(8,128)}, u32[]{:S(2)}) copy-start(f32[1024,512]{1,0:T(8,128)} %param.7) | copy-start | bytes 6291460
  0.6 49.8 %collective-permute-start = (f32[1024,512]{1,0:T(8,128)}, f32[1024,512]{1,0:T(8,128)}, u32[]{:S(2)}, u32[]{:S(2)}) collective-permute-start(f32[1024,512]{1,0:T(8,128)} %param.6), channel_id=1, source_target_pairs={{0,1},{1,0},{2,3},{3,2},{4,5},{5,4},{6,7},{7,6},{8,9},{9,8},{10,11... | collective-permute-start | bytes 6291464 | tf_op jit(solution)/shard_map/ppermute | solution.py:182
  7.7 8.9 %copy-start.9 = (f32[512,512]{1,0:T(8,128)}, f32[512,512]{1,0:T(8,128)S(1)}, u32[]{:S(2)}) copy-start(f32[512,512]{1,0:T(8,128)S(1)} %fusion.21) | copy-start | bytes 3145732
  8.8 15.3 %collective-permute-start.2 = (f32[2,64,512]{2,1,0:T(8,128)}, f32[2,64,512]{2,1,0:T(8,128)S(1)}, u32[]{:S(2)}, u32[]{:S(2)}) collective-permute-start(f32[2,64,512]{2,1,0:T(8,128)} %get-tuple-element.68), channel_id=1, source_target_pairs={{0,2},{2,0},{4,6},{6,4},{8,10},{10,8},{12,14},{14,12},{16,18},{18,... | collective-permute-start | bytes 786440 | tf_op jit(solution)/shard_map/ppermute | solution.py:130
  8.8 15.3 %collective-permute-start.3 = (f32[2,64,512]{2,1,0:T(8,128)}, f32[2,64,512]{2,1,0:T(8,128)}, u32[]{:S(2)}, u32[]{:S(2)}) collective-permute-start(f32[2,64,512]{2,1,0:T(8,128)} %get-tuple-element.70), channel_id=1, source_target_pairs={{0,4},{2,6},{4,0},{6,2},{8,12},{10,14},{12,8},{14,10},{16,20},{18,... | collective-permute-start | bytes 786440 | tf_op jit(solution)/shard_map/ppermute | solution.py:130
  10.3 13.8 %collective-permute-start.4 = (f32[2,64,512]{2,1,0:T(8,128)}, f32[2,64,512]{2,1,0:T(8,128)}, u32[]{:S(2)}, u32[]{:S(2)}) collective-permute-start(f32[2,64,512]{2,1,0:T(8,128)} %get-tuple-element.69), channel_id=1, source_target_pairs={{0,6},{2,4},{4,2},{6,0},{8,14},{10,12},{12,10},{14,8},{16,22},{18,... | collective-permute-start | bytes 786440 | tf_op jit(solution)/shard_map/ppermute | solution.py:130
  11.5 12.5 %collective-permute-start.1 = (f32[32,512]{1,0:T(8,128)S(1)}, f32[32,512]{1,0:T(8,128)S(1)}, u32[]{:S(2)}, u32[]{:S(2)}) collective-permute-start(f32[32,512]{1,0:T(8,128)S(1)} %slice.18), channel_id=1, source_target_pairs={{0,2},{2,0},{4,6},{6,4},{8,10},{10,8},{12,14},{14,12},{16,18},{18,... | collective-permute-start | bytes 196616 | tf_op jit(solution)/shard_map/ppermute | solution.py:108
  11.8 4.9 %copy-start.7 = (f32[1024,512]{1,0:T(8,128)S(1)}, f32[1024,512]{1,0:T(8,128)}, u32[]{:S(2)}) copy-start(f32[1024,512]{1,0:T(8,128)} %param.6) | copy-start | bytes 6291460
  11.8 4.9 %copy-start.11 = (f32[1024,512]{1,0:T(8,128)S(1)}, f32[1024,512]{1,0:T(8,128)}, u32[]{:S(2)}) copy-start(f32[1024,512]{1,0:T(8,128)} %param.8) | copy-start | bytes 6291460
  20.9 2.9 %copy-start.1 = (f32[512,512]{1,0:T(8,128)S(1)}, f32[512,512]{1,0:T(8,128)}, u32[]{:S(2)}) copy-start(f32[512,512]{1,0:T(8,128)} %constant_dynamic-slice_fusion.x_ref) | copy-start | bytes 3145732
  26.0 2.2 %collective-permute-start.5 = (f32[64,512]{1,0:T(8,128)S(1)}, f32[64,512]{1,0:T(8,128)S(1)}, u32[]{:S(2)}, u32[]{:S(2)}) collective-permute-start(f32[64,512]{1,0:T(8,128)S(1)} %pad_maximum_fusion), channel_id=1, source_target_pairs={{2,3},{3,2},{6,7},{7,6},{10,11},{11,10},{14,15},{15,14},{18,19},{1... | collective-permute-start | bytes 393224 | tf_op jit(solution)/shard_map/ppermute | solution.py:119
  28.0 22.5 %copy-start.6 = (f32[1024,512]{1,0:T(8,128)S(1)}, f32[1024,512]{1,0:T(8,128)}, u32[]{:S(2)}) copy-start(f32[1024,512]{1,0:T(8,128)} %param.5) | copy-start | bytes 6291460
  28.0 60.4 %collective-permute-start.13 = (f32[864,512]{1,0:T(8,128)}, f32[864,512]{1,0:T(8,128)}, u32[]{:S(2)}, u32[]{:S(2)}) collective-permute-start(f32[864,512]{1,0:T(8,128)} %slice.19), channel_id=1, source_target_pairs={{0,1},{1,0},{2,3},{3,2},{4,5},{5,4},{6,7},{7,6},{8,9},{9,8},{10,11... | collective-permute-start | bytes 5308424 | tf_op jit(solution)/shard_map/ppermute | solution.py:169
  54.0 6.1 %copy-start.8 = (f32[512,512]{1,0:T(8,128)}, f32[512,512]{1,0:T(8,128)S(1)}, u32[]{:S(2)}) copy-start(f32[512,512]{1,0:T(8,128)S(1)} %fusion.22) | copy-start | bytes 3145732
  54.0 7.6 %copy-start.12 = (f32[512]{0:T(512)S(1)}, f32[512]{0:T(512)}, u32[]{:S(2)}) copy-start(f32[512]{0:T(512)} %param.9) | copy-start | bytes 6148
  55.0 13.3 %collective-permute-start.6 = (f32[2,64,512]{2,1,0:T(8,128)}, f32[2,64,512]{2,1,0:T(8,128)}, u32[]{:S(2)}, u32[]{:S(2)}) collective-permute-start(f32[2,64,512]{2,1,0:T(8,128)} %get-tuple-element.67), channel_id=1, source_target_pairs={{0,2},{2,0},{4,6},{6,4},{8,10},{10,8},{12,14},{14,12},{16,18},{18,... | collective-permute-start | bytes 786440 | tf_op jit(solution)/shard_map/ppermute | solution.py:130
  58.0 10.7 %collective-permute-start.7 = (f32[2,64,512]{2,1,0:T(8,128)}, f32[2,64,512]{2,1,0:T(8,128)}, u32[]{:S(2)}, u32[]{:S(2)}) collective-permute-start(f32[2,64,512]{2,1,0:T(8,128)} %get-tuple-element.66), channel_id=1, source_target_pairs={{0,4},{2,6},{4,0},{6,2},{8,12},{10,14},{12,8},{14,10},{16,20},{18,... | collective-permute-start | bytes 786440 | tf_op jit(solution)/shard_map/ppermute | solution.py:130
  59.4 11.8 %collective-permute-start.8 = (f32[2,64,512]{2,1,0:T(8,128)}, f32[2,64,512]{2,1,0:T(8,128)}, u32[]{:S(2)}, u32[]{:S(2)}) collective-permute-start(f32[2,64,512]{2,1,0:T(8,128)} %get-tuple-element.65), channel_id=1, source_target_pairs={{0,6},{2,4},{4,2},{6,0},{8,14},{10,12},{12,10},{14,8},{16,22},{18,... | collective-permute-start | bytes 786440 | tf_op jit(solution)/shard_map/ppermute | solution.py:130
  60.1 33.8 %collective-permute-start.14 = (f32[128,512]{1,0:T(8,128)}, f32[128,512]{1,0:T(8,128)S(1)}, u32[]{:S(2)}, u32[]{:S(2)}) collective-permute-start(f32[128,512]{1,0:T(8,128)} %slice.23), channel_id=1, source_target_pairs={{0,1},{1,0},{2,3},{3,2},{4,5},{5,4},{6,7},{7,6},{8,9},{9,8},{10,11... | collective-permute-start | bytes 786440 | tf_op jit(solution)/shard_map/ppermute | solution.py:169
  63.7 7.4 %copy-start.10 = (f32[2,64,512]{2,1,0:T(8,128)S(1)}, f32[2,64,512]{2,1,0:T(8,128)}, u32[]{:S(2)}) copy-start(f32[2,64,512]{2,1,0:T(8,128)} %fusion.5) | copy-start | bytes 786436
  68.3 8.2 %collective-permute-start.12 = (f32[32,512]{1,0:T(8,128)S(1)}, f32[32,512]{1,0:T(8,128)S(1)}, u32[]{:S(2)}, u32[]{:S(2)}) collective-permute-start(f32[32,512]{1,0:T(8,128)S(1)} %slice.21), channel_id=1, source_target_pairs={{0,2},{2,0},{4,6},{6,4},{8,10},{10,8},{12,14},{14,12},{16,18},{18,... | collective-permute-start | bytes 196616 | tf_op jit(solution)/shard_map/ppermute | solution.py:108
  72.6 12.9 %collective-permute-start.10 = (f32[64,512]{1,0:T(8,128)S(1)}, f32[64,512]{1,0:T(8,128)S(1)}, u32[]{:S(2)}, u32[]{:S(2)}) collective-permute-start(f32[64,512]{1,0:T(8,128)S(1)} %get-tuple-element.73), channel_id=1, source_target_pairs={{0,16},{2,18},{4,20},{6,22},{8,24},{10,26},{12,28},{14,30},{16,0},... | collective-permute-start | bytes 393224 | tf_op jit(solution)/shard_map/ppermute | solution.py:130
  75.2 10.4 %collective-permute-start.11 = (f32[64,512]{1,0:T(8,128)S(1)}, f32[64,512]{1,0:T(8,128)S(1)}, u32[]{:S(2)}, u32[]{:S(2)}) collective-permute-start(f32[64,512]{1,0:T(8,128)S(1)} %get-tuple-element.71), channel_id=1, source_target_pairs={{0,24},{2,26},{4,28},{6,30},{8,16},{10,18},{12,20},{14,22},{16,8},... | collective-permute-start | bytes 393224 | tf_op jit(solution)/shard_map/ppermute | solution.py:130
  76.5 10.6 %collective-permute-start.9 = (f32[64,512]{1,0:T(8,128)S(1)}, f32[64,512]{1,0:T(8,128)S(1)}, u32[]{:S(2)}, u32[]{:S(2)}) collective-permute-start(f32[64,512]{1,0:T(8,128)S(1)} %get-tuple-element.72), channel_id=1, source_target_pairs={{0,8},{2,10},{4,12},{6,14},{8,0},{10,2},{12,4},{14,6},{16,24},{18,... | collective-permute-start | bytes 393224 | tf_op jit(solution)/shard_map/ppermute | solution.py:130
  (4 other events, 3.7 us)

commit v6 on v5

--- a/solution.py
+++ b/solution.py
@@ -203,7 +203,7 @@
     total, (phi, own) = exchange(jnp.concatenate(blocks), 0, near, (phi, own))
     gram = total * norm
     gram, psi, phi, own = lax.optimization_barrier((gram, psi, phi, own))
-    phi = add_rows(phi, most, rights[-1], weights, 0, cuts[1] // 2, True)
+    phi = add_rows(phi, most, rights[-1], weights, 0, cuts[1] // 3, True)
     phi = end_rows(phi, own, end, rights[-1], weights, cuts[2])
     return (gram, phi, psi)
 

time: 95.5 us -> 95.5 us (level)
  transfers between devices with their start and end apart: 15 -> 15, of which waited for: 6 -> 6; matrix products, arithmetic and copies ran while one was open for 31% -> 31% of each run, Pallas kernels for 11% -> 12%
where the time goes in v6:
time: 95.5 us; the launch traced here: 95 us
  waiting for transfers between devices  31.8 us (33%)
  starting transfers between devices  16.5 us (17%)
  matrix products  15.6 us (16%)
  local copies, waits for them, and re-layouts  13.5 us (14%)
  Pallas kernels  12.6 us (13%)
  other arithmetic  4.11 us (4%)
    ppermute x1, waiting for transfers between devices, shards(): adjoints.append(lax.ppermute(adjoints[-1], 'snap', ring))  20.5 us
    pallas_call x3, Pallas kernels, add_rows(): pl.pallas_call(functools.partial(add_rows_kernel, last), grid=(x.shape[0]...  11.2 us
    ppermute x9, starting transfers between devices, exchange(): arrived.append(lax.ppermute(give, 'rows', pairs))  10.4 us
    ppermute x9, waiting for transfers between devices, exchange(): arrived.append(lax.ppermute(give, 'rows', pairs))  9.99 us
    dot_general x2, matrix products, mul(): jnp.dot(left, right, precision=HIGH, preferred_element_type=jnp.float32)  8.06 us
    dot_general x2, matrix products, inner_cols(): lax.dot_general(left, right, (((0,), (0,)), ((), ())), precision=HIGH, pr...  7.55 us
    slice x3, local copies, waits for them, and re-layouts, shards(): primals = [[primal[a:b] for a, b in spans]]  4.51 us
    unnamed x26, local copies, waits for them, and re-layouts  3.7 us
  transfers between devices with their start and end apart: 15, of which 6 were waited for; matrix products, arithmetic and copies ran while one was open for 31% of the time, Pallas kernels for 12%

profile of v6, /device:TPU:0, one launch (start us, length us, event | category | flops | bytes accessed | tf_op | source)
XLA Modules:
  0.0 95.0 jit_solution(3920352632502483386)
XLA Ops:
  0.6 3.0 %collective-permute-start = (f32[1024,512]{1,0:T(8,128)}, f32[1024,512]{1,0:T(8,128)}, u32[]{:S(2)}, u32[]{:S(2)}) collective-permute-start(f32[1024,512]{1,0:T(8,128)} %param.6), channel_id=1, source_target_pairs={{0,1},{1,0},{2,3},{3,2},{4,5},{5,4},{6,7},{7,6},{8,9},{9,8},{10,11... | collective-permute-start | bytes 6291464 | tf_op jit(solution)/shard_map/ppermute | solution.py:182
  3.7 4.0 %fusion.21 = f32[512,512]{1,0:T(8,128)S(1)} fusion(f32[1024,512]{1,0:T(8,128)} %param.6, f32[1024,512]{1,0:T(8,128)} %param.5), kind=kOutput, calls=%fused_computation.44 | convolution fusion | flops 1610612736 | bytes 5242880 | tf_op jit(solution)/shard_map/dot_general | solution.py:42
  8.8 1.5 %collective-permute-start.3 = (f32[2,64,512]{2,1,0:T(8,128)}, f32[2,64,512]{2,1,0:T(8,128)}, u32[]{:S(2)}, u32[]{:S(2)}) collective-permute-start(f32[2,64,512]{2,1,0:T(8,128)} %get-tuple-element.70), channel_id=1, source_target_pairs={{0,4},{2,6},{4,0},{6,2},{8,12},{10,14},{12,8},{14,10},{16,20},{18,... | collective-permute-start | bytes 786440 | tf_op jit(solution)/shard_map/ppermute | solution.py:130
  11.8 4.9 %convolution_bitcast_fusion.total_ref = f32[1024,512]{1,0:T(8,128)} fusion(f32[1024,512]{1,0:T(8,128)} %param.5, f32[1024,512]{1,0:T(8,128)S(1)} %copy-done, s32[]{:T(128)S(6)} %select_n.99), kind=kOutput, calls=%fused_computation | convolution fusion | flops 1610612736 | bytes 5242884 | tf_op jit(solution)/shard_map/dot_general | solution.py:15
  16.7 3.2 %convolution_bitcast_fusion.1.total_ref = f32[1024,512]{1,0:T(8,128)} fusion(f32[1024,512]{1,0:T(8,128)S(1)} %copy-done.7, f32[1024,512]{1,0:T(8,128)S(1)} %copy-done.11, s32[]{:T(128)S(6)} %select_n.99), kind=kOutput, calls=%fused_computation.1 | convolution fusion | flops 1610612736 | bytes 5242884 | tf_op jit(solution)/shard_map/dot_general | solution.py:15
  19.9 1.1 %constant_dynamic-slice_fusion.x_ref = f32[512,512]{1,0:T(8,128)} fusion(f32[1024,512]{1,0:T(8,128)S(1)} %copy-done, s32[]{:T(128)S(6)} %select_n.93), kind=kLoop, calls=%fused_computation.42 | loop fusion | bytes 2097156 | tf_op jit(solution)/shard_map/dynamic_slice | solution.py:148
  20.9 2.9 %slice.19 = f32[864,512]{1,0:T(8,128)} slice(f32[1024,512]{1,0:T(8,128)} %param.5), slice={[0:864], [0:512]} | slice | bytes 3538944 | tf_op jit(solution)/shard_map/slice | solution.py:159
  24.1 1.9 %fusion.5 = f32[2,64,512]{2,1,0:T(8,128)} fusion(f32[2,64,512]{2,1,0:T(8,128)} %collective-permute-done.4, f32[2,64,512]{2,1,0:T(8,128)} %collective-permute-done.3, f32[2,64,512]{2,1,0:T(8,128)S(1)} %collective-permute-done.2, f32[2,4,64,512]{3,2,1,0:T(8,128)} %bitcast.61, s32[]{:T(128)S(6)} %select_n.95), kind=kLoop, calls=%fused_computation.17 | loop fusion | flops 196608 | bytes 1310724 | tf_op jit(solution)/shard_map/add | solution.py:133
  26.7 1.3 %constant_dynamic-slice_fusion.1.x_ref = f32[512,512]{1,0:T(8,128)S(1)} fusion(f32[1024,512]{1,0:T(8,128)} %param.8, s32[]{:T(128)S(6)} %select_n.93), kind=kLoop, calls=%fused_computation.43 | loop fusion | bytes 2097156 | tf_op jit(solution)/shard_map/dynamic_slice | solution.py:148
  30.0 20.5 %collective-permute-done.x_ref = f32[1024,512]{1,0:T(8,128)} collective-permute-done((f32[1024,512]{1,0:T(8,128)}, f32[1024,512]{1,0:T(8,128)}, u32[]{:S(2)}, u32[]{:S(2)}) %collective-permute-start) | collective-permute-done | bytes 2097184 | tf_op jit(solution)/shard_map/ppermute | solution.py:182
  50.5 3.5 %fusion.22 = f32[512,512]{1,0:T(8,128)S(1)} fusion(f32[1024,512]{1,0:T(8,128)} %collective-permute-done.x_ref, f32[1024,512]{1,0:T(8,128)S(1)} %copy-done.6), kind=kOutput, calls=%fused_computation.45 | convolution fusion | flops 1610612736 | bytes 5242880 | tf_op jit(solution)/shard_map/dot_general | solution.py:42
  55.0 3.0 %collective-permute-start.6 = (f32[2,64,512]{2,1,0:T(8,128)}, f32[2,64,512]{2,1,0:T(8,128)}, u32[]{:S(2)}, u32[]{:S(2)}) collective-permute-start(f32[2,64,512]{2,1,0:T(8,128)} %get-tuple-element.67), channel_id=1, source_target_pairs={{0,2},{2,0},{4,6},{6,4},{8,10},{10,8},{12,14},{14,12},{16,18},{18,... | collective-permute-start | bytes 786440 | tf_op jit(solution)/shard_map/ppermute | solution.py:130
  58.0 1.4 %collective-permute-start.7 = (f32[2,64,512]{2,1,0:T(8,128)}, f32[2,64,512]{2,1,0:T(8,128)}, u32[]{:S(2)}, u32[]{:S(2)}) collective-permute-start(f32[2,64,512]{2,1,0:T(8,128)} %get-tuple-element.66), channel_id=1, source_target_pairs={{0,4},{2,6},{4,0},{6,2},{8,12},{10,14},{12,8},{14,10},{16,20},{18,... | collective-permute-start | bytes 786440 | tf_op jit(solution)/shard_map/ppermute | solution.py:130
  60.1 1.5 %collective-permute-start.14 = (f32[128,512]{1,0:T(8,128)}, f32[128,512]{1,0:T(8,128)S(1)}, u32[]{:S(2)}, u32[]{:S(2)}) collective-permute-start(f32[128,512]{1,0:T(8,128)} %slice.23), channel_id=1, source_target_pairs={{0,1},{1,0},{2,3},{3,2},{4,5},{5,4},{6,7},{7,6},{8,9},{9,8},{10,11... | collective-permute-start | bytes 786440 | tf_op jit(solution)/shard_map/ppermute | solution.py:169
  63.7 4.5 %shard_map.78 = f32[1024,512]{1,0:T(8,128)} custom-call(f32[1024,512]{1,0:T(8,128)} %convolution_bitcast_fusion.1.total_ref, f32[1024,512]{1,0:T(8,128)} %collective-permute-done.x_ref, bf16[512,512]{1,0:T(8,128)(2,1)S(1)} %copy-done.3, bf16[512,512]{1,0:T(8,128)(2,1)S(1)} %copy-done.5, f32[1,512]{1,0:T(1,128)S(1)} %bitcast.54), custom_call_target="tpu_custom_call", output_to_operand_aliasing={{}: (0, {})} | custom-call | tf_op jit(solution)/shard_map/pallas_call | solution.py:62
  68.6 2.5 %collective-permute-done.8 = f32[2,64,512]{2,1,0:T(8,128)} collective-permute-done((f32[2,64,512]{2,1,0:T(8,128)}, f32[2,64,512]{2,1,0:T(8,128)}, u32[]{:S(2)}, u32[]{:S(2)}) %collective-permute-start.8) | collective-permute-done | bytes 262176 | tf_op jit(solution)/shard_map/ppermute | solution.py:130
  71.1 1.3 %broadcast_select_fusion = (f32[2,64,512]{2,1,0:T(8,128)S(1)}, f32[2,64,512]{2,1,0:T(8,128)S(1)}) fusion(f32[2,64,512]{2,1,0:T(8,128)S(1)} %copy-done.10, pred[]{:T(512)S(6)} %eq.13, f32[2,64,512]{2,1,0:T(8,128)} %collective-permute-done.8, f32[2,64,512]{2,1,0:T(8,128)} %collective-permute-done.7, f32[2,64,512]{2,1,0:T(8,128)} %collective-permute-done.6, ...), kind=kLoop, calls=%fused_computation.37 | loop fusion | flops 262144 | bytes 1835013 | tf_op jit(solution)/shard_map/jit(_where)/select_n | solution.py:201
  72.6 2.6 %collective-permute-start.10 = (f32[64,512]{1,0:T(8,128)S(1)}, f32[64,512]{1,0:T(8,128)S(1)}, u32[]{:S(2)}, u32[]{:S(2)}) collective-permute-start(f32[64,512]{1,0:T(8,128)S(1)} %get-tuple-element.73), channel_id=1, source_target_pairs={{0,16},{2,18},{4,20},{6,22},{8,24},{10,26},{12,28},{14,30},{16,0},... | collective-permute-start | bytes 393224 | tf_op jit(solution)/shard_map/ppermute | solution.py:130
  75.2 1.3 %collective-permute-start.11 = (f32[64,512]{1,0:T(8,128)S(1)}, f32[64,512]{1,0:T(8,128)S(1)}, u32[]{:S(2)}, u32[]{:S(2)}) collective-permute-start(f32[64,512]{1,0:T(8,128)S(1)} %get-tuple-element.71), channel_id=1, source_target_pairs={{0,24},{2,26},{4,28},{6,30},{8,16},{10,18},{12,20},{14,22},{16,8},... | collective-permute-start | bytes 393224 | tf_op jit(solution)/shard_map/ppermute | solution.py:130
  76.8 1.9 %shard_map.79.total_ref = f32[1024,512]{1,0:T(8,128)} custom-call(f32[1024,512]{1,0:T(8,128)} %convolution_bitcast_fusion.total_ref, f32[32,512]{1,0:T(8,128)S(1)} %slice_select_fusion.x_ref, bf16[512,512]{1,0:T(8,128)(2,1)S(1)} %get-tuple-element.50.high_ref, bf16[512,512]{1,0:T(8,128)(2,1)S(1)} %get-tuple-element.51.low_ref, ...), custom_call_target="tpu_custom_call", output_to_operand_aliasing={{}: (0, {})} | custom-call | tf_op jit(solution)/shard_map/pallas_call | solution.py:62
  79.6 6.0 %collective-permute-done.10 = f32[64,512]{1,0:T(8,128)S(1)} collective-permute-done((f32[64,512]{1,0:T(8,128)S(1)}, f32[64,512]{1,0:T(8,128)S(1)}, u32[]{:S(2)}, u32[]{:S(2)}) %collective-permute-start.10) | collective-permute-done | bytes 131104 | tf_op jit(solution)/shard_map/ppermute | solution.py:130
  85.6 1.5 %collective-permute-done.9 = f32[64,512]{1,0:T(8,128)S(1)} collective-permute-done((f32[64,512]{1,0:T(8,128)S(1)}, f32[64,512]{1,0:T(8,128)S(1)}, u32[]{:S(2)}, u32[]{:S(2)}) %collective-permute-start.9) | collective-permute-done | bytes 131104 | tf_op jit(solution)/shard_map/ppermute | solution.py:130
  88.4 4.8 %shard_map.80.total_ref = f32[1024,512]{1,0:T(8,128)} custom-call(f32[1024,512]{1,0:T(8,128)} %shard_map.79.total_ref, f32[864,512]{1,0:T(8,128)} %collective-permute-done.13.x_ref, bf16[512,512]{1,0:T(8,128)(2,1)S(1)} %get-tuple-element.50.high_ref, bf16[512,512]{1,0:T(8,128)(2,1)S(1)} %get-tuple-element.51.low_ref, ...), custom_call_target="tpu_custom_call", output_to_operand_aliasing={{}: (0, {})} | custom-call | tf_op jit(solution)/shard_map/pallas_call | solution.py:62
  93.9 1.1 %shard_map.81 = f32[1024,512]{1,0:T(8,128)} custom-call(f32[1024,512]{1,0:T(8,128)} %shard_map.80.total_ref, f32[128,512]{1,0:T(8,128)S(1)} %slice.24.own_ref, f32[128,512]{1,0:T(8,128)S(1)} %collective-permute-done.14.x_ref, bf16[512,512]{1,0:T(8,128)(2,1)S(1)} %get-tuple-element.50.high_ref, ...), custom_call_target="tpu_custom_call", output_to_operand_aliasing={{}: (0, {})} | custom-call | tf_op jit(solution)/shard_map/pallas_call | solution.py:95
  (59 shorter events, 12.9 us)
Async XLA Ops:
  0.6 11.2 %copy-start = (f32[1024,512]{1,0:T(8,128)S(1)}, f32[1024,512]{1,0:T(8,128)}, u32[]{:S(2)}) copy-start(f32[1024,512]{1,0:T(8,128)} %param.7) | copy-start | bytes 6291460
  0.6 49.8 %collective-permute-start = (f32[1024,512]{1,0:T(8,128)}, f32[1024,512]{1,0:T(8,128)}, u32[]{:S(2)}, u32[]{:S(2)}) collective-permute-start(f32[1024,512]{1,0:T(8,128)} %param.6), channel_id=1, source_target_pairs={{0,1},{1,0},{2,3},{3,2},{4,5},{5,4},{6,7},{7,6},{8,9},{9,8},{10,11... | collective-permute-start | bytes 6291464 | tf_op jit(solution)/shard_map/ppermute | solution.py:182
  7.7 8.9 %copy-start.9 = (f32[512,512]{1,0:T(8,128)}, f32[512,512]{1,0:T(8,128)S(1)}, u32[]{:S(2)}) copy-start(f32[512,512]{1,0:T(8,128)S(1)} %fusion.21) | copy-start | bytes 3145732
  8.8 15.3 %collective-permute-start.2 = (f32[2,64,512]{2,1,0:T(8,128)}, f32[2,64,512]{2,1,0:T(8,128)S(1)}, u32[]{:S(2)}, u32[]{:S(2)}) collective-permute-start(f32[2,64,512]{2,1,0:T(8,128)} %get-tuple-element.68), channel_id=1, source_target_pairs={{0,2},{2,0},{4,6},{6,4},{8,10},{10,8},{12,14},{14,12},{16,18},{18,... | collective-permute-start | bytes 786440 | tf_op jit(solution)/shard_map/ppermute | solution.py:130
  8.8 15.3 %collective-permute-start.3 = (f32[2,64,512]{2,1,0:T(8,128)}, f32[2,64,512]{2,1,0:T(8,128)}, u32[]{:S(2)}, u32[]{:S(2)}) collective-permute-start(f32[2,64,512]{2,1,0:T(8,128)} %get-tuple-element.70), channel_id=1, source_target_pairs={{0,4},{2,6},{4,0},{6,2},{8,12},{10,14},{12,8},{14,10},{16,20},{18,... | collective-permute-start | bytes 786440 | tf_op jit(solution)/shard_map/ppermute | solution.py:130
  10.3 13.8 %collective-permute-start.4 = (f32[2,64,512]{2,1,0:T(8,128)}, f32[2,64,512]{2,1,0:T(8,128)}, u32[]{:S(2)}, u32[]{:S(2)}) collective-permute-start(f32[2,64,512]{2,1,0:T(8,128)} %get-tuple-element.69), channel_id=1, source_target_pairs={{0,6},{2,4},{4,2},{6,0},{8,14},{10,12},{12,10},{14,8},{16,22},{18,... | collective-permute-start | bytes 786440 | tf_op jit(solution)/shard_map/ppermute | solution.py:130
  11.5 12.5 %collective-permute-start.1 = (f32[32,512]{1,0:T(8,128)S(1)}, f32[32,512]{1,0:T(8,128)S(1)}, u32[]{:S(2)}, u32[]{:S(2)}) collective-permute-start(f32[32,512]{1,0:T(8,128)S(1)} %slice.18), channel_id=1, source_target_pairs={{0,2},{2,0},{4,6},{6,4},{8,10},{10,8},{12,14},{14,12},{16,18},{18,... | collective-permute-start | bytes 196616 | tf_op jit(solution)/shard_map/ppermute | solution.py:108
  11.8 4.9 %copy-start.7 = (f32[1024,512]{1,0:T(8,128)S(1)}, f32[1024,512]{1,0:T(8,128)}, u32[]{:S(2)}) copy-start(f32[1024,512]{1,0:T(8,128)} %param.6) | copy-start | bytes 6291460
  11.8 4.9 %copy-start.11 = (f32[1024,512]{1,0:T(8,128)S(1)}, f32[1024,512]{1,0:T(8,128)}, u32[]{:S(2)}) copy-start(f32[1024,512]{1,0:T(8,128)} %param.8) | copy-start | bytes 6291460
  20.9 2.9 %copy-start.1 = (f32[512,512]{1,0:T(8,128)S(1)}, f32[512,512]{1,0:T(8,128)}, u32[]{:S(2)}) copy-start(f32[512,512]{1,0:T(8,128)} %constant_dynamic-slice_fusion.x_ref) | copy-start | bytes 3145732
  26.0 2.2 %collective-permute-start.5 = (f32[64,512]{1,0:T(8,128)S(1)}, f32[64,512]{1,0:T(8,128)S(1)}, u32[]{:S(2)}, u32[]{:S(2)}) collective-permute-start(f32[64,512]{1,0:T(8,128)S(1)} %pad_maximum_fusion), channel_id=1, source_target_pairs={{2,3},{3,2},{6,7},{7,6},{10,11},{11,10},{14,15},{15,14},{18,19},{1... | collective-permute-start | bytes 393224 | tf_op jit(solution)/shard_map/ppermute | solution.py:119
  28.0 22.5 %copy-start.6 = (f32[1024,512]{1,0:T(8,128)S(1)}, f32[1024,512]{1,0:T(8,128)}, u32[]{:S(2)}) copy-start(f32[1024,512]{1,0:T(8,128)} %param.5) | copy-start | bytes 6291460
  28.0 60.4 %collective-permute-start.13 = (f32[864,512]{1,0:T(8,128)}, f32[864,512]{1,0:T(8,128)}, u32[]{:S(2)}, u32[]{:S(2)}) collective-permute-start(f32[864,512]{1,0:T(8,128)} %slice.19), channel_id=1, source_target_pairs={{0,1},{1,0},{2,3},{3,2},{4,5},{5,4},{6,7},{7,6},{8,9},{9,8},{10,11... | collective-permute-start | bytes 5308424 | tf_op jit(solution)/shard_map/ppermute | solution.py:169
  54.0 6.1 %copy-start.8 = (f32[512,512]{1,0:T(8,128)}, f32[512,512]{1,0:T(8,128)S(1)}, u32[]{:S(2)}) copy-start(f32[512,512]{1,0:T(8,128)S(1)} %fusion.22) | copy-start | bytes 3145732
  54.0 7.6 %copy-start.12 = (f32[512]{0:T(512)S(1)}, f32[512]{0:T(512)}, u32[]{:S(2)}) copy-start(f32[512]{0:T(512)} %param.9) | copy-start | bytes 6148
  55.0 13.3 %collective-permute-start.6 = (f32[2,64,512]{2,1,0:T(8,128)}, f32[2,64,512]{2,1,0:T(8,128)}, u32[]{:S(2)}, u32[]{:S(2)}) collective-permute-start(f32[2,64,512]{2,1,0:T(8,128)} %get-tuple-element.67), channel_id=1, source_target_pairs={{0,2},{2,0},{4,6},{6,4},{8,10},{10,8},{12,14},{14,12},{16,18},{18,... | collective-permute-start | bytes 786440 | tf_op jit(solution)/shard_map/ppermute | solution.py:130
  58.0 10.7 %collective-permute-start.7 = (f32[2,64,512]{2,1,0:T(8,128)}, f32[2,64,512]{2,1,0:T(8,128)}, u32[]{:S(2)}, u32[]{:S(2)}) collective-permute-start(f32[2,64,512]{2,1,0:T(8,128)} %get-tuple-element.66), channel_id=1, source_target_pairs={{0,4},{2,6},{4,0},{6,2},{8,12},{10,14},{12,8},{14,10},{16,20},{18,... | collective-permute-start | bytes 786440 | tf_op jit(solution)/shard_map/ppermute | solution.py:130
  59.4 11.8 %collective-permute-start.8 = (f32[2,64,512]{2,1,0:T(8,128)}, f32[2,64,512]{2,1,0:T(8,128)}, u32[]{:S(2)}, u32[]{:S(2)}) collective-permute-start(f32[2,64,512]{2,1,0:T(8,128)} %get-tuple-element.65), channel_id=1, source_target_pairs={{0,6},{2,4},{4,2},{6,0},{8,14},{10,12},{12,10},{14,8},{16,22},{18,... | collective-permute-start | bytes 786440 | tf_op jit(solution)/shard_map/ppermute | solution.py:130
  60.1 33.8 %collective-permute-start.14 = (f32[128,512]{1,0:T(8,128)}, f32[128,512]{1,0:T(8,128)S(1)}, u32[]{:S(2)}, u32[]{:S(2)}) collective-permute-start(f32[128,512]{1,0:T(8,128)} %slice.23), channel_id=1, source_target_pairs={{0,1},{1,0},{2,3},{3,2},{4,5},{5,4},{6,7},{7,6},{8,9},{9,8},{10,11... | collective-permute-start | bytes 786440 | tf_op jit(solution)/shard_map/ppermute | solution.py:169
  63.7 7.4 %copy-start.10 = (f32[2,64,512]{2,1,0:T(8,128)S(1)}, f32[2,64,512]{2,1,0:T(8,128)}, u32[]{:S(2)}) copy-start(f32[2,64,512]{2,1,0:T(8,128)} %fusion.5) | copy-start | bytes 786436
  68.3 8.2 %collective-permute-start.12 = (f32[32,512]{1,0:T(8,128)S(1)}, f32[32,512]{1,0:T(8,128)S(1)}, u32[]{:S(2)}, u32[]{:S(2)}) collective-permute-start(f32[32,512]{1,0:T(8,128)S(1)} %slice.21), channel_id=1, source_target_pairs={{0,2},{2,0},{4,6},{6,4},{8,10},{10,8},{12,14},{14,12},{16,18},{18,... | collective-permute-start | bytes 196616 | tf_op jit(solution)/shard_map/ppermute | solution.py:108
  72.6 12.9 %collective-permute-start.10 = (f32[64,512]{1,0:T(8,128)S(1)}, f32[64,512]{1,0:T(8,128)S(1)}, u32[]{:S(2)}, u32[]{:S(2)}) collective-permute-start(f32[64,512]{1,0:T(8,128)S(1)} %get-tuple-element.73), channel_id=1, source_target_pairs={{0,16},{2,18},{4,20},{6,22},{8,24},{10,26},{12,28},{14,30},{16,0},... | collective-permute-start | bytes 393224 | tf_op jit(solution)/shard_map/ppermute | solution.py:130
  75.2 10.4 %collective-permute-start.11 = (f32[64,512]{1,0:T(8,128)S(1)}, f32[64,512]{1,0:T(8,128)S(1)}, u32[]{:S(2)}, u32[]{:S(2)}) collective-permute-start(f32[64,512]{1,0:T(8,128)S(1)} %get-tuple-element.71), channel_id=1, source_target_pairs={{0,24},{2,26},{4,28},{6,30},{8,16},{10,18},{12,20},{14,22},{16,8},... | collective-permute-start | bytes 393224 | tf_op jit(solution)/shard_map/ppermute | solution.py:130
  76.5 10.6 %collective-permute-start.9 = (f32[64,512]{1,0:T(8,128)S(1)}, f32[64,512]{1,0:T(8,128)S(1)}, u32[]{:S(2)}, u32[]{:S(2)}) collective-permute-start(f32[64,512]{1,0:T(8,128)S(1)} %get-tuple-element.72), channel_id=1, source_target_pairs={{0,8},{2,10},{4,12},{6,14},{8,0},{10,2},{12,4},{14,6},{16,24},{18,... | collective-permute-start | bytes 393224 | tf_op jit(solution)/shard_map/ppermute | solution.py:130
  (4 other events, 3.7 us)

commit v7 on v5

--- a/solution.py
+++ b/solution.py
@@ -141,7 +141,7 @@
     weights = 1.0 / jnp.sqrt(singular)
     norm = 1.0 / jnp.sqrt(jnp.float32(rows * count))
     ring = [(i, (i + 1) % sides) for i in range(sides)]
-    cuts = [0, rows * 27 // 32, rows * 28 // 32, rows]
+    cuts = [0, rows * 26 // 32, rows * 27 // 32, rows]
     spans = list(zip(cuts[:-1], cuts[1:]))
 
     def block(matrix, owner):

time: 95.5 us -> 95.6 us (level)
  waiting for transfers between devices: 32.5 us -> 30.3 us
    ppermute x9, waiting for transfers between devices: 9.99 us -> 8.24 us  [exchange(): arrived.append(lax.ppermute(give, 'rows', pairs))]
  transfers between devices with their start and end apart: 15 -> 15, of which waited for: 6 -> 5; matrix products, arithmetic and copies ran while one was open for 31% -> 33% of each run, Pallas kernels for 11% -> 11%
where the time goes in v7:
time: 95.6 us; the launch traced here: 95 us
  waiting for transfers between devices  30.3 us (32%)
  starting transfers between devices  17.1 us (18%)
  matrix products  15.6 us (16%)
  local copies, waits for them, and re-layouts  14.4 us (15%)
  Pallas kernels  11.8 us (12%)
  other arithmetic  4.94 us (5%)
    ppermute x1, waiting for transfers between devices, shards(): adjoints.append(lax.ppermute(adjoints[-1], 'snap', ring))  19.9 us
    pallas_call x3, Pallas kernels, add_rows(): pl.pallas_call(functools.partial(add_rows_kernel, last), grid=(x.shape[0]...  10.4 us
    ppermute x9, starting transfers between devices, exchange(): arrived.append(lax.ppermute(give, 'rows', pairs))  10.4 us
    ppermute x9, waiting for transfers between devices, exchange(): arrived.append(lax.ppermute(give, 'rows', pairs))  8.24 us
    dot_general x2, matrix products, mul(): jnp.dot(left, right, precision=HIGH, preferred_element_type=jnp.float32)  8.06 us
    dot_general x2, matrix products, inner_cols(): lax.dot_general(left, right, (((0,), (0,)), ((), ())), precision=HIGH, pr...  7.55 us
    slice x3, local copies, waits for them, and re-layouts, shards(): primals = [[primal[a:b] for a, b in spans]]  4.51 us
    unnamed x26, local copies, waits for them, and re-layouts  3.69 us
  transfers between devices with their start and end apart: 15, of which 5 were waited for; matrix products, arithmetic and copies ran while one was open for 33% of the time, Pallas kernels for 11%

profile of v7, /device:TPU:0, one launch (start us, length us, event | category | flops | bytes accessed | tf_op | source)
XLA Modules:
  0.0 95.0 jit_solution(16657951045742763119)
XLA Ops:
  0.6 3.0 %collective-permute-start = (f32[1024,512]{1,0:T(8,128)}, f32[1024,512]{1,0:T(8,128)}, u32[]{:S(2)}, u32[]{:S(2)}) collective-permute-start(f32[1024,512]{1,0:T(8,128)} %param.6), channel_id=1, source_target_pairs={{0,1},{1,0},{2,3},{3,2},{4,5},{5,4},{6,7},{7,6},{8,9},{9,8},{10,11... | collective-permute-start | bytes 6291464 | tf_op jit(solution)/shard_map/ppermute | solution.py:182
  3.7 4.0 %fusion.21 = f32[512,512]{1,0:T(8,128)S(1)} fusion(f32[1024,512]{1,0:T(8,128)} %param.6, f32[1024,512]{1,0:T(8,128)} %param.5), kind=kOutput, calls=%fused_computation.44 | convolution fusion | flops 1610612736 | bytes 5242880 | tf_op jit(solution)/shard_map/dot_general | solution.py:42
  8.8 1.5 %collective-permute-start.3 = (f32[2,64,512]{2,1,0:T(8,128)}, f32[2,64,512]{2,1,0:T(8,128)}, u32[]{:S(2)}, u32[]{:S(2)}) collective-permute-start(f32[2,64,512]{2,1,0:T(8,128)} %get-tuple-element.70), channel_id=1, source_target_pairs={{0,4},{2,6},{4,0},{6,2},{8,12},{10,14},{12,8},{14,10},{16,20},{18,... | collective-permute-start | bytes 786440 | tf_op jit(solution)/shard_map/ppermute | solution.py:130
  11.8 4.9 %convolution_bitcast_fusion.total_ref = f32[1024,512]{1,0:T(8,128)} fusion(f32[1024,512]{1,0:T(8,128)} %param.5, f32[1024,512]{1,0:T(8,128)S(1)} %copy-done, s32[]{:T(128)S(6)} %select_n.99), kind=kOutput, calls=%fused_computation | convolution fusion | flops 1610612736 | bytes 5242884 | tf_op jit(solution)/shard_map/dot_general | solution.py:15
  16.6 3.2 %convolution_bitcast_fusion.1.total_ref = f32[1024,512]{1,0:T(8,128)} fusion(f32[1024,512]{1,0:T(8,128)S(1)} %copy-done.7, f32[1024,512]{1,0:T(8,128)S(1)} %copy-done.11, s32[]{:T(128)S(6)} %select_n.99), kind=kOutput, calls=%fused_computation.1 | convolution fusion | flops 1610612736 | bytes 5242884 | tf_op jit(solution)/shard_map/dot_general | solution.py:15
  20.9 2.9 %slice.19 = f32[832,512]{1,0:T(8,128)} slice(f32[1024,512]{1,0:T(8,128)} %param.5), slice={[0:832], [0:512]} | slice | bytes 3407872 | tf_op jit(solution)/shard_map/slice | solution.py:159
  24.0 1.9 %fusion.5 = f32[2,64,512]{2,1,0:T(8,128)} fusion(f32[2,64,512]{2,1,0:T(8,128)} %collective-permute-done.4, f32[2,64,512]{2,1,0:T(8,128)} %collective-permute-done.3, f32[2,64,512]{2,1,0:T(8,128)S(1)} %collective-permute-done.2, f32[2,4,64,512]{3,2,1,0:T(8,128)} %bitcast.61, s32[]{:T(128)S(6)} %select_n.95), kind=kLoop, calls=%fused_computation.17 | loop fusion | flops 196608 | bytes 1310724 | tf_op jit(solution)/shard_map/add | solution.py:133
  25.9 1.3 %collective-permute-start.5 = (f32[64,512]{1,0:T(8,128)S(1)}, f32[64,512]{1,0:T(8,128)}, u32[]{:S(2)}, u32[]{:S(2)}) collective-permute-start(f32[64,512]{1,0:T(8,128)S(1)} %pad_maximum_fusion), channel_id=1, source_target_pairs={{2,3},{3,2},{6,7},{7,6},{10,11},{11,10},{14,15},{15,14},{18,19},{1... | collective-permute-start | bytes 393224 | tf_op jit(solution)/shard_map/ppermute | solution.py:119
  27.2 1.3 %constant_dynamic-slice_fusion.1.x_ref = f32[512,512]{1,0:T(8,128)S(1)} fusion(f32[1024,512]{1,0:T(8,128)} %param.8, s32[]{:T(128)S(6)} %select_n.93), kind=kLoop, calls=%fused_computation.43 | loop fusion | bytes 2097156 | tf_op jit(solution)/shard_map/dynamic_slice | solution.py:148
  30.5 19.9 %collective-permute-done.x_ref = f32[1024,512]{1,0:T(8,128)} collective-permute-done((f32[1024,512]{1,0:T(8,128)}, f32[1024,512]{1,0:T(8,128)}, u32[]{:S(2)}, u32[]{:S(2)}) %collective-permute-start) | collective-permute-done | bytes 2097184 | tf_op jit(solution)/shard_map/ppermute | solution.py:182
  50.5 3.5 %fusion.22 = f32[512,512]{1,0:T(8,128)S(1)} fusion(f32[1024,512]{1,0:T(8,128)} %collective-permute-done.x_ref, f32[1024,512]{1,0:T(8,128)S(1)} %copy-done.6), kind=kOutput, calls=%fused_computation.45 | convolution fusion | flops 1610612736 | bytes 5242880 | tf_op jit(solution)/shard_map/dot_general | solution.py:42
  55.0 3.0 %collective-permute-start.6 = (f32[2,64,512]{2,1,0:T(8,128)}, f32[2,64,512]{2,1,0:T(8,128)}, u32[]{:S(2)}, u32[]{:S(2)}) collective-permute-start(f32[2,64,512]{2,1,0:T(8,128)} %get-tuple-element.67), channel_id=1, source_target_pairs={{0,2},{2,0},{4,6},{6,4},{8,10},{10,8},{12,14},{14,12},{16,18},{18,... | collective-permute-start | bytes 786440 | tf_op jit(solution)/shard_map/ppermute | solution.py:130
  57.9 1.4 %collective-permute-start.7 = (f32[2,64,512]{2,1,0:T(8,128)}, f32[2,64,512]{2,1,0:T(8,128)}, u32[]{:S(2)}, u32[]{:S(2)}) collective-permute-start(f32[2,64,512]{2,1,0:T(8,128)} %get-tuple-element.66), channel_id=1, source_target_pairs={{0,4},{2,6},{4,0},{6,2},{8,12},{10,14},{12,8},{14,10},{16,20},{18,... | collective-permute-start | bytes 786440 | tf_op jit(solution)/shard_map/ppermute | solution.py:130
  60.1 1.5 %collective-permute-start.14 = (f32[160,512]{1,0:T(8,128)}, f32[160,512]{1,0:T(8,128)S(1)}, u32[]{:S(2)}, u32[]{:S(2)}) collective-permute-start(f32[160,512]{1,0:T(8,128)} %slice.23), channel_id=1, source_target_pairs={{0,1},{1,0},{2,3},{3,2},{4,5},{5,4},{6,7},{7,6},{8,9},{9,8},{10,11... | collective-permute-start | bytes 983048 | tf_op jit(solution)/shard_map/ppermute | solution.py:169
  64.6 4.5 %shard_map.78 = f32[1024,512]{1,0:T(8,128)} custom-call(f32[1024,512]{1,0:T(8,128)} %convolution_bitcast_fusion.1.total_ref, f32[1024,512]{1,0:T(8,128)} %collective-permute-done.x_ref, bf16[512,512]{1,0:T(8,128)(2,1)S(1)} %copy-done.3, bf16[512,512]{1,0:T(8,128)(2,1)S(1)} %copy-done.5, f32[1,512]{1,0:T(1,128)S(1)} %bitcast.54), custom_call_target="tpu_custom_call", output_to_operand_aliasing={{}: (0, {})} | custom-call | tf_op jit(solution)/shard_map/pallas_call | solution.py:62
  69.5 1.6 %collective-permute-done.8 = f32[2,64,512]{2,1,0:T(8,128)} collective-permute-done((f32[2,64,512]{2,1,0:T(8,128)}, f32[2,64,512]{2,1,0:T(8,128)}, u32[]{:S(2)}, u32[]{:S(2)}) %collective-permute-start.8) | collective-permute-done | bytes 262176 | tf_op jit(solution)/shard_map/ppermute | solution.py:130
  71.1 1.3 %broadcast_select_fusion = (f32[2,64,512]{2,1,0:T(8,128)S(1)}, f32[2,64,512]{2,1,0:T(8,128)S(1)}) fusion(f32[2,64,512]{2,1,0:T(8,128)S(1)} %copy-done.10, pred[]{:T(512)S(6)} %eq.13, f32[2,64,512]{2,1,0:T(8,128)} %collective-permute-done.8, f32[2,64,512]{2,1,0:T(8,128)} %collective-permute-done.7, f32[2,64,512]{2,1,0:T(8,128)} %collective-permute-done.6, ...), kind=kLoop, calls=%fused_computation.37 | loop fusion | flops 262144 | bytes 1835013 | tf_op jit(solution)/shard_map/jit(_where)/select_n | solution.py:201
  72.6 2.6 %collective-permute-start.10 = (f32[64,512]{1,0:T(8,128)S(1)}, f32[64,512]{1,0:T(8,128)S(1)}, u32[]{:S(2)}, u32[]{:S(2)}) collective-permute-start(f32[64,512]{1,0:T(8,128)S(1)} %get-tuple-element.73), channel_id=1, source_target_pairs={{0,16},{2,18},{4,20},{6,22},{8,24},{10,26},{12,28},{14,30},{16,0},... | collective-permute-start | bytes 393224 | tf_op jit(solution)/shard_map/ppermute | solution.py:130
  75.1 1.3 %collective-permute-start.11 = (f32[64,512]{1,0:T(8,128)S(1)}, f32[64,512]{1,0:T(8,128)S(1)}, u32[]{:S(2)}, u32[]{:S(2)}) collective-permute-start(f32[64,512]{1,0:T(8,128)S(1)} %get-tuple-element.71), channel_id=1, source_target_pairs={{0,24},{2,26},{4,28},{6,30},{8,16},{10,18},{12,20},{14,22},{16,8},... | collective-permute-start | bytes 393224 | tf_op jit(solution)/shard_map/ppermute | solution.py:130
  77.6 1.9 %shard_map.79.total_ref = f32[1024,512]{1,0:T(8,128)} custom-call(f32[1024,512]{1,0:T(8,128)} %convolution_bitcast_fusion.total_ref, f32[32,512]{1,0:T(8,128)S(1)} %slice_select_fusion.x_ref, bf16[512,512]{1,0:T(8,128)(2,1)S(1)} %get-tuple-element.50.high_ref, bf16[512,512]{1,0:T(8,128)(2,1)S(1)} %get-tuple-element.51.low_ref, ...), custom_call_target="tpu_custom_call", output_to_operand_aliasing={{}: (0, {})} | custom-call | tf_op jit(solution)/shard_map/pallas_call | solution.py:62
  80.4 5.1 %collective-permute-done.10 = f32[64,512]{1,0:T(8,128)S(1)} collective-permute-done((f32[64,512]{1,0:T(8,128)S(1)}, f32[64,512]{1,0:T(8,128)S(1)}, u32[]{:S(2)}, u32[]{:S(2)}) %collective-permute-start.10) | collective-permute-done | bytes 131104 | tf_op jit(solution)/shard_map/ppermute | solution.py:130
  85.5 1.5 %collective-permute-done.9 = f32[64,512]{1,0:T(8,128)S(1)} collective-permute-done((f32[64,512]{1,0:T(8,128)S(1)}, f32[64,512]{1,0:T(8,128)S(1)}, u32[]{:S(2)}, u32[]{:S(2)}) %collective-permute-start.9) | collective-permute-done | bytes 131104 | tf_op jit(solution)/shard_map/ppermute | solution.py:130
  87.7 4.0 %shard_map.80.total_ref = f32[1024,512]{1,0:T(8,128)} custom-call(f32[1024,512]{1,0:T(8,128)} %shard_map.79.total_ref, f32[832,512]{1,0:T(8,128)} %collective-permute-done.13.x_ref, bf16[512,512]{1,0:T(8,128)(2,1)S(1)} %get-tuple-element.50.high_ref, bf16[512,512]{1,0:T(8,128)(2,1)S(1)} %get-tuple-element.51.low_ref, ...), custom_call_target="tpu_custom_call", output_to_operand_aliasing={{}: (0, {})} | custom-call | tf_op jit(solution)/shard_map/pallas_call | solution.py:62
  91.8 2.1 %collective-permute-done.14.x_ref = f32[160,512]{1,0:T(8,128)S(1)} collective-permute-done((f32[160,512]{1,0:T(8,128)}, f32[160,512]{1,0:T(8,128)S(1)}, u32[]{:S(2)}, u32[]{:S(2)}) %collective-permute-start.14) | collective-permute-done | bytes 327712 | tf_op jit(solution)/shard_map/ppermute | solution.py:169
  (59 shorter events, 14.9 us)
Async XLA Ops:
  0.6 11.1 %copy-start = (f32[1024,512]{1,0:T(8,128)S(1)}, f32[1024,512]{1,0:T(8,128)}, u32[]{:S(2)}) copy-start(f32[1024,512]{1,0:T(8,128)} %param.7) | copy-start | bytes 6291460
  0.6 49.8 %collective-permute-start = (f32[1024,512]{1,0:T(8,128)}, f32[1024,512]{1,0:T(8,128)}, u32[]{:S(2)}, u32[]{:S(2)}) collective-permute-start(f32[1024,512]{1,0:T(8,128)} %param.6), channel_id=1, source_target_pairs={{0,1},{1,0},{2,3},{3,2},{4,5},{5,4},{6,7},{7,6},{8,9},{9,8},{10,11... | collective-permute-start | bytes 6291464 | tf_op jit(solution)/shard_map/ppermute | solution.py:182
  7.7 8.9 %copy-start.9 = (f32[512,512]{1,0:T(8,128)}, f32[512,512]{1,0:T(8,128)S(1)}, u32[]{:S(2)}) copy-start(f32[512,512]{1,0:T(8,128)S(1)} %fusion.21) | copy-start | bytes 3145732
  8.8 15.2 %collective-permute-start.2 = (f32[2,64,512]{2,1,0:T(8,128)}, f32[2,64,512]{2,1,0:T(8,128)S(1)}, u32[]{:S(2)}, u32[]{:S(2)}) collective-permute-start(f32[2,64,512]{2,1,0:T(8,128)} %get-tuple-element.68), channel_id=1, source_target_pairs={{0,2},{2,0},{4,6},{6,4},{8,10},{10,8},{12,14},{14,12},{16,18},{18,... | collective-permute-start | bytes 786440 | tf_op jit(solution)/shard_map/ppermute | solution.py:130
  8.8 15.2 %collective-permute-start.3 = (f32[2,64,512]{2,1,0:T(8,128)}, f32[2,64,512]{2,1,0:T(8,128)}, u32[]{:S(2)}, u32[]{:S(2)}) collective-permute-start(f32[2,64,512]{2,1,0:T(8,128)} %get-tuple-element.70), channel_id=1, source_target_pairs={{0,4},{2,6},{4,0},{6,2},{8,12},{10,14},{12,8},{14,10},{16,20},{18,... | collective-permute-start | bytes 786440 | tf_op jit(solution)/shard_map/ppermute | solution.py:130
  10.3 13.7 %collective-permute-start.4 = (f32[2,64,512]{2,1,0:T(8,128)}, f32[2,64,512]{2,1,0:T(8,128)}, u32[]{:S(2)}, u32[]{:S(2)}) collective-permute-start(f32[2,64,512]{2,1,0:T(8,128)} %get-tuple-element.69), channel_id=1, source_target_pairs={{0,6},{2,4},{4,2},{6,0},{8,14},{10,12},{12,10},{14,8},{16,22},{18,... | collective-permute-start | bytes 786440 | tf_op jit(solution)/shard_map/ppermute | solution.py:130
  11.5 12.5 %collective-permute-start.1 = (f32[32,512]{1,0:T(8,128)S(1)}, f32[32,512]{1,0:T(8,128)S(1)}, u32[]{:S(2)}, u32[]{:S(2)}) collective-permute-start(f32[32,512]{1,0:T(8,128)S(1)} %slice.18), channel_id=1, source_target_pairs={{0,2},{2,0},{4,6},{6,4},{8,10},{10,8},{12,14},{14,12},{16,18},{18,... | collective-permute-start | bytes 196616 | tf_op jit(solution)/shard_map/ppermute | solution.py:108
  11.8 4.9 %copy-start.7 = (f32[1024,512]{1,0:T(8,128)S(1)}, f32[1024,512]{1,0:T(8,128)}, u32[]{:S(2)}) copy-start(f32[1024,512]{1,0:T(8,128)} %param.6) | copy-start | bytes 6291460
  11.8 4.9 %copy-start.11 = (f32[1024,512]{1,0:T(8,128)S(1)}, f32[1024,512]{1,0:T(8,128)}, u32[]{:S(2)}) copy-start(f32[1024,512]{1,0:T(8,128)} %param.8) | copy-start | bytes 6291460
  20.9 2.9 %copy-start.1 = (f32[512,512]{1,0:T(8,128)S(1)}, f32[512,512]{1,0:T(8,128)}, u32[]{:S(2)}) copy-start(f32[512,512]{1,0:T(8,128)} %constant_dynamic-slice_fusion.x_ref) | copy-start | bytes 3145732
  25.9 2.9 %collective-permute-start.5 = (f32[64,512]{1,0:T(8,128)S(1)}, f32[64,512]{1,0:T(8,128)}, u32[]{:S(2)}, u32[]{:S(2)}) collective-permute-start(f32[64,512]{1,0:T(8,128)S(1)} %pad_maximum_fusion), channel_id=1, source_target_pairs={{2,3},{3,2},{6,7},{7,6},{10,11},{11,10},{14,15},{15,14},{18,19},{1... | collective-permute-start | bytes 393224 | tf_op jit(solution)/shard_map/ppermute | solution.py:119
  28.5 21.9 %copy-start.6 = (f32[1024,512]{1,0:T(8,128)S(1)}, f32[1024,512]{1,0:T(8,128)}, u32[]{:S(2)}) copy-start(f32[1024,512]{1,0:T(8,128)} %param.5) | copy-start | bytes 6291460
  28.5 59.2 %collective-permute-start.13 = (f32[832,512]{1,0:T(8,128)}, f32[832,512]{1,0:T(8,128)}, u32[]{:S(2)}, u32[]{:S(2)}) collective-permute-start(f32[832,512]{1,0:T(8,128)} %slice.19), channel_id=1, source_target_pairs={{0,1},{1,0},{2,3},{3,2},{4,5},{5,4},{6,7},{7,6},{8,9},{9,8},{10,11... | collective-permute-start | bytes 5111816 | tf_op jit(solution)/shard_map/ppermute | solution.py:169
  54.0 6.2 %copy-start.8 = (f32[512,512]{1,0:T(8,128)}, f32[512,512]{1,0:T(8,128)S(1)}, u32[]{:S(2)}) copy-start(f32[512,512]{1,0:T(8,128)S(1)} %fusion.22) | copy-start | bytes 3145732
  54.0 7.7 %copy-start.12 = (f32[512]{0:T(512)S(1)}, f32[512]{0:T(512)}, u32[]{:S(2)}) copy-start(f32[512]{0:T(512)} %param.9) | copy-start | bytes 6148
  55.0 14.2 %collective-permute-start.6 = (f32[2,64,512]{2,1,0:T(8,128)}, f32[2,64,512]{2,1,0:T(8,128)}, u32[]{:S(2)}, u32[]{:S(2)}) collective-permute-start(f32[2,64,512]{2,1,0:T(8,128)} %get-tuple-element.67), channel_id=1, source_target_pairs={{0,2},{2,0},{4,6},{6,4},{8,10},{10,8},{12,14},{14,12},{16,18},{18,... | collective-permute-start | bytes 786440 | tf_op jit(solution)/shard_map/ppermute | solution.py:130
  57.9 11.6 %collective-permute-start.7 = (f32[2,64,512]{2,1,0:T(8,128)}, f32[2,64,512]{2,1,0:T(8,128)}, u32[]{:S(2)}, u32[]{:S(2)}) collective-permute-start(f32[2,64,512]{2,1,0:T(8,128)} %get-tuple-element.66), channel_id=1, source_target_pairs={{0,4},{2,6},{4,0},{6,2},{8,12},{10,14},{12,8},{14,10},{16,20},{18,... | collective-permute-start | bytes 786440 | tf_op jit(solution)/shard_map/ppermute | solution.py:130
  59.3 11.8 %collective-permute-start.8 = (f32[2,64,512]{2,1,0:T(8,128)}, f32[2,64,512]{2,1,0:T(8,128)}, u32[]{:S(2)}, u32[]{:S(2)}) collective-permute-start(f32[2,64,512]{2,1,0:T(8,128)} %get-tuple-element.65), channel_id=1, source_target_pairs={{0,6},{2,4},{4,2},{6,0},{8,14},{10,12},{12,10},{14,8},{16,22},{18,... | collective-permute-start | bytes 786440 | tf_op jit(solution)/shard_map/ppermute | solution.py:130
  60.1 33.7 %collective-permute-start.14 = (f32[160,512]{1,0:T(8,128)}, f32[160,512]{1,0:T(8,128)S(1)}, u32[]{:S(2)}, u32[]{:S(2)}) collective-permute-start(f32[160,512]{1,0:T(8,128)} %slice.23), channel_id=1, source_target_pairs={{0,1},{1,0},{2,3},{3,2},{4,5},{5,4},{6,7},{7,6},{8,9},{9,8},{10,11... | collective-permute-start | bytes 983048 | tf_op jit(solution)/shard_map/ppermute | solution.py:169
  64.6 6.5 %copy-start.10 = (f32[2,64,512]{2,1,0:T(8,128)S(1)}, f32[2,64,512]{2,1,0:T(8,128)}, u32[]{:S(2)}) copy-start(f32[2,64,512]{2,1,0:T(8,128)} %fusion.5) | copy-start | bytes 786436
  69.1 7.4 %collective-permute-start.12 = (f32[32,512]{1,0:T(8,128)S(1)}, f32[32,512]{1,0:T(8,128)S(1)}, u32[]{:S(2)}, u32[]{:S(2)}) collective-permute-start(f32[32,512]{1,0:T(8,128)S(1)} %slice.21), channel_id=1, source_target_pairs={{0,2},{2,0},{4,6},{6,4},{8,10},{10,8},{12,14},{14,12},{16,18},{18,... | collective-permute-start | bytes 196616 | tf_op jit(solution)/shard_map/ppermute | solution.py:108
  72.6 12.9 %collective-permute-start.10 = (f32[64,512]{1,0:T(8,128)S(1)}, f32[64,512]{1,0:T(8,128)S(1)}, u32[]{:S(2)}, u32[]{:S(2)}) collective-permute-start(f32[64,512]{1,0:T(8,128)S(1)} %get-tuple-element.73), channel_id=1, source_target_pairs={{0,16},{2,18},{4,20},{6,22},{8,24},{10,26},{12,28},{14,30},{16,0},... | collective-permute-start | bytes 393224 | tf_op jit(solution)/shard_map/ppermute | solution.py:130
  75.1 10.4 %collective-permute-start.11 = (f32[64,512]{1,0:T(8,128)S(1)}, f32[64,512]{1,0:T(8,128)S(1)}, u32[]{:S(2)}, u32[]{:S(2)}) collective-permute-start(f32[64,512]{1,0:T(8,128)S(1)} %get-tuple-element.71), channel_id=1, source_target_pairs={{0,24},{2,26},{4,28},{6,30},{8,16},{10,18},{12,20},{14,22},{16,8},... | collective-permute-start | bytes 393224 | tf_op jit(solution)/shard_map/ppermute | solution.py:130
  76.5 10.5 %collective-permute-start.9 = (f32[64,512]{1,0:T(8,128)S(1)}, f32[64,512]{1,0:T(8,128)S(1)}, u32[]{:S(2)}, u32[]{:S(2)}) collective-permute-start(f32[64,512]{1,0:T(8,128)S(1)} %get-tuple-element.72), channel_id=1, source_target_pairs={{0,8},{2,10},{4,12},{6,14},{8,0},{10,2},{12,4},{14,6},{16,24},{18,... | collective-permute-start | bytes 393224 | tf_op jit(solution)/shard_map/ppermute | solution.py:130
  (4 other events, 3.7 us)
